TPU v7x, 256 devices: a whole 4x4x8 slice. The times are simulated.
256 devices in a mesh: rep: 2 (over x_lo), tok: 2 (over x_hi), voc: 64 (over y, z, core).
Axes of the slice: x: 4 (x_hi: 2, x_lo: 2; x = x_hi * 2 + x_lo), y: 4, z: 8, core: 2. Of those that a mesh axis runs over, the one named last changes fastest.
Arguments:
- hidden: bfloat16 [2, 768, 3584], P('rep', 'tok'), may hold values from -30 to 30
- head: bfloat16 [3584, 131072], P('tok', 'voc'), may hold values from -0.3125 to 0.3125
- targets: int32 [768], P('tok'), may hold values from 0 to 131071
- loss_mask: int32 [768], P('tok'), may hold values 0 or 1
Outputs:
- grad_hidden: bfloat16 [2, 768, 3584], P('rep', ('tok', 'voc'))
- token_loss: float32 [2, 768], P('rep', 'tok')
All inputs are finite; a program needn't handle non-finite values. No bound on the sum of `loss_mask` on one device may be relied on, other than what follows from the above.
Results may differ from a plain program's by a relative error of at most 0.0065.
Values may be sent and summed in bfloat16 or wider, within the bound.
No kernel may reach another device: no remote copies, remote signals or barrier semaphores. Data moves between devices by JAX's collectives and lax.ppermute only.
A program may use at most 128 MiB of HBM per device.

v0:
```python
import jax
import jax.numpy as jnp
from jax import lax
from jax.sharding import PartitionSpec as P

softcap_limit = 30.0
kl_weight = 0.5
loss_scale = 16.0


def partner(block, axis, stride):
    count = lax.axis_size(axis)
    route = []
    for low in range(count):
        high = low | 1 << stride
        if high != low and high < count:
            route += [(low, high), (high, low)]
    return lax.ppermute(block, axis, route)


def capped(raw_logits):
    return softcap_limit * jnp.tanh(raw_logits / softcap_limit)


def shards(hidden, head, targets, loss_mask):
    states = hidden[0]
    vocab_part = head.shape[1]
    voc_start = lax.axis_index("voc") * vocab_part
    columns = voc_start + lax.broadcasted_iota(jnp.int32, (1, vocab_part), 1)
    left_sides = (states,)
    full_head = lax.all_gather(head, "tok", axis=0, tiled=True)
    raw_list = tuple(
        (jnp.dot(left, full_head, preferred_element_type=jnp.float32) for left in left_sides)
    )
    own_logits = capped(raw_list[0])
    partner_logits = partner(own_logits.astype(jnp.bfloat16), "rep", 0).astype(jnp.float32)
    target_hit = columns == targets[:, None]
    own_exp = jnp.exp(own_logits)
    own_part = jnp.sum(own_exp, axis=1)
    picked_part = jnp.sum(jnp.where(target_hit, own_logits, jnp.float32(0.0)), axis=1)
    partner_exp = jnp.exp(partner_logits)
    partner_part = jnp.sum(partner_exp, axis=1)
    cross_part = jnp.sum(partner_exp * (partner_logits - own_logits), axis=1)
    own_total, picked = lax.psum((own_part, picked_part), "voc")
    partner_total, cross = lax.psum((partner_part, cross_part), "voc")
    weights_tok = loss_mask.astype(jnp.float32)
    own_lse = jnp.log(own_total)
    partner_lse = jnp.log(partner_total)
    token_loss = weights_tok * (
        own_lse - picked + kl_weight * (cross / partner_total - partner_lse + own_lse)
    )
    logit_grad = (
        (loss_scale * weights_tok)[:, None]
        * (
            (1.0 + kl_weight) * own_exp / own_total[:, None]
            - target_hit.astype(jnp.float32)
            - kl_weight * partner_exp / partner_total[:, None]
        )
        * (1.0 - (own_logits / softcap_limit) ** 2)
    )
    grad_low = logit_grad.astype(jnp.bfloat16)
    grad_terms = lax.dot_general(
        grad_low, full_head, (((1,), (1,)), ((), ())), preferred_element_type=jnp.float32
    )
    grad_rows = lax.psum_scatter(grad_terms, "voc", scatter_dimension=0, tiled=True)
    return (grad_rows.astype(jnp.bfloat16)[None], token_loss[None])


def solution(mesh):
    placed = (P("rep", "tok", None), P("tok", "voc"), P("tok"), P("tok"))
    return jax.shard_map(
        shards,
        mesh=mesh,
        in_specs=placed,
        out_specs=(P("rep", ("tok", "voc"), None), P("rep", "tok")),
        check_vma=False,
    )
```

profile of v0, /device:TPU:2, one launch (start us, length us, event | category | flops | bytes accessed | tf_op | source)
XLA Modules:
  0.0 629.1 jit_solution(17950968800682240693)
XLA Ops:
  7.2 0.0 copy-start
  7.2 0.0 all-gather.2.cloned.1.call-start
  7.2 0.7 all-gather.2.cloned.1.call-update
  7.9 186.1 %all-gather.2.cloned.1.call-done = bf16[3584,2048]{1,0:T(8,128)(2,1)} async-done(((bf16[1792,2048]{1,0:T(8,128)(2,1)}), bf16[3584,2048]{1,0:T(8,128)(2,1)}) %all-gather.2.cloned.1.call-update) | async-done | bytes 14680080 | tf_op jit(solution)/shard_map/all_gather | solution.py:31
  194.0 10.6 %multiply_convert_fusion = (bf16[384,2048]{1,0:T(8,128)(2,1)}, f32[384,2048]{1,0:T(8,128)}) fusion(bf16[3584,2048]{1,0:T(8,128)(2,1)} %all-gather.2.cloned.1.call-done, bf16[1,384,3584]{2,1,0:T(8,128)(2,1)S(1)} %copy-done), kind=kOutput, calls=%fused_computation.17 | convolution fusion | flops 5639503872 | bytes 22151168 | tf_op jit(solution)/shard_map/dot_general | solution.py:33
  204.6 1.5 collective-permute-start
  206.1 35.0 %collective-permute-done = bf16[384,2048]{1,0:T(8,128)(2,1)} collective-permute-done((bf16[384,2048]{1,0:T(8,128)(2,1)}, bf16[384,2048]{1,0:T(8,128)(2,1)}, u32[]{:S(2)}, u32[]{:S(2)}) %collective-permute-start) | collective-permute-done | bytes 1572896 | tf_op jit(solution)/shard_map/ppermute | solution.py:18
  241.1 4.4 fusion.10
  245.5 130.1 %all-reduce.2 = (f32[384]{0:T(512)S(1)}, f32[384]{0:T(512)S(1)}, f32[384]{0:T(512)S(1)}, f32[384]{0:T(512)S(1)}) all-reduce(f32[384]{0:T(512)S(1)} %get-tuple-element.5, f32[384]{0:T(512)S(1)} %get-tuple-element.4, f32[384]{0:T(512)S(1)} %get-tuple-element.3, ...), channel_id=1, replica_groups=mesh['rep'=2,'tok'=2,'voc'=64] {'voc'}, use_global_device_ids=true, to_apply=%region_3.4 | all-reduce | flops 1536 | bytes 12288 | tf_op jit(solution)/shard_map/psum | solution.py:45
  375.6 0.6 add_multiply_fusion
  376.2 19.2 %fusion.13 = f32[384,3584]{1,0:T(8,128)} fusion(bf16[3584,2048]{1,0:T(8,128)(2,1)} %all-gather.2.cloned.1.call-done, f32[384,2048]{1,0:T(8,128)} %get-tuple-element.28, bf16[384,2048]{1,0:T(8,128)(2,1)} %collective-permute-done, f32[384]{0:T(512)S(1)} %get-tuple-element.6, s32[2048]{0:T(1024)S(1)} %iota_add_fusion, f32[384]{0:T(512)S(1)} %get-tuple-element.7, ...), kind=kOutput, calls=%fused_computation.19 | convolution fusion | flops 5648941056 | bytes 24918016 | tf_op jit(solution)/shard_map/dot_general | solution.py:62
  395.4 147.1 %fusion = f32[8,3584]{1,0:T(8,128)S(1)} fusion(f32[384,3584]{1,0:T(8,128)} %fusion.13), kind=kCustom, calls=%all-reduce-scatter | all-reduce-scatter fusion | flops 1835009 | bytes 5620736
  542.6 1.3 collective-permute-start.16
  543.9 1.3 collective-permute-start.1
  545.2 1.3 collective-permute-start.10
  546.5 1.3 collective-permute-start.11
  547.8 1.3 collective-permute-start.12
  549.1 0.0 collective-permute-done.16
  549.1 11.2 %collective-permute-start.13 = (bf16[8,3584]{1,0:T(8,128)(2,1)S(1)}, bf16[8,3584]{1,0:T(8,128)(2,1)S(1)}, u32[]{:S(2)}, u32[]{:S(2)}) collective-permute-start(bf16[8,3584]{1,0:T(8,128)(2,1)S(1)} %convert.30), channel_id=1, source_target_pairs={{0,13},{1,14},{2,15},{3,16},{4,17},{5,18},{6,19},{7,20},{8,21},{9,... | collective-permute-start | bytes 172040
  560.3 0.0 collective-permute-done.1
  560.3 1.8 collective-permute-start.14
  562.2 0.0 collective-permute-done.10
  562.2 1.4 collective-permute-start.15
  563.6 0.0 collective-permute-done.11
  563.6 3.0 collective-permute-start.2
  566.6 0.0 collective-permute-done.12
  566.6 1.3 collective-permute-start.3
  567.9 0.0 collective-permute-done.13
  567.9 3.2 collective-permute-start.4
  571.2 0.0 collective-permute-done.14
  571.2 4.8 collective-permute-start.5
  576.0 0.0 collective-permute-done.15
  576.0 4.3 collective-permute-start.6
  580.3 0.0 collective-permute-done.2
  580.3 3.1 collective-permute-start.7
  583.5 0.0 collective-permute-done.3
  583.5 3.1 collective-permute-start.8
  586.6 0.0 collective-permute-done.4
  586.6 5.0 collective-permute-start.9
  591.6 1.3 dynamic-slice.4
  593.5 1.2 broadcast_in_dim.16
  594.7 0.0 collective-permute-done.5
  594.7 0.0 collective-permute-done.6
  594.7 0.0 collective-permute-done.7
  594.7 0.0 collective-permute-done.8
  594.7 0.0 collective-permute-done.9
  594.8 25.9 %concatenate = bf16[134,3584]{1,0:T(8,128)(2,1)} concatenate(bf16[6,3584]{1,0:T(8,128)(2,1)S(1)} %collective-permute-done.16, bf16[8,3584]{1,0:T(8,128)(2,1)S(1)} %collective-permute-done.15, bf16[8,3584]{1,0:T(8,128)(2,1)S(1)} %collective-permute-done.14, bf16[8,3584]{1,0:T(8,128)(2,1)S(1)} %collective-permute-done.13, bf16[8,3584]{1,0:T(8,128)(2,1)S(1)} %collective-permute-done.12, ...), dimensions={0} | concatenate | bytes 1978368
  620.7 1.5 fusion.24
  (8 shorter events, 0.0 us)
Async XLA Ops:
  7.2 186.9 %copy-start = (bf16[1,384,3584]{2,1,0:T(8,128)(2,1)S(1)}, bf16[1,384,3584]{2,1,0:T(8,128)(2,1)}, u32[]{:S(2)}) copy-start(bf16[1,384,3584]{2,1,0:T(8,128)(2,1)} %param.4) | copy-start | bytes 8257540
  7.2 186.8 %all-gather.2.cloned.1.call-start = ((), (), s32[]{:S(2)}) async-start(), calls=%async_computation | async-start | bytes 22020096 | tf_op jit(solution)/shard_map/all_gather | solution.py:31
  7.9 233.2 %copy-start.1 = (s32[384]{0:T(512)S(1)}, s32[384]{0:T(512)}, u32[]{:S(2)}) copy-start(s32[384]{0:T(512)} %param.6) | copy-start | bytes 4612
  204.6 171.0 %copy-start.2 = (s32[384]{0:T(512)S(1)}, s32[384]{0:T(512)}, u32[]{:S(2)}) copy-start(s32[384]{0:T(512)} %param.7) | copy-start | bytes 4612
  204.6 36.5 %collective-permute-start = (bf16[384,2048]{1,0:T(8,128)(2,1)}, bf16[384,2048]{1,0:T(8,128)(2,1)}, u32[]{:S(2)}, u32[]{:S(2)}) collective-permute-start(bf16[384,2048]{1,0:T(8,128)(2,1)} %get-tuple-element.27), channel_id=1, source_target_pairs={{0,128},{128,0},{1,129},{129,1},{2,130},{130,2},{3,131},{131,3},{4... | collective-permute-start | bytes 4718600 | tf_op jit(solution)/shard_map/ppermute | solution.py:18
  542.6 6.5 %collective-permute-start.16 = (bf16[6,3584]{1,0:T(8,128)(2,1)S(1)}, bf16[6,3584]{1,0:T(8,128)(2,1)S(1)}, u32[]{:S(2)}, u32[]{:S(2)}) collective-permute-start(bf16[6,3584]{1,0:T(8,128)(2,1)S(1)} %slice), channel_id=1, source_target_pairs={{0,16},{1,17},{2,18},{3,19},{4,20},{5,21},{6,22},{7,23},{8,24},{9,... | collective-permute-start | bytes 129032
  543.9 16.4 %collective-permute-start.1 = (bf16[8,3584]{1,0:T(8,128)(2,1)S(1)}, bf16[8,3584]{1,0:T(8,128)(2,1)S(1)}, u32[]{:S(2)}, u32[]{:S(2)}) collective-permute-start(bf16[8,3584]{1,0:T(8,128)(2,1)S(1)} %convert.30), channel_id=1, source_target_pairs={{0,1},{1,2},{2,3},{3,4},{4,5},{5,6},{6,7},{7,8},{8,9},{9,10},{10,1... | collective-permute-start | bytes 172040
  545.2 17.0 %collective-permute-start.10 = (bf16[8,3584]{1,0:T(8,128)(2,1)S(1)}, bf16[8,3584]{1,0:T(8,128)(2,1)S(1)}, u32[]{:S(2)}, u32[]{:S(2)}) collective-permute-start(bf16[8,3584]{1,0:T(8,128)(2,1)S(1)} %convert.30), channel_id=1, source_target_pairs={{0,10},{1,11},{2,12},{3,13},{4,14},{5,15},{6,16},{7,17},{8,18},{9,... | collective-permute-start | bytes 172040
  546.5 17.1 %collective-permute-start.11 = (bf16[8,3584]{1,0:T(8,128)(2,1)S(1)}, bf16[8,3584]{1,0:T(8,128)(2,1)S(1)}, u32[]{:S(2)}, u32[]{:S(2)}) collective-permute-start(bf16[8,3584]{1,0:T(8,128)(2,1)S(1)} %convert.30), channel_id=1, source_target_pairs={{0,11},{1,12},{2,13},{3,14},{4,15},{5,16},{6,17},{7,18},{8,19},{9,... | collective-permute-start | bytes 172040
  547.8 18.8 %collective-permute-start.12 = (bf16[8,3584]{1,0:T(8,128)(2,1)S(1)}, bf16[8,3584]{1,0:T(8,128)(2,1)S(1)}, u32[]{:S(2)}, u32[]{:S(2)}) collective-permute-start(bf16[8,3584]{1,0:T(8,128)(2,1)S(1)} %convert.30), channel_id=1, source_target_pairs={{0,12},{1,13},{2,14},{3,15},{4,16},{5,17},{6,18},{7,19},{8,20},{9,... | collective-permute-start | bytes 172040
  549.1 18.8 %collective-permute-start.13 = (bf16[8,3584]{1,0:T(8,128)(2,1)S(1)}, bf16[8,3584]{1,0:T(8,128)(2,1)S(1)}, u32[]{:S(2)}, u32[]{:S(2)}) collective-permute-start(bf16[8,3584]{1,0:T(8,128)(2,1)S(1)} %convert.30), channel_id=1, source_target_pairs={{0,13},{1,14},{2,15},{3,16},{4,17},{5,18},{6,19},{7,20},{8,21},{9,... | collective-permute-start | bytes 172040
  560.3 10.8 %collective-permute-start.14 = (bf16[8,3584]{1,0:T(8,128)(2,1)S(1)}, bf16[8,3584]{1,0:T(8,128)(2,1)S(1)}, u32[]{:S(2)}, u32[]{:S(2)}) collective-permute-start(bf16[8,3584]{1,0:T(8,128)(2,1)S(1)} %convert.30), channel_id=1, source_target_pairs={{0,14},{1,15},{2,16},{3,17},{4,18},{5,19},{6,20},{7,21},{8,22},{9,... | collective-permute-start | bytes 172040
  562.2 13.8 %collective-permute-start.15 = (bf16[8,3584]{1,0:T(8,128)(2,1)S(1)}, bf16[8,3584]{1,0:T(8,128)(2,1)S(1)}, u32[]{:S(2)}, u32[]{:S(2)}) collective-permute-start(bf16[8,3584]{1,0:T(8,128)(2,1)S(1)} %convert.30), channel_id=1, source_target_pairs={{0,15},{1,16},{2,17},{3,18},{4,19},{5,20},{6,21},{7,22},{8,23},{9,... | collective-permute-start | bytes 172040
  563.6 16.8 %collective-permute-start.2 = (bf16[8,3584]{1,0:T(8,128)(2,1)S(1)}, bf16[8,3584]{1,0:T(8,128)(2,1)S(1)}, u32[]{:S(2)}, u32[]{:S(2)}) collective-permute-start(bf16[8,3584]{1,0:T(8,128)(2,1)S(1)} %convert.30), channel_id=1, source_target_pairs={{0,2},{1,3},{2,4},{3,5},{4,6},{5,7},{6,8},{7,9},{8,10},{9,11},{10,... | collective-permute-start | bytes 172040
  566.6 16.8 %collective-permute-start.3 = (bf16[8,3584]{1,0:T(8,128)(2,1)S(1)}, bf16[8,3584]{1,0:T(8,128)(2,1)S(1)}, u32[]{:S(2)}, u32[]{:S(2)}) collective-permute-start(bf16[8,3584]{1,0:T(8,128)(2,1)S(1)} %convert.30), channel_id=1, source_target_pairs={{0,3},{1,4},{2,5},{3,6},{4,7},{5,8},{6,9},{7,10},{8,11},{9,12},{10... | collective-permute-start | bytes 172040
  567.9 18.7 %collective-permute-start.4 = (bf16[8,3584]{1,0:T(8,128)(2,1)S(1)}, bf16[8,3584]{1,0:T(8,128)(2,1)S(1)}, u32[]{:S(2)}, u32[]{:S(2)}) collective-permute-start(bf16[8,3584]{1,0:T(8,128)(2,1)S(1)} %convert.30), channel_id=1, source_target_pairs={{0,4},{1,5},{2,6},{3,7},{4,8},{5,9},{6,10},{7,11},{8,12},{9,13},{1... | collective-permute-start | bytes 172040
  571.2 23.6 %collective-permute-start.5 = (bf16[8,3584]{1,0:T(8,128)(2,1)S(1)}, bf16[8,3584]{1,0:T(8,128)(2,1)}, u32[]{:S(2)}, u32[]{:S(2)}) collective-permute-start(bf16[8,3584]{1,0:T(8,128)(2,1)S(1)} %convert.30), channel_id=1, source_target_pairs={{0,5},{1,6},{2,7},{3,8},{4,9},{5,10},{6,11},{7,12},{8,13},{9,14},{... | collective-permute-start | bytes 172040
  576.0 18.7 %collective-permute-start.6 = (bf16[8,3584]{1,0:T(8,128)(2,1)S(1)}, bf16[8,3584]{1,0:T(8,128)(2,1)}, u32[]{:S(2)}, u32[]{:S(2)}) collective-permute-start(bf16[8,3584]{1,0:T(8,128)(2,1)S(1)} %convert.30), channel_id=1, source_target_pairs={{0,6},{1,7},{2,8},{3,9},{4,10},{5,11},{6,12},{7,13},{8,14},{9,15},... | collective-permute-start | bytes 172040
  580.3 14.4 %collective-permute-start.7 = (bf16[8,3584]{1,0:T(8,128)(2,1)S(1)}, bf16[8,3584]{1,0:T(8,128)(2,1)}, u32[]{:S(2)}, u32[]{:S(2)}) collective-permute-start(bf16[8,3584]{1,0:T(8,128)(2,1)S(1)} %convert.30), channel_id=1, source_target_pairs={{0,7},{1,8},{2,9},{3,10},{4,11},{5,12},{6,13},{7,14},{8,15},{9,16}... | collective-permute-start | bytes 172040
  583.5 11.3 %collective-permute-start.8 = (bf16[8,3584]{1,0:T(8,128)(2,1)S(1)}, bf16[8,3584]{1,0:T(8,128)(2,1)}, u32[]{:S(2)}, u32[]{:S(2)}) collective-permute-start(bf16[8,3584]{1,0:T(8,128)(2,1)S(1)} %convert.30), channel_id=1, source_target_pairs={{0,8},{1,9},{2,10},{3,11},{4,12},{5,13},{6,14},{7,15},{8,16},{9,17... | collective-permute-start | bytes 172040
  586.6 8.2 %collective-permute-start.9 = (bf16[8,3584]{1,0:T(8,128)(2,1)S(1)}, bf16[8,3584]{1,0:T(8,128)(2,1)}, u32[]{:S(2)}, u32[]{:S(2)}) collective-permute-start(bf16[8,3584]{1,0:T(8,128)(2,1)S(1)} %convert.30), channel_id=1, source_target_pairs={{0,9},{1,10},{2,11},{3,12},{4,13},{5,14},{6,15},{7,16},{8,17},{9,1... | collective-permute-start | bytes 172040
Sparse Core Ops, SparseCore 0:
  9.8 184.1 all-gather.1
where the time goes:
time: 632 us; the launch traced here: 629 us
  blocking collectives  277 us (44%)
  waiting for transfers between devices  222 us (35%)
  starting transfers between devices  50.3 us (8%)
  local copies, waits for them, and re-layouts  30 us (5%)
  matrix products  29.8 us (5%)
  between operations  14.9 us (2%)
    all_gather x1, waiting for transfers between devices, shards(): full_head = lax.all_gather(head, 'tok', axis=0, tiled=True)  186 us
    unnamed x1, blocking collectives  147 us
    psum x1, blocking collectives, shards(): partner_total, cross = lax.psum((partner_part, cross_part), 'voc')  130 us
    unnamed x16, starting transfers between devices  48.8 us
    ppermute x1, waiting for transfers between devices, partner(): return lax.ppermute(block, axis, route)  35 us
    unnamed x9, local copies, waits for them, and re-layouts  27.2 us
    dot_general x1, matrix products, shards(): lax.dot_general(grad_low, full_head, (((1,), (1,)), ((), ())), preferred_...  19.2 us
  transfers between devices with their start and end apart: 18, of which 2 were waited for; matrix products, arithmetic and copies ran while one was open for 0% of the time, Pallas kernels for 0%

commit v1 on v0

v1 whole, which is shorter than its diff:
```python
import jax
import jax.numpy as jnp
from jax import lax
from jax.sharding import PartitionSpec as P

softcap_limit = 30.0
kl_weight = 0.5
loss_scale = 16.0

N_Y, N_Z, N_C, N_X = 4, 8, 2, 4
LINE = ("rep", "tok")


def line_xor(block, k):
    k = (k % 2) * 2 + k // 2
    return lax.ppermute(block, LINE, [(x, x ^ k) for x in range(N_X)])


def voc_xor(block, k):
    return lax.ppermute(block, "voc", [(v, v ^ k) for v in range(N_Y * N_Z * N_C)])


def tree_sum(values):
    values = list(values)
    while len(values) > 1:
        values = [a + b for a, b in zip(values[::2], values[1::2])]
    return values[0]


def sum_over(stats):
    stats = tree_sum([stats] + [line_xor(stats, k) for k in (1, 2, 3)])
    stats = tree_sum([stats, voc_xor(stats, 1)])
    stats = tree_sum([stats] + [voc_xor(stats, 16 * k) for k in (1, 2, 3)])
    stats = tree_sum([stats] + [voc_xor(stats, 2 * k) for k in range(1, 8)])
    return stats


def capped(raw_logits):
    return softcap_limit * jnp.tanh(raw_logits / softcap_limit)


def gather_hidden(states, voc):
    k = voc % 16
    c, y, zh = k // 8, (k // 2) % 4, k % 2
    d_block = voc // 16
    slab = lax.dynamic_slice(states, (y * 96 + zh * 48, d_block * 896), (48, 896))
    x = lax.axis_index("tok") * 2 + lax.axis_index("rep")
    slabs = jnp.stack([slab] + [line_xor(slab, j) for j in (1, 2, 3)])
    out = lax.broadcasted_iota(jnp.int32, (96, 192), 0)
    src = lax.broadcasted_iota(jnp.int32, (96, 192), 1)
    rep, z, tok, i = out // 48, out % 48 // 12, out % 12 // 6, out % 6
    wanted = ((tok * 2 + rep) ^ x) * 48 + z * 12 + c * 6 + i
    pick = (src == wanted).astype(jnp.bfloat16)
    piece = jnp.dot(pick, slabs.reshape(192, 896), preferred_element_type=jnp.float32)
    piece = piece.astype(jnp.bfloat16).reshape(1, 2, 48, 896)
    full = lax.all_gather(piece, "voc", axis=0, tiled=True)
    return full.reshape(4, 16, 2, 48, 896)


def shards(hidden, head, targets, loss_mask):
    rep, tok, voc = (lax.axis_index(a) for a in ("rep", "tok", "voc"))
    x = tok * 2 + rep
    width = head.shape[1] // N_X

    def quarter(q):
        return lax.dynamic_slice(head, (0, q * width), (head.shape[0], width))

    other_half = line_xor(quarter(3 - x), 3)
    own_half = quarter(x)
    rows = gather_hidden(hidden[0], voc)
    rows = rows.transpose(2, 1, 3, 0, 4).reshape(2 * 768, 3584)

    low = jnp.where(tok == 0, own_half, other_half)
    high = jnp.where(tok == 0, other_half, own_half)
    raw = jnp.dot(rows[:, :1792], low, preferred_element_type=jnp.float32) + jnp.dot(
        rows[:, 1792:], high, preferred_element_type=jnp.float32
    )
    logits = capped(raw).reshape(2, 768, width)
    shared = lax.optimization_barrier(logits.astype(jnp.bfloat16)).astype(jnp.float32)
    partner = shared[::-1]

    scal = jnp.stack([targets, loss_mask])
    both = jnp.stack([scal, line_xor(scal, 2)])
    both = jnp.where(tok == 0, both, both[::-1])
    both = both.reshape(2, 2, 4, 8, 2, 6).transpose(1, 4, 2, 3, 0, 5).reshape(2, 768)
    row_targets, row_mask = both[0], both[1].astype(jnp.float32)

    columns = voc * head.shape[1] + x * width + lax.broadcasted_iota(jnp.int32, (1, 1, width), 2)
    hit = columns == row_targets[None, :, None]
    own_exp = jnp.exp(logits)
    partner_exp = jnp.exp(partner)
    stats = jnp.stack([
        jnp.sum(own_exp, axis=2),
        jnp.sum(partner_exp, axis=2),
        jnp.sum(jnp.where(hit, logits, 0.0), axis=2),
        jnp.sum(partner_exp * (partner - logits), axis=2),
    ])
    own_total, partner_total, picked, cross = sum_over(stats)

    own_lse, partner_lse = jnp.log(own_total), jnp.log(partner_total)
    losses = row_mask * (
        own_lse - picked + kl_weight * (cross / partner_total - partner_lse + own_lse)
    )
    loss = lax.dynamic_index_in_dim(losses, rep, 0, keepdims=False)
    loss = loss.reshape(2, 4, 8, 2, 6)
    loss = lax.dynamic_index_in_dim(loss, tok, 3, keepdims=False)
    token_loss = loss.transpose(1, 2, 0, 3).reshape(1, 384)

    grad = (loss_scale * row_mask)[None, :, None] * (
        (1.0 + kl_weight) * own_exp / own_total[..., None]
        - hit.astype(jnp.float32)
        - kl_weight * partner_exp / partner_total[..., None]
    ) * (1.0 - (logits / softcap_limit) ** 2)
    grad = grad.astype(jnp.bfloat16)

    mine = lax.dynamic_index_in_dim(grad, rep, 0, keepdims=False)
    theirs = lax.dynamic_index_in_dim(grad, 1 - rep, 0, keepdims=False)
    parts = [mine, line_xor(theirs, 1), line_xor(mine, 2), line_xor(theirs, 3)]
    terms = sum(
        lax.dot_general(p, quarter(x ^ j), (((1,), (1,)), ((), ())), preferred_element_type=jnp.float32)
        for j, p in enumerate(parts)
    )

    def scatter(parts, me, xor, count):
        low = parts.astype(jnp.bfloat16)
        total = lax.dynamic_index_in_dim(parts, me, 0, keepdims=False)
        got = [
            voc_xor(lax.dynamic_index_in_dim(low, me ^ k, 0, keepdims=False), k * xor)
            for k in range(1, count)
        ]
        for g in got:
            total = total + g.astype(jnp.float32)
        return total

    c, y, z = voc % 2, voc // 16, (voc // 2) % 8
    part = scatter(terms.reshape(2, 384, 1792), c, 1, 2)
    part = scatter(part.reshape(4, 96, 1792), y, 16, 4)
    part = scatter(part.reshape(8, 12, 1792), z, 2, 8)
    part = part.astype(jnp.bfloat16).reshape(2, 6, 1792)
    keep = lax.dynamic_index_in_dim(part, tok, 0, keepdims=False)
    sent = lax.dynamic_index_in_dim(part, 1 - tok, 0, keepdims=False)
    got = line_xor(sent, 2)
    out = jnp.where(
        tok == 0, jnp.concatenate([keep, got], axis=1), jnp.concatenate([got, keep], axis=1)
    )
    return out[None], token_loss


def solution(mesh):
    placed = (P("rep", "tok", None), P("tok", "voc"), P("tok"), P("tok"))
    return jax.shard_map(
        shards,
        mesh=mesh,
        in_specs=placed,
        out_specs=(P("rep", ("tok", "voc"), None), P("rep", "tok")),
        check_vma=False,
    )
```

time: 632 us -> 289 us (0.46)
  blocking collectives: 277 us -> 0 us
  waiting for transfers between devices: 222 us -> 144 us
  other arithmetic: 5.02 us -> 17.2 us
  matrix products: 29.8 us -> 20.7 us
  starting transfers between devices: 50.3 us -> 58.6 us
    unnamed x1 -> x0, blocking collectives: 147 us -> none
    psum x1 -> x0, blocking collectives: 130 us -> none  [shards(): partner_total, cross = lax.psum((partner_part, cross_part), 'voc')]
    all_gather x1, waiting for transfers between devices: 186 us -> 77.5 us  [gather_hidden(): full = lax.all_gather(piece, 'voc', axis=0, tiled=True)]
    ppermute x1 -> x34, starting transfers between devices: 1.46 us -> 58.6 us  [the longest x22 36.1 us: voc_xor(): lax.ppermute(block, 'voc', [(v, v ^ k) for v in range(N_Y * N_Z * N_C)])]
    unnamed x16 -> x0, starting transfers between devices: 48.8 us -> none
    ppermute x1 -> x34, waiting for transfers between devices: 35 us -> 66.1 us  [the longest x12 33.2 us: line_xor(): return lax.ppermute(block, LINE, [(x, x ^ k) for x in range(N_X)])]
    unnamed x9 -> x25, local copies, waits for them, and re-layouts: 27.2 us -> 7.16 us
    transpose x0 -> x2, local copies, waits for them, and re-layouts: none -> 13.3 us  [the longest x1 13.2 us: shards(): rows = rows.transpose(2, 1, 3, 0, 4).reshape(2 * 768, 3584)]
  transfers between devices with their start and end apart: 18 -> 35, of which waited for: 2 -> 23; matrix products, arithmetic and copies ran while one was open for 0% -> 11% of each run, Pallas kernels for 0% -> 0%
where the time goes in v1:
time: 289 us; the launch traced here: 285 us
  waiting for transfers between devices  144 us (50%)
  starting transfers between devices  58.6 us (20%)
  local copies, waits for them, and re-layouts  29.7 us (10%)
  matrix products  20.7 us (7%)
  other arithmetic  17.2 us (6%)
  between operations  15 us (5%)
    all_gather x1, waiting for transfers between devices, gather_hidden(): full = lax.all_gather(piece, 'voc', axis=0, tiled=True)  77.5 us
    ppermute x22, starting transfers between devices, voc_xor(): lax.ppermute(block, 'voc', [(v, v ^ k) for v in range(N_Y * N_Z * N_C)])  36.1 us
    ppermute x12, waiting for transfers between devices, line_xor(): return lax.ppermute(block, LINE, [(x, x ^ k) for x in range(N_X)])  33.2 us
    ppermute x22, waiting for transfers between devices, voc_xor(): lax.ppermute(block, 'voc', [(v, v ^ k) for v in range(N_Y * N_Z * N_C)])  32.9 us
    ppermute x12, starting transfers between devices, line_xor(): return lax.ppermute(block, LINE, [(x, x ^ k) for x in range(N_X)])  22.4 us
    transpose x1, local copies, waits for them, and re-layouts, shards(): rows = rows.transpose(2, 1, 3, 0, 4).reshape(2 * 768, 3584)  13.2 us
    dot_general x4, matrix products, shards(): lax.dot_general(p, quarter(x ^ j), (((1,), (1,)), ((), ())), preferred_el...  12.2 us
    unnamed x25, local copies, waits for them, and re-layouts  7.16 us
  transfers between devices with their start and end apart: 35, of which 23 were waited for; matrix products, arithmetic and copies ran while one was open for 11% of the time, Pallas kernels for 0%

profile of v1, /device:TPU:2, one launch (start us, length us, event | category | flops | bytes accessed | tf_op | source)
XLA Modules:
  0.0 284.7 jit_solution(4044736381840743462)
XLA Ops:
  7.3 1.6 copy-done
  9.0 2.4 collective-permute-start.1
  13.8 3.6 %collective-permute-done.2 = bf16[48,896]{1,0:T(8,128)(2,1)S(1)} collective-permute-done((bf16[48,896]{1,0:T(8,128)(2,1)S(1)}, bf16[48,896]{1,0:T(8,128)(2,1)S(1)}, u32[]{:S(2)}, u32[]{:S(2)}) %collective-permute-start.2) | collective-permute-done | bytes 86048 | tf_op jit(solution)/shard_map/ppermute | solution.py:16
  18.6 3.0 %constant_dynamic-slice_fusion.6 = bf16[1792,512]{1,0:T(8,128)(2,1)} fusion(bf16[1792,2048]{1,0:T(8,128)(2,1)} %param.5, s32[]{:T(128)S(6)} %select_n.209), kind=kLoop, calls=%fused_computation.123 | loop fusion | bytes 3670020 | tf_op jit(solution)/shard_map/dynamic_slice | solution.py:66
  22.4 3.7 %collective-permute-start = (s32[2,384]{1,0:T(2,128)S(1)}, s32[2,384]{1,0:T(2,128)S(1)}, u32[]{:S(2)}, u32[]{:S(2)}) collective-permute-start(s32[2,384]{1,0:T(2,128)S(1)} %get-tuple-element.29), channel_id=1, source_target_pairs={{0,64},{64,0},{128,192},{192,128},{1,65},{65,1},{129,193},{193,129... | collective-permute-start | bytes 9224 | tf_op jit(solution)/shard_map/ppermute | solution.py:16
  26.1 1.8 collective-permute-done
  30.9 77.5 %all-gather.2.cloned.1.call-done = bf16[64,2,48,896]{3,2,1,0:T(8,128)(2,1)} async-done(((bf16[1,2,48,896]{3,2,1,0:T(8,128)(2,1)}), bf16[64,2,48,896]{3,2,1,0:T(8,128)(2,1)}) %all-gather.2.cloned.1.call-update) | async-done | bytes 11010064 | tf_op jit(solution)/shard_map/all_gather | solution.py:56
  108.3 13.2 %copy.20 = bf16[2,16,48,4,896]{4,3,2,1,0:T(4,128)(2,1)S(1)} copy(bf16[2,16,48,4,896]{4,2,0,1,3:T(8,128)(2,1)} %bitcast.117) | data formatting | bytes 22020096 | tf_op jit(solution)/shard_map/transpose | solution.py:71
  121.5 3.8 %copy.24 = bf16[192,8,4,896]{3,1,2,0:T(8,128)(2,1)S(1)} copy(bf16[192,8,4,896]{3,2,1,0:T(4,128)(2,1)S(1)} %bitcast.110) | data formatting | bytes 22020096
  125.4 3.1 %fusion = f32[1536,512]{1,0:T(8,128)S(1)} fusion(bf16[1536,3584]{1,0:T(8,128)(2,1)S(1)} %bitcast.111, bf16[1792,512]{1,0:T(8,128)(2,1)S(1)} %collective-permute-done.4, pred[]{:T(512)S(6)} %eq.42, bf16[1792,2048]{1,0:T(8,128)(2,1)S(1)} %bitcast.114, s32[]{:T(128)S(6)} %select_n.208), kind=kOutput, calls=%fused_computation | convolution fusion | flops 2819489792 | bytes 12320773 | tf_op jit(solution)/shard_map/dot_general | solution.py:75
  128.5 4.4 %exponential_reduce_fusion = (f32[1536]{0:T(1024)S(1)}, f32[1536]{0:T(1024)S(1)}, f32[1536,512]{1,0:T(8,128)S(1)}) fusion(pred[768,512]{1,0:T(8,128)(4,1)S(1)} %get-tuple-element.27, f32[1536,512]{1,0:T(8,128)S(1)} %fusion, bf16[1792,512]{1,0:T(8,128)(2,1)} %copy-done.3, pred[]{:T(512)S(6)} %eq.42, bf16[1792,2048]{1,0:T(8,128)(2,1)S(1)} %bitcast.114, ...), kind=kOutput, calls=%fused_computation.12 | convolution fusion | flops 2824205312 | bytes 15872005 | tf_op jit(solution)/shard_map/dot_general | solution.py:75
  133.5 1.6 copy-done.2
  136.8 3.9 %collective-permute-start.6 = (f32[4,2,768]{2,1,0:T(2,128)S(1)}, f32[4,2,768]{2,1,0:T(2,128)S(1)}, u32[]{:S(2)}, u32[]{:S(2)}) collective-permute-start(f32[4,2,768]{2,1,0:T(2,128)S(1)} %pad_maximum_fusion.1), channel_id=1, source_target_pairs={{0,64},{64,0},{128,192},{192,128},{1,65},{65,1},{129,193},{193,129... | collective-permute-start | bytes 73736 | tf_op jit(solution)/shard_map/ppermute | solution.py:16
  140.7 2.1 collective-permute-done.6
  142.7 1.8 collective-permute-done.7
  146.0 1.5 collective-permute-start.10
  149.6 1.9 collective-permute-done.10
  152.8 3.2 %collective-permute-start.15 = (f32[4,2,768]{2,1,0:T(2,128)S(1)}, f32[4,2,768]{2,1,0:T(2,128)S(1)}, u32[]{:S(2)}, u32[]{:S(2)}) collective-permute-start(f32[4,2,768]{2,1,0:T(2,128)S(1)} %bitcast.123), channel_id=1, source_target_pairs={{0,8},{1,9},{2,10},{3,11},{4,12},{5,13},{6,14},{7,15},{8,0},{9,1},... | collective-permute-start | bytes 73736 | tf_op jit(solution)/shard_map/ppermute | solution.py:20
  156.1 2.4 collective-permute-start.16
  158.7 2.3 collective-permute-start.13
  162.3 3.4 %collective-permute-start.17 = (f32[4,2,768]{2,1,0:T(2,128)S(1)}, f32[4,2,768]{2,1,0:T(2,128)S(1)}, u32[]{:S(2)}, u32[]{:S(2)}) collective-permute-start(f32[4,2,768]{2,1,0:T(2,128)S(1)} %bitcast.128), channel_id=1, source_target_pairs={{0,12},{1,13},{2,14},{3,15},{4,8},{5,9},{6,10},{7,11},{8,4},{9,5},... | collective-permute-start | bytes 73736 | tf_op jit(solution)/shard_map/ppermute | solution.py:20
  168.3 2.6 collective-permute-done.18
  170.8 3.4 %multiply_convert_fusion = bf16[2,768,512]{2,1,0:T(8,128)(2,1)S(1)} fusion(f32[2,768,512]{2,1,0:T(8,128)S(1)} %bitcast.109, f32[2,768,512]{2,1,0:T(8,128)} %copy-done.2, f32[2,768]{1,0:T(2,128)S(1)} %get-tuple-element.24, f32[768,512]{1,0:T(8,128)} %get-tuple-element.26, f32[2,768]{1,0:T(2,128)S(1)} %get-tuple-element.25, f32[768]{0:T(1024)S(1)} %broadcast_multiply_fusion), kind=kLoop, calls=%fused_computation.9 | loop fusion | flops 9437184 | bytes 9452544 | tf_op jit(solution)/shard_map/convert_element_type | solution.py:114
  174.4 3.1 %collective-permute-start.19 = (bf16[768,512]{1,0:T(8,128)(2,1)S(1)}, bf16[768,512]{1,0:T(8,128)(2,1)S(1)}, u32[]{:S(2)}, u32[]{:S(2)}) collective-permute-start(bf16[768,512]{1,0:T(8,128)(2,1)S(1)} %get-tuple-element.6), channel_id=1, source_target_pairs={{0,128},{64,192},{128,0},{192,64},{1,129},{65,193},{129,1},{193,65... | collective-permute-start | bytes 2359304 | tf_op jit(solution)/shard_map/ppermute | solution.py:16
  177.5 1.8 collective-permute-start.21
  179.3 3.3 %fusion.29 = f32[768,1792]{1,0:T(8,128)S(1)} fusion(bf16[768,512]{1,0:T(8,128)(2,1)S(1)} %get-tuple-element.7, bf16[1792,2048]{1,0:T(8,128)(2,1)} %param.5, s32[]{:T(128)S(6)} %select_n.208), kind=kOutput, calls=%fused_computation.27 | convolution fusion | flops 1409286144 | bytes 8126468 | tf_op jit(solution)/shard_map/dot_general | solution.py:120
  182.6 13.4 %collective-permute-done.19 = bf16[768,512]{1,0:T(8,128)(2,1)S(1)} collective-permute-done((bf16[768,512]{1,0:T(8,128)(2,1)S(1)}, bf16[768,512]{1,0:T(8,128)(2,1)S(1)}, u32[]{:S(2)}, u32[]{:S(2)}) %collective-permute-start.19) | collective-permute-done | bytes 786464 | tf_op jit(solution)/shard_map/ppermute | solution.py:16
  195.9 3.1 %fusion.23 = f32[768,1792]{1,0:T(8,128)S(1)} fusion(bf16[768,512]{1,0:T(8,128)(2,1)S(1)} %collective-permute-done.19, bf16[1792,2048]{1,0:T(8,128)(2,1)} %param.5, s32[]{:T(128)S(6)} %select_n.215), kind=kOutput, calls=%fused_computation.21 | convolution fusion | flops 1409286144 | bytes 8126468 | tf_op jit(solution)/shard_map/dot_general | solution.py:120
  199.1 8.4 %collective-permute-done.20 = bf16[768,512]{1,0:T(8,128)(2,1)S(1)} collective-permute-done((bf16[768,512]{1,0:T(8,128)(2,1)S(1)}, bf16[768,512]{1,0:T(8,128)(2,1)S(1)}, u32[]{:S(2)}, u32[]{:S(2)}) %collective-permute-start.20) | collective-permute-done | bytes 786464 | tf_op jit(solution)/shard_map/ppermute | solution.py:16
  207.5 1.6 fusion.21
  209.6 4.1 %add_add_fusion = f32[768,1792]{1,0:T(8,128)} fusion(f32[768,1792]{1,0:T(8,128)S(1)} %fusion.21, f32[768,1792]{1,0:T(8,128)S(1)} %fusion.29, f32[768,1792]{1,0:T(8,128)S(1)} %fusion.23, bf16[768,512]{1,0:T(8,128)(2,1)S(1)} %collective-permute-done.21, bf16[1792,2048]{1,0:T(8,128)(2,1)S(1)} %bitcast.116, s32[]{:T(128)S(6)} %select_n.217), kind=kOutput, calls=%fused_computation.4 | convolution fusion | flops 1413414912 | bytes 24641540 | tf_op jit(solution)/shard_map/dot_general | solution.py:120
  213.8 1.9 fusion.33
  215.8 3.1 %collective-permute-done.22 = bf16[384,1792]{1,0:T(8,128)(2,1)S(1)} collective-permute-done((bf16[384,1792]{1,0:T(8,128)(2,1)S(1)}, bf16[384,1792]{1,0:T(8,128)(2,1)S(1)}, u32[]{:S(2)}, u32[]{:S(2)}) %collective-permute-start.22) | collective-permute-done | bytes 1376288 | tf_op jit(solution)/shard_map/ppermute | solution.py:20
  218.9 3.6 %bitcast_add_fusion = f32[384,1792]{1,0:T(8,128)} fusion(bf16[384,1792]{1,0:T(8,128)(2,1)S(1)} %collective-permute-done.22, f32[2,384,1792]{2,1,0:T(8,128)} %bitcast.19, s32[]{:T(128)S(6)} %select_n.219), kind=kLoop, calls=%fused_computation.16 | loop fusion | flops 1376256 | bytes 6881284 | tf_op jit(solution)/shard_map/add | solution.py:132
  222.5 1.9 convert_element_type.89
  226.0 2.6 collective-permute-start.24
  230.0 6.4 %collective-permute-done.23 = bf16[96,1792]{1,0:T(8,128)(2,1)S(1)} collective-permute-done((bf16[96,1792]{1,0:T(8,128)(2,1)}, bf16[96,1792]{1,0:T(8,128)(2,1)S(1)}, u32[]{:S(2)}, u32[]{:S(2)}) %collective-permute-start.23) | collective-permute-done | bytes 344096 | tf_op jit(solution)/shard_map/ppermute | solution.py:20
  236.5 8.0 %collective-permute-done.24 = bf16[96,1792]{1,0:T(8,128)(2,1)} collective-permute-done((bf16[96,1792]{1,0:T(8,128)(2,1)}, bf16[96,1792]{1,0:T(8,128)(2,1)}, u32[]{:S(2)}, u32[]{:S(2)}) %collective-permute-start.24) | collective-permute-done | bytes 344096 | tf_op jit(solution)/shard_map/ppermute | solution.py:20
  244.5 2.4 collective-permute-done.25
  246.8 1.6 fusion.35
  250.7 2.1 collective-permute-start.26
  252.8 2.5 collective-permute-start.28
  255.3 3.0 %collective-permute-start.29 = (bf16[12,1792]{1,0:T(8,128)(2,1)S(1)}, bf16[12,1792]{1,0:T(8,128)(2,1)S(1)}, u32[]{:S(2)}, u32[]{:S(2)}) collective-permute-start(bf16[12,1792]{1,0:T(8,128)(2,1)S(1)} %get-tuple-element.15), channel_id=1, source_target_pairs={{0,8},{1,9},{2,10},{3,11},{4,12},{5,13},{6,14},{7,15},{8,0},{9,1},... | collective-permute-start | bytes 129032 | tf_op jit(solution)/shard_map/ppermute | solution.py:20
  258.2 2.5 collective-permute-start.30
  262.3 2.1 collective-permute-start.32
  265.5 1.5 collective-permute-done.31
  267.1 2.3 collective-permute-done.32
  270.4 4.5 %collective-permute-start.33 = (bf16[6,1792]{1,0:T(8,128)(2,1)S(1)}, bf16[6,1792]{1,0:T(8,128)(2,1)S(1)}, u32[]{:S(2)}, u32[]{:S(2)}) collective-permute-start(bf16[6,1792]{1,0:T(8,128)(2,1)S(1)} %get-tuple-element.21), channel_id=1, source_target_pairs={{0,64},{64,0},{128,192},{192,128},{1,65},{65,1},{129,193},{193,129... | collective-permute-start | bytes 64520 | tf_op jit(solution)/shard_map/ppermute | solution.py:16
  (114 shorter events, 30.9 us)
Async XLA Ops:
  7.2 1.8 copy-start
  7.2 101.1 %all-gather.2.cloned.1.call-start = ((), (), s32[]{:S(2)}) async-start(), calls=%async_computation | async-start | bytes 11182080 | tf_op jit(solution)/shard_map/all_gather | solution.py:56
  9.0 4.8 %collective-permute-start.1 = (bf16[48,896]{1,0:T(8,128)(2,1)S(1)}, bf16[48,896]{1,0:T(8,128)(2,1)S(1)}, u32[]{:S(2)}, u32[]{:S(2)}) collective-permute-start(bf16[48,896]{1,0:T(8,128)(2,1)S(1)} %fusion.108), channel_id=1, source_target_pairs={{0,128},{64,192},{128,0},{192,64},{1,129},{65,193},{129,1},{193,65... | collective-permute-start | bytes 258056 | tf_op jit(solution)/shard_map/ppermute | solution.py:16
  11.3 6.1 %collective-permute-start.2 = (bf16[48,896]{1,0:T(8,128)(2,1)S(1)}, bf16[48,896]{1,0:T(8,128)(2,1)S(1)}, u32[]{:S(2)}, u32[]{:S(2)}) collective-permute-start(bf16[48,896]{1,0:T(8,128)(2,1)S(1)} %fusion.108), channel_id=1, source_target_pairs={{0,64},{64,0},{128,192},{192,128},{1,65},{65,1},{129,193},{193,129... | collective-permute-start | bytes 258056 | tf_op jit(solution)/shard_map/ppermute | solution.py:16
  12.0 5.4 %collective-permute-start.3 = (bf16[48,896]{1,0:T(8,128)(2,1)S(1)}, bf16[48,896]{1,0:T(8,128)(2,1)S(1)}, u32[]{:S(2)}, u32[]{:S(2)}) collective-permute-start(bf16[48,896]{1,0:T(8,128)(2,1)S(1)} %fusion.108), channel_id=1, source_target_pairs={{0,192},{64,128},{128,64},{192,0},{1,193},{65,129},{129,65},{193,1... | collective-permute-start | bytes 258056 | tf_op jit(solution)/shard_map/ppermute | solution.py:16
  17.4 5.0 %copy-start.6 = (s32[384]{0:T(512)S(1)}, s32[384]{0:T(512)}, u32[]{:S(2)}) copy-start(s32[384]{0:T(512)} %param.6) | copy-start | bytes 4612
  17.4 5.0 %copy-start.7 = (s32[384]{0:T(512)S(1)}, s32[384]{0:T(512)}, u32[]{:S(2)}) copy-start(s32[384]{0:T(512)} %param.7) | copy-start | bytes 4612
  21.5 103.8 %collective-permute-start.4 = (bf16[1792,512]{1,0:T(8,128)(2,1)}, bf16[1792,512]{1,0:T(8,128)(2,1)S(1)}, u32[]{:S(2)}, u32[]{:S(2)}) collective-permute-start(bf16[1792,512]{1,0:T(8,128)(2,1)} %constant_dynamic-slice_fusion.6), channel_id=1, source_target_pairs={{0,192},{64,128},{128,64},{192,0},{1,193},{65,129},{129,65},{193,1... | collective-permute-start | bytes 5505032 | tf_op jit(solution)/shard_map/ppermute | solution.py:16
  22.4 5.5 %collective-permute-start = (s32[2,384]{1,0:T(2,128)S(1)}, s32[2,384]{1,0:T(2,128)S(1)}, u32[]{:S(2)}, u32[]{:S(2)}) collective-permute-start(s32[2,384]{1,0:T(2,128)S(1)} %get-tuple-element.29), channel_id=1, source_target_pairs={{0,64},{64,0},{128,192},{192,128},{1,65},{65,1},{129,193},{193,129... | collective-permute-start | bytes 9224 | tf_op jit(solution)/shard_map/ppermute | solution.py:16
  108.3 17.0 %slice-start = ((s8[7340032]{0:T(1024)(128)(4,1)}), s8[4194304]{0:T(1024)(128)(4,1)S(1)}, s32[]{:S(2)}) async-start(s8[7340032]{0:T(1024)(128)(4,1)} %bitcast.113), calls=%async_computation.1 | async-start | bytes 8388608
  121.5 3.9 %slice-start.1 = ((s8[7340032]{0:T(1024)(128)(4,1)}), s8[3145728]{0:T(1024)(128)(4,1)S(1)}, s32[]{:S(2)}) async-start(s8[7340032]{0:T(1024)(128)(4,1)} %bitcast.113), calls=%async_computation.2 | async-start | bytes 6291456
  125.4 3.1 %copy-start.3 = (bf16[1792,512]{1,0:T(8,128)(2,1)}, bf16[1792,512]{1,0:T(8,128)(2,1)S(1)}, u32[]{:S(2)}) copy-start(bf16[1792,512]{1,0:T(8,128)(2,1)S(1)} %collective-permute-done.4) | copy-start | bytes 5505028
  133.5 1.6 copy-start.2
  135.2 23.2 %copy-start.5 = (f32[1,2,4,8,2,6]{3,2,5,4,1,0:T(4,128)S(1)}, f32[1,2,4,8,2,6]{3,2,5,4,1,0:T(4,128)}, u32[]{:S(2)}) copy-start(f32[1,2,4,8,2,6]{3,2,5,4,1,0:T(4,128)} %get-tuple-element.18) | copy-start | bytes 9220
  136.1 4.5 %collective-permute-start.5 = (f32[4,2,768]{2,1,0:T(2,128)S(1)}, f32[4,2,768]{2,1,0:T(2,128)S(1)}, u32[]{:S(2)}, u32[]{:S(2)}) collective-permute-start(f32[4,2,768]{2,1,0:T(2,128)S(1)} %pad_maximum_fusion.1), channel_id=1, source_target_pairs={{0,128},{64,192},{128,0},{192,64},{1,129},{65,193},{129,1},{193,65... | collective-permute-start | bytes 73736 | tf_op jit(solution)/shard_map/ppermute | solution.py:16
  136.8 5.9 %collective-permute-start.6 = (f32[4,2,768]{2,1,0:T(2,128)S(1)}, f32[4,2,768]{2,1,0:T(2,128)S(1)}, u32[]{:S(2)}, u32[]{:S(2)}) collective-permute-start(f32[4,2,768]{2,1,0:T(2,128)S(1)} %pad_maximum_fusion.1), channel_id=1, source_target_pairs={{0,64},{64,0},{128,192},{192,128},{1,65},{65,1},{129,193},{193,129... | collective-permute-start | bytes 73736 | tf_op jit(solution)/shard_map/ppermute | solution.py:16
  140.7 3.8 %collective-permute-start.7 = (f32[4,2,768]{2,1,0:T(2,128)S(1)}, f32[4,2,768]{2,1,0:T(2,128)S(1)}, u32[]{:S(2)}, u32[]{:S(2)}) collective-permute-start(f32[4,2,768]{2,1,0:T(2,128)S(1)} %pad_maximum_fusion.1), channel_id=1, source_target_pairs={{0,192},{64,128},{128,64},{192,0},{1,193},{65,129},{129,65},{193,1... | collective-permute-start | bytes 73736 | tf_op jit(solution)/shard_map/ppermute | solution.py:16
  144.5 1.5 collective-permute-start.8
  146.0 5.4 %collective-permute-start.10 = (f32[4,2,768]{2,1,0:T(2,128)S(1)}, f32[4,2,768]{2,1,0:T(2,128)S(1)}, u32[]{:S(2)}, u32[]{:S(2)}) collective-permute-start(f32[4,2,768]{2,1,0:T(2,128)S(1)} %add.284), channel_id=1, source_target_pairs={{0,32},{1,33},{2,34},{3,35},{4,36},{5,37},{6,38},{7,39},{8,40},{9,... | collective-permute-start | bytes 73736 | tf_op jit(solution)/shard_map/ppermute | solution.py:20
  147.6 5.0 %collective-permute-start.11 = (f32[4,2,768]{2,1,0:T(2,128)S(1)}, f32[4,2,768]{2,1,0:T(2,128)S(1)}, u32[]{:S(2)}, u32[]{:S(2)}) collective-permute-start(f32[4,2,768]{2,1,0:T(2,128)S(1)} %add.284), channel_id=1, source_target_pairs={{0,48},{1,49},{2,50},{3,51},{4,52},{5,53},{6,54},{7,55},{8,56},{9,... | collective-permute-start | bytes 73736 | tf_op jit(solution)/shard_map/ppermute | solution.py:20
  149.0 3.8 %collective-permute-start.9 = (f32[4,2,768]{2,1,0:T(2,128)S(1)}, f32[4,2,768]{2,1,0:T(2,128)S(1)}, u32[]{:S(2)}, u32[]{:S(2)}) collective-permute-start(f32[4,2,768]{2,1,0:T(2,128)S(1)} %add.284), channel_id=1, source_target_pairs={{0,16},{1,17},{2,18},{3,19},{4,20},{5,21},{6,22},{7,23},{8,24},{9,... | collective-permute-start | bytes 73736 | tf_op jit(solution)/shard_map/ppermute | solution.py:20
  152.8 9.5 %collective-permute-start.15 = (f32[4,2,768]{2,1,0:T(2,128)S(1)}, f32[4,2,768]{2,1,0:T(2,128)S(1)}, u32[]{:S(2)}, u32[]{:S(2)}) collective-permute-start(f32[4,2,768]{2,1,0:T(2,128)S(1)} %bitcast.123), channel_id=1, source_target_pairs={{0,8},{1,9},{2,10},{3,11},{4,12},{5,13},{6,14},{7,15},{8,0},{9,1},... | collective-permute-start | bytes 73736 | tf_op jit(solution)/shard_map/ppermute | solution.py:20
  156.1 9.7 %collective-permute-start.16 = (f32[4,2,768]{2,1,0:T(2,128)S(1)}, f32[4,2,768]{2,1,0:T(2,128)S(1)}, u32[]{:S(2)}, u32[]{:S(2)}) collective-permute-start(f32[4,2,768]{2,1,0:T(2,128)S(1)} %bitcast.124), channel_id=1, source_target_pairs={{0,10},{1,11},{2,8},{3,9},{4,14},{5,15},{6,12},{7,13},{8,2},{9,3},... | collective-permute-start | bytes 73736 | tf_op jit(solution)/shard_map/ppermute | solution.py:20
  158.7 8.2 %collective-permute-start.13 = (f32[4,2,768]{2,1,0:T(2,128)S(1)}, f32[4,2,768]{2,1,0:T(2,128)S(1)}, u32[]{:S(2)}, u32[]{:S(2)}) collective-permute-start(f32[4,2,768]{2,1,0:T(2,128)S(1)} %bitcast.125), channel_id=1, source_target_pairs={{0,4},{1,5},{2,6},{3,7},{4,0},{5,1},{6,2},{7,3},{8,12},{9,13},{10,... | collective-permute-start | bytes 73736 | tf_op jit(solution)/shard_map/ppermute | solution.py:20
  161.0 5.9 %collective-permute-start.14 = (f32[4,2,768]{2,1,0:T(2,128)S(1)}, f32[4,2,768]{2,1,0:T(2,128)S(1)}, u32[]{:S(2)}, u32[]{:S(2)}) collective-permute-start(f32[4,2,768]{2,1,0:T(2,128)S(1)} %bitcast.126), channel_id=1, source_target_pairs={{0,6},{1,7},{2,4},{3,5},{4,2},{5,3},{6,0},{7,1},{8,14},{9,15},{10,... | collective-permute-start | bytes 73736 | tf_op jit(solution)/shard_map/ppermute | solution.py:20
  162.2 4.7 %collective-permute-start.12 = (f32[4,2,768]{2,1,0:T(2,128)S(1)}, f32[4,2,768]{2,1,0:T(2,128)S(1)}, u32[]{:S(2)}, u32[]{:S(2)}) collective-permute-start(f32[4,2,768]{2,1,0:T(2,128)S(1)} %bitcast.127), channel_id=1, source_target_pairs={{0,2},{1,3},{2,0},{3,1},{4,6},{5,7},{6,4},{7,5},{8,10},{9,11},{10,... | collective-permute-start | bytes 73736 | tf_op jit(solution)/shard_map/ppermute | solution.py:20
  162.3 5.9 %collective-permute-start.17 = (f32[4,2,768]{2,1,0:T(2,128)S(1)}, f32[4,2,768]{2,1,0:T(2,128)S(1)}, u32[]{:S(2)}, u32[]{:S(2)}) collective-permute-start(f32[4,2,768]{2,1,0:T(2,128)S(1)} %bitcast.128), channel_id=1, source_target_pairs={{0,12},{1,13},{2,14},{3,15},{4,8},{5,9},{6,10},{7,11},{8,4},{9,5},... | collective-permute-start | bytes 73736 | tf_op jit(solution)/shard_map/ppermute | solution.py:20
  165.8 5.0 %collective-permute-start.18 = (f32[4,2,768]{2,1,0:T(2,128)S(1)}, f32[4,2,768]{2,1,0:T(2,128)S(1)}, u32[]{:S(2)}, u32[]{:S(2)}) collective-permute-start(f32[4,2,768]{2,1,0:T(2,128)S(1)} %bitcast.129), channel_id=1, source_target_pairs={{0,14},{1,15},{2,12},{3,13},{4,10},{5,11},{6,8},{7,9},{8,6},{9,7},... | collective-permute-start | bytes 73736 | tf_op jit(solution)/shard_map/ppermute | solution.py:20
  174.4 21.6 %collective-permute-start.19 = (bf16[768,512]{1,0:T(8,128)(2,1)S(1)}, bf16[768,512]{1,0:T(8,128)(2,1)S(1)}, u32[]{:S(2)}, u32[]{:S(2)}) collective-permute-start(bf16[768,512]{1,0:T(8,128)(2,1)S(1)} %get-tuple-element.6), channel_id=1, source_target_pairs={{0,128},{64,192},{128,0},{192,64},{1,129},{65,193},{129,1},{193,65... | collective-permute-start | bytes 2359304 | tf_op jit(solution)/shard_map/ppermute | solution.py:16
  177.5 30.0 %collective-permute-start.20 = (bf16[768,512]{1,0:T(8,128)(2,1)S(1)}, bf16[768,512]{1,0:T(8,128)(2,1)S(1)}, u32[]{:S(2)}, u32[]{:S(2)}) collective-permute-start(bf16[768,512]{1,0:T(8,128)(2,1)S(1)} %get-tuple-element.7), channel_id=1, source_target_pairs={{0,64},{64,0},{128,192},{192,128},{1,65},{65,1},{129,193},{193,129... | collective-permute-start | bytes 2359304 | tf_op jit(solution)/shard_map/ppermute | solution.py:16
  177.5 32.2 %collective-permute-start.21 = (bf16[768,512]{1,0:T(8,128)(2,1)S(1)}, bf16[768,512]{1,0:T(8,128)(2,1)S(1)}, u32[]{:S(2)}, u32[]{:S(2)}) collective-permute-start(bf16[768,512]{1,0:T(8,128)(2,1)S(1)} %get-tuple-element.6), channel_id=1, source_target_pairs={{0,192},{64,128},{128,64},{192,0},{1,193},{65,129},{129,65},{193,1... | collective-permute-start | bytes 2359304 | tf_op jit(solution)/shard_map/ppermute | solution.py:16
  179.3 28.2 %slice-start.2 = ((s8[7340032]{0:T(1024)(128)(4,1)}), s8[4194304]{0:T(1024)(128)(4,1)S(1)}, s32[]{:S(2)}) async-start(s8[7340032]{0:T(1024)(128)(4,1)} %bitcast.115), calls=%async_computation.3 | async-start | bytes 8388608
  182.6 24.9 %slice-start.3 = ((s8[7340032]{0:T(1024)(128)(4,1)}), s8[3145728]{0:T(1024)(128)(4,1)S(1)}, s32[]{:S(2)}) async-start(s8[7340032]{0:T(1024)(128)(4,1)} %bitcast.115), calls=%async_computation.4 | async-start | bytes 6291456
  215.7 3.2 %collective-permute-start.22 = (bf16[384,1792]{1,0:T(8,128)(2,1)S(1)}, bf16[384,1792]{1,0:T(8,128)(2,1)S(1)}, u32[]{:S(2)}, u32[]{:S(2)}) collective-permute-start(bf16[384,1792]{1,0:T(8,128)(2,1)S(1)} %fusion.33), channel_id=1, source_target_pairs={{0,1},{1,0},{2,3},{3,2},{4,5},{5,4},{6,7},{7,6},{8,9},{9,8},{10,11... | collective-permute-start | bytes 4128776 | tf_op jit(solution)/shard_map/ppermute | solution.py:20
  225.3 11.1 %collective-permute-start.23 = (bf16[96,1792]{1,0:T(8,128)(2,1)}, bf16[96,1792]{1,0:T(8,128)(2,1)S(1)}, u32[]{:S(2)}, u32[]{:S(2)}) collective-permute-start(bf16[96,1792]{1,0:T(8,128)(2,1)} %get-tuple-element.8), channel_id=1, source_target_pairs={{0,16},{1,17},{2,18},{3,19},{4,20},{5,21},{6,22},{7,23},{8,24},{9,... | collective-permute-start | bytes 1032200 | tf_op jit(solution)/shard_map/ppermute | solution.py:20
  226.0 18.5 %collective-permute-start.24 = (bf16[96,1792]{1,0:T(8,128)(2,1)}, bf16[96,1792]{1,0:T(8,128)(2,1)}, u32[]{:S(2)}, u32[]{:S(2)}) collective-permute-start(bf16[96,1792]{1,0:T(8,128)(2,1)} %get-tuple-element.10), channel_id=1, source_target_pairs={{0,32},{1,33},{2,34},{3,35},{4,36},{5,37},{6,38},{7,39},{8,40},{9,... | collective-permute-start | bytes 1032200 | tf_op jit(solution)/shard_map/ppermute | solution.py:20
  228.6 18.2 %collective-permute-start.25 = (bf16[96,1792]{1,0:T(8,128)(2,1)S(1)}, bf16[96,1792]{1,0:T(8,128)(2,1)}, u32[]{:S(2)}, u32[]{:S(2)}) collective-permute-start(bf16[96,1792]{1,0:T(8,128)(2,1)S(1)} %get-tuple-element.9), channel_id=1, source_target_pairs={{0,48},{1,49},{2,50},{3,51},{4,52},{5,53},{6,54},{7,55},{8,56},{9,... | collective-permute-start | bytes 1032200 | tf_op jit(solution)/shard_map/ppermute | solution.py:20
  230.0 47.4 %copy-start.1 = (bf16[1,384,3584]{2,1,0:T(8,128)(2,1)S(1)}, bf16[1,384,3584]{2,1,0:T(8,128)(2,1)}, u32[]{:S(2)}) copy-start(bf16[1,384,3584]{2,1,0:T(8,128)(2,1)} %param.4) | copy-start | bytes 8257540
  236.4 8.0 %copy-start.4 = (bf16[96,1792]{1,0:T(8,128)(2,1)}, bf16[96,1792]{1,0:T(8,128)(2,1)S(1)}, u32[]{:S(2)}) copy-start(bf16[96,1792]{1,0:T(8,128)(2,1)S(1)} %collective-permute-done.23) | copy-start | bytes 1032196
  250.7 10.0 %collective-permute-start.26 = (bf16[12,1792]{1,0:T(8,128)(2,1)S(1)}, bf16[12,1792]{1,0:T(8,128)(2,1)S(1)}, u32[]{:S(2)}, u32[]{:S(2)}) collective-permute-start(bf16[12,1792]{1,0:T(8,128)(2,1)S(1)} %get-tuple-element.11), channel_id=1, source_target_pairs={{0,2},{1,3},{2,0},{3,1},{4,6},{5,7},{6,4},{7,5},{8,10},{9,11},{10,... | collective-permute-start | bytes 129032 | tf_op jit(solution)/shard_map/ppermute | solution.py:20
  252.8 9.5 %collective-permute-start.27 = (bf16[12,1792]{1,0:T(8,128)(2,1)S(1)}, bf16[12,1792]{1,0:T(8,128)(2,1)S(1)}, u32[]{:S(2)}, u32[]{:S(2)}) collective-permute-start(bf16[12,1792]{1,0:T(8,128)(2,1)S(1)} %get-tuple-element.17), channel_id=1, source_target_pairs={{0,4},{1,5},{2,6},{3,7},{4,0},{5,1},{6,2},{7,3},{8,12},{9,13},{10,... | collective-permute-start | bytes 129032 | tf_op jit(solution)/shard_map/ppermute | solution.py:20
  252.8 11.8 %collective-permute-start.28 = (bf16[12,1792]{1,0:T(8,128)(2,1)S(1)}, bf16[12,1792]{1,0:T(8,128)(2,1)S(1)}, u32[]{:S(2)}, u32[]{:S(2)}) collective-permute-start(bf16[12,1792]{1,0:T(8,128)(2,1)S(1)} %get-tuple-element.16), channel_id=1, source_target_pairs={{0,6},{1,7},{2,4},{3,5},{4,2},{5,3},{6,0},{7,1},{8,14},{9,15},{10,... | collective-permute-start | bytes 129032 | tf_op jit(solution)/shard_map/ppermute | solution.py:20
  255.3 9.4 %collective-permute-start.29 = (bf16[12,1792]{1,0:T(8,128)(2,1)S(1)}, bf16[12,1792]{1,0:T(8,128)(2,1)S(1)}, u32[]{:S(2)}, u32[]{:S(2)}) collective-permute-start(bf16[12,1792]{1,0:T(8,128)(2,1)S(1)} %get-tuple-element.15), channel_id=1, source_target_pairs={{0,8},{1,9},{2,10},{3,11},{4,12},{5,13},{6,14},{7,15},{8,0},{9,1},... | collective-permute-start | bytes 129032 | tf_op jit(solution)/shard_map/ppermute | solution.py:20
  258.2 7.3 %collective-permute-start.30 = (bf16[12,1792]{1,0:T(8,128)(2,1)S(1)}, bf16[12,1792]{1,0:T(8,128)(2,1)S(1)}, u32[]{:S(2)}, u32[]{:S(2)}) collective-permute-start(bf16[12,1792]{1,0:T(8,128)(2,1)S(1)} %get-tuple-element.14), channel_id=1, source_target_pairs={{0,10},{1,11},{2,8},{3,9},{4,14},{5,15},{6,12},{7,13},{8,2},{9,3},... | collective-permute-start | bytes 129032 | tf_op jit(solution)/shard_map/ppermute | solution.py:20
  260.8 6.3 %collective-permute-start.31 = (bf16[12,1792]{1,0:T(8,128)(2,1)S(1)}, bf16[12,1792]{1,0:T(8,128)(2,1)S(1)}, u32[]{:S(2)}, u32[]{:S(2)}) collective-permute-start(bf16[12,1792]{1,0:T(8,128)(2,1)S(1)} %get-tuple-element.13), channel_id=1, source_target_pairs={{0,12},{1,13},{2,14},{3,15},{4,8},{5,9},{6,10},{7,11},{8,4},{9,5},... | collective-permute-start | bytes 129032 | tf_op jit(solution)/shard_map/ppermute | solution.py:20
  262.3 7.1 %collective-permute-start.32 = (bf16[12,1792]{1,0:T(8,128)(2,1)S(1)}, bf16[12,1792]{1,0:T(8,128)(2,1)S(1)}, u32[]{:S(2)}, u32[]{:S(2)}) collective-permute-start(bf16[12,1792]{1,0:T(8,128)(2,1)S(1)} %get-tuple-element.12), channel_id=1, source_target_pairs={{0,14},{1,15},{2,12},{3,13},{4,10},{5,11},{6,8},{7,9},{8,6},{9,7},... | collective-permute-start | bytes 129032 | tf_op jit(solution)/shard_map/ppermute | solution.py:20
  270.4 6.4 %collective-permute-start.33 = (bf16[6,1792]{1,0:T(8,128)(2,1)S(1)}, bf16[6,1792]{1,0:T(8,128)(2,1)S(1)}, u32[]{:S(2)}, u32[]{:S(2)}) collective-permute-start(bf16[6,1792]{1,0:T(8,128)(2,1)S(1)} %get-tuple-element.21), channel_id=1, source_target_pairs={{0,64},{64,0},{128,192},{192,128},{1,65},{65,1},{129,193},{193,129... | collective-permute-start | bytes 64520 | tf_op jit(solution)/shard_map/ppermute | solution.py:16
Sparse Core Ops, SparseCore 0:
  18.7 89.6 all-gather.1

commit v2 on v0

v2 whole, which is shorter than its diff:
```python
import functools

import jax
import jax.numpy as jnp
from jax import lax
from jax.experimental import pallas as pl
from jax.experimental.pallas import tpu as pltpu
from jax.sharding import Mesh, PartitionSpec as P

softcap_limit = 30.0
kl_weight = 0.5
loss_scale = 16.0

N_Y, N_Z, N_C, N_X = 4, 8, 2, 4
LINE = ("rep", "tok")
ROWS = 192
QUARTER = 512
HALF_D = 1792
TILE = 256
VMEM = 50 * 1024 * 1024
F32, BF16 = jnp.float32, jnp.bfloat16


def line_xor(block, k):
    k = (k % 2) * 2 + k // 2
    return lax.ppermute(block, LINE, [(x, x ^ k) for x in range(N_X)])


def axis_xor(block, axis, k):
    return lax.ppermute(block, axis, [(i, i ^ k) for i in range(lax.axis_size(axis))])


def logits_kernel(at, own, nbr, far, head_a, head_b, got_a, got_b, tgt, logits, stats, rows, sums):
    step = pl.program_id(0)
    tok = at[0]

    @pl.when(step == 0)
    def _():
        for side in range(2):
            half = tok if side == 0 else 1 - tok
            begin = pl.multiple_of(half * HALF_D, HALF_D)
            to = pl.ds(side * HALF_D, HALF_D)
            rows[0:ROWS, to] = own[:, pl.ds(begin, HALF_D)]
            rows[ROWS : 2 * ROWS, to] = nbr[:, pl.ds(begin, HALF_D)]
            for part in range(2):
                rows[2 * ROWS :, pl.ds(side * HALF_D + part * 896, 896)] = far[
                    half * 2 + part
                ].reshape(2 * ROWS, 896)
        sums[...] = jnp.zeros_like(sums)

    def one(head, got, core):
        raw = jnp.dot(rows[:, :HALF_D], head[...], preferred_element_type=F32)
        raw = raw + jnp.dot(rows[:, HALF_D:], got[...], preferred_element_type=F32)
        capped = softcap_limit * jnp.tanh(raw * (1.0 / softcap_limit))
        far_part = capped[2 * ROWS :].reshape(8, 2, 24, TILE)
        blocks = [
            capped[:ROWS],
            capped[ROWS : 2 * ROWS],
            far_part[:, 0].reshape(ROWS, TILE),
            far_part[:, 1].reshape(ROWS, TILE),
        ]
        lane = lax.broadcasted_iota(jnp.int32, (ROWS, TILE), 1) + at[2 + core]
        for j in range(4):
            mine = blocks[j]
            shared = blocks[j ^ 1].astype(BF16).astype(F32)
            logits[j] = mine
            partner = jnp.exp(shared)
            hit = lane == tgt[j // 2]
            terms = (
                jnp.exp(mine),
                partner,
                jnp.where(hit, mine, 0.0),
                partner * (shared - mine),
            )
            for s, term in enumerate(terms):
                sums[s, j] += term[:, :128] + term[:, 128:]

    @pl.when(step == 0)
    def _():
        one(head_a, got_a, 0)

    @pl.when(step == 1)
    def _():
        one(head_b, got_b, 1)
        lane = lax.broadcasted_iota(jnp.int32, (ROWS, 128), 1)
        for j in range(4):
            wide = jnp.zeros((ROWS, 128), F32)
            for s in range(4):
                wide = jnp.where(lane == s, jnp.sum(sums[s, j], axis=1, keepdims=True), wide)
            wide = jnp.concatenate([wide, jnp.zeros((256 - ROWS, 128), F32)], axis=0)
            stats[j] = wide.T[:8]


def logits_call(at, own, nbr, far, head, mate, got, got_mate, tgt, part):
    def whole(*shape):
        return pl.BlockSpec(shape, lambda s, at: (0,) * len(shape))

    return pl.pallas_call(
        logits_kernel,
        grid_spec=pltpu.PrefetchScalarGridSpec(
            num_scalar_prefetch=1,
            grid=(2,),
            in_specs=[
                whole(ROWS, 2 * HALF_D),
                whole(ROWS, 2 * HALF_D),
                whole(4, 8, 48, 896),
                pl.BlockSpec((HALF_D, TILE), lambda s, at: (0, at[1] * 2 + part)),
                pl.BlockSpec((HALF_D, TILE), lambda s, at: (0, at[1] * 2 + part)),
                whole(HALF_D, TILE),
                whole(HALF_D, TILE),
                whole(2, ROWS, 1),
            ],
            out_specs=[
                pl.BlockSpec((4, ROWS, TILE), lambda s, at: (0, 0, s)),
                whole(4, 8, 256),
            ],
            scratch_shapes=[
                pltpu.VMEM((4 * ROWS, 2 * HALF_D), BF16),
                pltpu.VMEM((4, 4, ROWS, 128), F32),
            ],
        ),
        out_shape=[
            jax.ShapeDtypeStruct((4, ROWS, 2 * TILE), F32),
            jax.ShapeDtypeStruct((4, 8, 256), F32),
        ],
        compiler_params=pltpu.CompilerParams(vmem_limit_bytes=VMEM),
        cost_estimate=pl.CostEstimate(
            flops=4 * ROWS * 2 * TILE * 2 * HALF_D * 2, bytes_accessed=16 << 20, transcendentals=1 << 21
        ),
        name="logits",
    )(at, own, nbr, far, head, mate, got, got_mate, tgt)


def grad_kernel(at, first, second, stats, tgt, mask, mine, theirs, scales):
    step = pl.program_id(0)

    @pl.when(step == 0)
    def _():
        for j in range(4):
            total = stats[j].T
            weight = loss_scale * mask[j // 2]
            scales[0, j] = (1.0 + kl_weight) * weight / total[:ROWS, 0:1]
            scales[1, j] = kl_weight * weight / total[:ROWS, 1:2]

    core, part = step // 2, step % 2
    column = lax.broadcasted_iota(jnp.int32, (ROWS, TILE), 1)
    column = column + jnp.where(core == 0, at[2], at[3]) + part * TILE

    def work(logits):
        for j in range(4):
            own = logits[j]
            shared = logits[j ^ 1].astype(BF16).astype(F32)
            weight = loss_scale * mask[j // 2]
            hit = jnp.where(column == tgt[j // 2], weight, 0.0)
            slope = own * (1.0 / softcap_limit)
            value = jnp.exp(own) * scales[0, j] - hit - jnp.exp(shared) * scales[1, j]
            value = (value * (1.0 - slope * slope)).astype(BF16)
            if j % 2 == 0:
                mine[j // 2] = value
            else:
                theirs[j // 2] = value

    @pl.when(part == 0)
    def _():
        work(first)

    @pl.when(part == 1)
    def _():
        work(second)


def grad_call(at, first, second, stats, tgt, mask):
    def whole(*shape):
        return pl.BlockSpec(shape, lambda s, at: (0,) * len(shape))

    out = pl.BlockSpec((2, ROWS, TILE), lambda s, at: (0, 0, s))
    return pl.pallas_call(
        grad_kernel,
        grid_spec=pltpu.PrefetchScalarGridSpec(
            num_scalar_prefetch=1,
            grid=(4,),
            in_specs=[
                pl.BlockSpec((4, ROWS, TILE), lambda s, at: (0, 0, s // 2)),
                pl.BlockSpec((4, ROWS, TILE), lambda s, at: (0, 0, s // 2)),
                whole(4, 8, 256),
                whole(2, ROWS, 1),
                whole(2, ROWS, 1),
            ],
            out_specs=[out, out],
            scratch_shapes=[pltpu.VMEM((2, 4, ROWS, 1), F32)],
        ),
        out_shape=[jax.ShapeDtypeStruct((2, ROWS, 4 * TILE), BF16)] * 2,
        compiler_params=pltpu.CompilerParams(vmem_limit_bytes=VMEM),
        name="logit_grad",
    )(at, first, second, stats, tgt, mask)


def terms_kernel(at, grad, head, mate, *rest, order):
    acc, out = rest if len(rest) == 2 else (None, rest[0])
    contract = (((1,), (1,)), ((), ()))
    left = jnp.concatenate([grad[k] for k in order], axis=0)
    total = lax.dot_general(left[:, :QUARTER], head[...], contract, preferred_element_type=F32)
    total = total + lax.dot_general(left[:, QUARTER:], mate[...], contract, preferred_element_type=F32)
    if acc is not None:
        total = total + acc[...]
    out[...] = total


def terms_call(at, grad, head, mate, acc, k):
    order = (0, 1) if k < 2 else (1, 0)

    def weights(s, at):
        return (s, at[1] ^ k)

    tile = pl.BlockSpec((2 * ROWS, TILE), lambda s, at: (0, s))
    accs = [] if acc is None else [acc]
    return pl.pallas_call(
        functools.partial(terms_kernel, order=order),
        grid_spec=pltpu.PrefetchScalarGridSpec(
            num_scalar_prefetch=1,
            grid=(HALF_D // TILE,),
            in_specs=[
                pl.BlockSpec((2, ROWS, 4 * TILE), lambda s, at: (0, 0, 0)),
                pl.BlockSpec((TILE, QUARTER), weights),
                pl.BlockSpec((TILE, QUARTER), weights),
            ] + [tile] * len(accs),
            out_specs=tile,
        ),
        out_shape=jax.ShapeDtypeStruct((2 * ROWS, HALF_D), F32),
        compiler_params=pltpu.CompilerParams(vmem_limit_bytes=VMEM),
        cost_estimate=pl.CostEstimate(
            flops=2 * 2 * ROWS * HALF_D * 2 * QUARTER, bytes_accessed=8 << 20, transcendentals=0
        ),
        name="gradient_terms",
    )(at, grad, head, mate, *accs)


def add_over_slice(stats):
    for k in (1, 2):
        other = line_xor(stats, k)
        stats = stats + jnp.stack([other[j ^ k] for j in range(4)])
    for k in (1, 2):
        stats = stats + axis_xor(stats, "y", k)
    for k in (1, 2, 4):
        stats = stats + axis_xor(stats, "z", k)
    return stats


def pick_rows(block, count, core):
    out = lax.broadcasted_iota(jnp.int32, (count, 2 * count), 0)
    src = lax.broadcasted_iota(jnp.int32, (count, 2 * count), 1)
    pick = (src == out // 6 * 12 + core * 6 + out % 6).astype(BF16)
    return jnp.dot(pick, block, preferred_element_type=F32).astype(BF16)


def shards(hidden, head, targets, loss_mask):
    rep, tok, y, z, core = (lax.axis_index(a) for a in ("rep", "tok", "y", "z", "core"))
    x = tok * 2 + rep
    states = hidden[0]

    slab = pick_rows(lax.dynamic_slice(states, (z * 48, y * 896), (48, 896)), 24, core)
    piece = jnp.concatenate([line_xor(slab, 2), line_xor(slab, 3)], axis=0)[None]
    far = lax.all_gather(piece, ("y", "z"), axis=0, tiled=True).reshape(4, 8, 48, 896)

    got, got_mate = [], []
    for part in range(2):
        sent = lax.dynamic_slice(head, (0, (3 - x) * QUARTER + part * TILE), (HALF_D, TILE))
        got.append(line_xor(sent, 3))
        got_mate.append(axis_xor(got[-1], "core", 1))
    own = pick_rows(states, ROWS, core)
    nbr = line_xor(own, 1)
    mate = axis_xor(head, "core", 1)

    voc = (y * 8 + z) * 2
    begin = [(voc + c) * 2048 + x * QUARTER for c in (core, 1 - core)]
    scal = jnp.stack([targets, loss_mask]).reshape(2, 32, 2, 6)
    scal = lax.dynamic_index_in_dim(scal, core, 2, keepdims=False).reshape(2, ROWS)
    scal = jnp.stack([scal, line_xor(scal, 2)], axis=1)[..., None]
    tgt, mask = scal[0], scal[1].astype(F32)

    parts = []
    for part in range(2):
        at = jnp.stack([tok, x, begin[0] + part * TILE, begin[1] + part * TILE]).astype(jnp.int32)
        parts.append(
            logits_call(at, own, nbr, far, head, mate, got[part], got_mate[part], tgt, part)
        )
    at = jnp.stack([tok, x, begin[0], begin[1]]).astype(jnp.int32)
    stats = add_over_slice(parts[0][1] + parts[1][1])

    mine, theirs = grad_call(at, parts[0][0], parts[1][0], stats, tgt, mask)
    grads = [mine, line_xor(theirs, 1), line_xor(mine, 2), line_xor(theirs, 3)]
    terms = None
    for k, grad in enumerate(grads):
        terms = terms_call(at, grad, head, mate, terms, k)

    own_total, partner_total, picked, cross = (stats[0, s, :ROWS] for s in range(4))
    own_lse, partner_lse = jnp.log(own_total), jnp.log(partner_total)
    loss = mask[0, :, 0] * (
        own_lse - picked + kl_weight * (cross / partner_total - partner_lse + own_lse)
    )
    pair = jnp.stack([loss, axis_xor(loss, "core", 1)]).reshape(2, 32, 6)
    pair = jnp.where(core == 0, pair, pair[::-1])
    token_loss = pair.transpose(1, 0, 2).reshape(1, 384)

    terms = terms.reshape(2, 4, 48, HALF_D)
    low = terms.astype(BF16)

    def part_of(array, at, axis):
        return lax.dynamic_index_in_dim(array, at, axis, keepdims=False)

    total = part_of(terms, y, 1)
    for other in [axis_xor(part_of(low, y ^ k, 1), "y", k) for k in (1, 2, 3)]:
        total = total + other.astype(F32)
    out = lax.broadcasted_iota(jnp.int32, (128, 96), 0)
    src = lax.broadcasted_iota(jnp.int32, (128, 96), 1)
    wanted = (out // 8 % 2) * 48 + out // 16 * 6 + out % 8
    pick = ((src == wanted) & (out % 8 < 6)).astype(BF16)
    low = jnp.dot(pick, total.reshape(96, HALF_D).astype(BF16), preferred_element_type=F32)
    low = low.astype(BF16).reshape(8, 16, HALF_D)
    total = part_of(low, z, 0).astype(F32)
    for other in [axis_xor(part_of(low, z ^ k, 0), "z", k) for k in range(1, 8)]:
        total = total + other.astype(F32)
    total = total.astype(BF16).reshape(2, 8, HALF_D)
    got = line_xor(total[1], 2)[:6]
    keep = total[0, :6]
    out = jnp.where(
        tok == 0, jnp.concatenate([keep, got], axis=1), jnp.concatenate([got, keep], axis=1)
    )
    return out[None], token_loss


def solution(mesh):
    fine = Mesh(
        mesh.devices.reshape(2, 2, N_Y, N_Z, N_C), ("rep", "tok", "y", "z", "core")
    )
    voc = ("y", "z", "core")
    placed = (P("rep", "tok", None), P("tok", voc), P("tok"), P("tok"))
    return jax.shard_map(
        shards,
        mesh=fine,
        in_specs=placed,
        out_specs=(P("rep", ("tok", *voc), None), P("rep", "tok")),
        check_vma=False,
    )
```

time: 632 us -> 262 us (0.41)
  blocking collectives: 277 us -> 0 us
  waiting for transfers between devices: 222 us -> 118 us
  Pallas kernels: 0 us -> 53 us
  matrix products: 29.8 us -> 2.74 us
  local copies, waits for them, and re-layouts: 30 us -> 17.6 us
    all_gather x1, waiting for transfers between devices: 186 us -> 33.2 us  [shards(): lax.all_gather(piece, ('y', 'z'), axis=0, tiled=True).reshape(4, 8, 48, 896)]
    unnamed x1 -> x0, blocking collectives: 147 us -> none
    psum x1 -> x0, blocking collectives: 130 us -> none  [shards(): partner_total, cross = lax.psum((partner_part, cross_part), 'voc')]
    pallas_call x0 -> x7, Pallas kernels: none -> 53 us  [the longest x4 28.4 us: terms_call(): pl.pallas_call(functools.partial(terms_kernel, order=order), grid_spec=pl...]
    ppermute x1 -> x31, waiting for transfers between devices: 35 us -> 84.5 us  [the longest x12 51 us: line_xor(): return lax.ppermute(block, LINE, [(x, x ^ k) for x in range(N_X)])]
    unnamed x16 -> x0, starting transfers between devices: 48.8 us -> none
    ppermute x1 -> x31, starting transfers between devices: 1.46 us -> 46.6 us  [the longest x19 24.4 us: axis_xor(): lax.ppermute(block, axis, [(i, i ^ k) for i in range(lax.axis_size(axis))])]
    dot_general x2 -> x3, matrix products: 29.8 us -> 2.74 us  [the longest x2 2.29 us: pick_rows(): return jnp.dot(pick, block, preferred_element_type=F32).astype(BF16)]
  transfers between devices with their start and end apart: 18 -> 32, of which waited for: 2 -> 21; matrix products, arithmetic and copies ran while one was open for 0% -> 5% of each run, Pallas kernels for 0% -> 12%
where the time goes in v2:
time: 262 us; the launch traced here: 260 us
  waiting for transfers between devices  118 us (45%)
  Pallas kernels  53 us (20%)
  starting transfers between devices  46.7 us (18%)
  local copies, waits for them, and re-layouts  17.6 us (7%)
  between operations  14.4 us (5%)
  other arithmetic  7.57 us (3%)
  matrix products  2.74 us (1%)
    ppermute x12, waiting for transfers between devices, line_xor(): return lax.ppermute(block, LINE, [(x, x ^ k) for x in range(N_X)])  51 us
    ppermute x19, waiting for transfers between devices, axis_xor(): lax.ppermute(block, axis, [(i, i ^ k) for i in range(lax.axis_size(axis))])  33.5 us
    all_gather x1, waiting for transfers between devices, shards(): lax.all_gather(piece, ('y', 'z'), axis=0, tiled=True).reshape(4, 8, 48, 896)  33.2 us
    pallas_call x4, Pallas kernels, terms_call(): pl.pallas_call(functools.partial(terms_kernel, order=order), grid_spec=pl...  28.4 us
    ppermute x19, starting transfers between devices, axis_xor(): lax.ppermute(block, axis, [(i, i ^ k) for i in range(lax.axis_size(axis))])  24.4 us
    ppermute x12, starting transfers between devices, line_xor(): return lax.ppermute(block, LINE, [(x, x ^ k) for x in range(N_X)])  22.2 us
    pallas_call x2, Pallas kernels, logits_call(): pl.pallas_call(logits_kernel, grid_spec=pltpu.PrefetchScalarGridSpec(num_...  18.8 us
    unnamed x24, local copies, waits for them, and re-layouts  8.79 us
  transfers between devices with their start and end apart: 32, of which 21 were waited for; matrix products, arithmetic and copies ran while one was open for 5% of the time, Pallas kernels for 12%

profile of v2, /device:TPU:2, one launch (start us, length us, event | category | flops | bytes accessed | tf_op | source)
XLA Modules:
  0.0 259.6 jit_solution(8696640082989844838)
XLA Ops:
  7.4 1.6 copy-done
  9.2 2.2 collective-permute-start.1
  11.4 1.6 collective-permute-start.2
  13.0 1.8 collective-permute-done.1
  16.1 1.6 constant_dynamic-slice_fusion
  17.7 1.7 collective-permute-start.7
  19.8 2.1 convolution_convert_fusion.own
  21.9 3.9 %collective-permute-start = (bf16[192,3584]{1,0:T(8,128)(2,1)}, bf16[192,3584]{1,0:T(8,128)(2,1)}, u32[]{:S(2)}, u32[]{:S(2)}) collective-permute-start(bf16[192,3584]{1,0:T(8,128)(2,1)} %convolution_convert_fusion.own), channel_id=1, source_target_pairs={{0,128},{64,192},{128,0},{192,64},{1,129},{65,193},{129,1},{193,65... | collective-permute-start | bytes 4128776 | tf_op jit(solution)/shard_map/ppermute | solution.py:26
  25.8 15.4 %collective-permute-done.7.got_a = bf16[1792,256]{1,0:T(8,128)(2,1)} collective-permute-done((bf16[1792,256]{1,0:T(8,128)(2,1)S(1)}, bf16[1792,256]{1,0:T(8,128)(2,1)}, u32[]{:S(2)}, u32[]{:S(2)}) %collective-permute-start.7) | collective-permute-done | bytes 917536 | tf_op jit(solution)/shard_map/ppermute | solution.py:26
  41.2 17.2 %collective-permute-done.4.got_a = bf16[1792,256]{1,0:T(8,128)(2,1)} collective-permute-done((bf16[1792,256]{1,0:T(8,128)(2,1)S(1)}, bf16[1792,256]{1,0:T(8,128)(2,1)}, u32[]{:S(2)}, u32[]{:S(2)}) %collective-permute-start.4) | collective-permute-done | bytes 917536 | tf_op jit(solution)/shard_map/ppermute | solution.py:26
  59.1 4.6 %collective-permute-start.6 = (s32[2,192]{1,0:T(2,128)S(1)}, s32[2,192]{1,0:T(2,128)S(1)}, u32[]{:S(2)}, u32[]{:S(2)}) collective-permute-start(s32[2,192]{1,0:T(2,128)S(1)} %reshape.201), channel_id=1, source_target_pairs={{0,64},{64,0},{128,192},{192,128},{1,65},{65,1},{129,193},{193,129... | collective-permute-start | bytes 4616 | tf_op jit(solution)/shard_map/ppermute | solution.py:26
  65.4 33.2 %all-gather.3.cloned.1.call-done = bf16[1536,896]{1,0:T(8,128)(2,1)} async-done(((bf16[48,896]{1,0:T(8,128)(2,1)}), bf16[1536,896]{1,0:T(8,128)(2,1)}) %all-gather.3.cloned.1.call-update) | async-done | bytes 2752528 | tf_op jit(solution)/shard_map/all_gather | solution.py:263
  98.6 9.4 %logits.3 = (f32[4,192,512]{2,1,0:T(8,128)}, f32[4,8,256]{2,1,0:T(8,128)S(1)}) custom-call(s32[4]{0:T(128)S(1)} %pad_add_fusion.3.at, bf16[192,3584]{1,0:T(8,128)(2,1)} %convolution_convert_fusion.own, bf16[192,3584]{1,0:T(8,128)(2,1)} %collective-permute-done.nbr, bf16[4,8,48,896]{3,2,1,0:T(8,128)(2,1)} %bitcast.67, bf16[1792,2048]{1,0:T(8,128)(2,1)} %head.7, ...), custom_call_target="tpu_custom_call" | custom-call | flops 2818572288 | bytes 16777216 | tf_op jit(solution)/shard_map/logits/pallas_call | solution.py:98
  108.0 9.3 %logits.2 = (f32[4,192,512]{2,1,0:T(8,128)}, f32[4,8,256]{2,1,0:T(8,128)S(1)}) custom-call(s32[4]{0:T(128)S(1)} %pad_add_fusion.1.at, bf16[192,3584]{1,0:T(8,128)(2,1)} %convolution_convert_fusion.own, bf16[192,3584]{1,0:T(8,128)(2,1)} %collective-permute-done.nbr, bf16[4,8,48,896]{3,2,1,0:T(8,128)(2,1)} %bitcast.68, bf16[1792,2048]{1,0:T(8,128)(2,1)} %head.7, ...), custom_call_target="tpu_custom_call" | custom-call | flops 2818572288 | bytes 16777216 | tf_op jit(solution)/shard_map/logits/pallas_call | solution.py:98
  118.0 3.5 %collective-permute-done.9 = f32[4,8,256]{2,1,0:T(8,128)S(1)} collective-permute-done((f32[4,8,256]{2,1,0:T(8,128)S(1)}, f32[4,8,256]{2,1,0:T(8,128)S(1)}, u32[]{:S(2)}, u32[]{:S(2)}) %collective-permute-start.9) | collective-permute-done | bytes 32800 | tf_op jit(solution)/shard_map/ppermute | solution.py:26
  121.5 2.1 collective-permute-start.10
  123.6 3.4 %collective-permute-done.10 = f32[4,8,256]{2,1,0:T(8,128)S(1)} collective-permute-done((f32[4,8,256]{2,1,0:T(8,128)S(1)}, f32[4,8,256]{2,1,0:T(8,128)S(1)}, u32[]{:S(2)}, u32[]{:S(2)}) %collective-permute-start.10) | collective-permute-done | bytes 32800 | tf_op jit(solution)/shard_map/ppermute | solution.py:26
  127.5 3.5 %collective-permute-done.11 = f32[4,8,256]{2,1,0:T(8,128)S(1)} collective-permute-done((f32[4,8,256]{2,1,0:T(8,128)S(1)}, f32[4,8,256]{2,1,0:T(8,128)S(1)}, u32[]{:S(2)}, u32[]{:S(2)}) %collective-permute-start.11) | collective-permute-done | bytes 32800 | tf_op jit(solution)/shard_map/ppermute | solution.py:30
  131.0 1.8 collective-permute-start.12
  132.8 3.6 %collective-permute-done.12 = f32[4,8,256]{2,1,0:T(8,128)S(1)} collective-permute-done((f32[4,8,256]{2,1,0:T(8,128)S(1)}, f32[4,8,256]{2,1,0:T(8,128)S(1)}, u32[]{:S(2)}, u32[]{:S(2)}) %collective-permute-start.12) | collective-permute-done | bytes 32800 | tf_op jit(solution)/shard_map/ppermute | solution.py:30
  136.8 3.9 %collective-permute-done.13 = f32[4,8,256]{2,1,0:T(8,128)S(1)} collective-permute-done((f32[4,8,256]{2,1,0:T(8,128)S(1)}, f32[4,8,256]{2,1,0:T(8,128)S(1)}, u32[]{:S(2)}, u32[]{:S(2)}) %collective-permute-start.13) | collective-permute-done | bytes 32800 | tf_op jit(solution)/shard_map/ppermute | solution.py:30
  141.8 3.7 %collective-permute-done.14 = f32[4,8,256]{2,1,0:T(8,128)S(1)} collective-permute-done((f32[4,8,256]{2,1,0:T(8,128)S(1)}, f32[4,8,256]{2,1,0:T(8,128)S(1)}, u32[]{:S(2)}, u32[]{:S(2)}) %collective-permute-start.14) | collective-permute-done | bytes 32800 | tf_op jit(solution)/shard_map/ppermute | solution.py:30
  145.5 2.2 collective-permute-start.15
  147.9 5.4 %collective-permute-done.15 = f32[4,8,256]{2,1,0:T(8,128)S(1)} collective-permute-done((f32[4,8,256]{2,1,0:T(8,128)S(1)}, f32[4,8,256]{2,1,0:T(8,128)S(1)}, u32[]{:S(2)}, u32[]{:S(2)}) %collective-permute-start.15) | collective-permute-done | bytes 32800 | tf_op jit(solution)/shard_map/ppermute | solution.py:30
  154.8 5.8 %logit_grad.1 = (bf16[2,192,1024]{2,1,0:T(8,128)(2,1)}, bf16[2,192,1024]{2,1,0:T(8,128)(2,1)}) custom-call(s32[4]{0:T(128)S(1)} %pad_add_fusion.1.at, f32[4,192,512]{2,1,0:T(8,128)S(1)} %copy-done.5, f32[4,192,512]{2,1,0:T(8,128)} %get-tuple-element.9.second, f32[4,8,256]{2,1,0:T(8,128)S(1)} %add.256.stats, s32[2,192,1]{2,1,0:T(8,128)S(1)} %copy.24.tgt, ...), custom_call_target="tpu_custom_call" | custom-call | tf_op jit(solution)/shard_map/logit_grad/pallas_call | solution.py:177
  161.2 2.1 collective-permute-start.17
  164.1 6.7 %gradient_terms.4.rest_0_ = f32[384,1792]{1,0:T(8,128)S(1)} custom-call(s32[4]{0:T(128)S(1)} %pad_add_fusion.1.at, bf16[2,192,1024]{2,1,0:T(8,128)(2,1)} %get-tuple-element.13.grad, bf16[1792,2048]{1,0:T(8,128)(2,1)} %head.7, bf16[1792,2048]{1,0:T(8,128)(2,1)} %collective-permute-done.3.head_b.mate), custom_call_target="tpu_custom_call" | custom-call | flops 1409286144 | bytes 8388608 | tf_op jit(solution)/shard_map/gradient_terms/pallas_call | solution.py:217
  170.9 1.6 copy-done.4
  172.5 5.5 %collective-permute-done.18.grad = bf16[2,192,1024]{2,1,0:T(8,128)(2,1)} collective-permute-done((bf16[2,192,1024]{2,1,0:T(8,128)(2,1)}, bf16[2,192,1024]{2,1,0:T(8,128)(2,1)}, u32[]{:S(2)}, u32[]{:S(2)}) %collective-permute-start.18) | collective-permute-done | bytes 786464 | tf_op jit(solution)/shard_map/ppermute | solution.py:26
  178.0 7.3 %gradient_terms.5.rest_0_ = f32[384,1792]{1,0:T(8,128)S(1)} custom-call(s32[4]{0:T(128)S(1)} %pad_add_fusion.1.at, bf16[2,192,1024]{2,1,0:T(8,128)(2,1)} %collective-permute-done.18.grad, bf16[1792,2048]{1,0:T(8,128)(2,1)} %head.7, bf16[1792,2048]{1,0:T(8,128)(2,1)} %collective-permute-done.3.head_b.mate, f32[384,1792]{1,0:T(8,128)} %copy-done.4), custom_call_target="tpu_custom_call" | custom-call | flops 1409286144 | bytes 8388608 | tf_op jit(solution)/shard_map/gradient_terms/pallas_call | solution.py:217
  185.4 1.6 copy-done.3
  187.0 7.3 %gradient_terms.6.rest_0_ = f32[384,1792]{1,0:T(8,128)S(1)} custom-call(s32[4]{0:T(128)S(1)} %pad_add_fusion.1.at, bf16[2,192,1024]{2,1,0:T(8,128)(2,1)} %collective-permute-done.17.grad, bf16[1792,2048]{1,0:T(8,128)(2,1)} %head.7, bf16[1792,2048]{1,0:T(8,128)(2,1)} %collective-permute-done.3.head_b.mate, f32[384,1792]{1,0:T(8,128)} %copy-done.3), custom_call_target="tpu_custom_call" | custom-call | flops 1409286144 | bytes 8388608 | tf_op jit(solution)/shard_map/gradient_terms/pallas_call | solution.py:217
  194.3 1.5 copy-done.2
  195.9 7.0 %gradient_terms.7 = f32[384,1792]{1,0:T(8,128)S(1)} custom-call(s32[4]{0:T(128)S(1)} %pad_add_fusion.1.at, bf16[2,192,1024]{2,1,0:T(8,128)(2,1)S(1)} %collective-permute-done.16.grad, bf16[1792,2048]{1,0:T(8,128)(2,1)} %head.7, bf16[1792,2048]{1,0:T(8,128)(2,1)} %collective-permute-done.3.head_b.mate, f32[384,1792]{1,0:T(8,128)} %copy-done.2), custom_call_target="tpu_custom_call" | custom-call | flops 1409286144 | bytes 8388608 | tf_op jit(solution)/shard_map/gradient_terms/pallas_call | solution.py:217
  205.1 1.9 collective-permute-start.20
  207.0 2.4 collective-permute-start.21
  209.4 2.7 %collective-permute-done.19 = bf16[2,48,1792]{2,1,0:T(8,128)(2,1)S(1)} collective-permute-done((bf16[2,48,1792]{2,1,0:T(8,128)(2,1)}, bf16[2,48,1792]{2,1,0:T(8,128)(2,1)S(1)}, u32[]{:S(2)}, u32[]{:S(2)}) %collective-permute-start.19) | collective-permute-done | bytes 344096 | tf_op jit(solution)/shard_map/ppermute | solution.py:30
  212.1 4.2 %collective-permute-done.20 = bf16[2,48,1792]{2,1,0:T(8,128)(2,1)} collective-permute-done((bf16[2,48,1792]{2,1,0:T(8,128)(2,1)}, bf16[2,48,1792]{2,1,0:T(8,128)(2,1)}, u32[]{:S(2)}, u32[]{:S(2)}) %collective-permute-start.20) | collective-permute-done | bytes 344096 | tf_op jit(solution)/shard_map/ppermute | solution.py:30
  216.3 2.9 %collective-permute-done.21 = bf16[2,48,1792]{2,1,0:T(8,128)(2,1)} collective-permute-done((bf16[2,48,1792]{2,1,0:T(8,128)(2,1)S(1)}, bf16[2,48,1792]{2,1,0:T(8,128)(2,1)}, u32[]{:S(2)}, u32[]{:S(2)}) %collective-permute-start.21) | collective-permute-done | bytes 344096 | tf_op jit(solution)/shard_map/ppermute | solution.py:30
  219.2 1.5 fusion.3
  222.1 1.8 collective-permute-start.23
  224.5 1.5 fusion.69
  228.0 2.3 collective-permute-start.24
  230.3 2.7 %collective-permute-start.25 = (bf16[16,1792]{1,0:T(8,128)(2,1)}, bf16[16,1792]{1,0:T(8,128)(2,1)S(1)}, u32[]{:S(2)}, u32[]{:S(2)}) collective-permute-start(bf16[16,1792]{1,0:T(8,128)(2,1)} %get-tuple-element.25), channel_id=1, source_target_pairs={{0,8},{2,10},{4,12},{6,14},{8,0},{10,2},{12,4},{14,6},{1,9},{3,11}... | collective-permute-start | bytes 172040 | tf_op jit(solution)/shard_map/ppermute | solution.py:30
  234.1 4.6 %collective-permute-start.27 = (bf16[16,1792]{1,0:T(8,128)(2,1)}, bf16[16,1792]{1,0:T(8,128)(2,1)S(1)}, u32[]{:S(2)}, u32[]{:S(2)}) collective-permute-start(bf16[16,1792]{1,0:T(8,128)(2,1)} %get-tuple-element.23), channel_id=1, source_target_pairs={{0,12},{2,14},{4,8},{6,10},{8,4},{10,6},{12,0},{14,2},{1,13},{3,15... | collective-permute-start | bytes 172040 | tf_op jit(solution)/shard_map/ppermute | solution.py:30
  243.1 2.6 %collective-permute-done.28 = bf16[16,1792]{1,0:T(8,128)(2,1)} collective-permute-done((bf16[16,1792]{1,0:T(8,128)(2,1)}, bf16[16,1792]{1,0:T(8,128)(2,1)}, u32[]{:S(2)}, u32[]{:S(2)}) %collective-permute-start.28) | collective-permute-done | bytes 57376 | tf_op jit(solution)/shard_map/ppermute | solution.py:30
  246.7 1.7 collective-permute-start.29
  249.9 2.3 collective-permute-done.29
  (108 shorter events, 24.9 us)
Async XLA Ops:
  7.2 1.8 copy-start
  7.2 91.4 %all-gather.3.cloned.1.call-start = ((), (), s32[]{:S(2)}) async-start(), calls=%async_computation | async-start | bytes 2838528 | tf_op jit(solution)/shard_map/all_gather | solution.py:263
  7.2 91.3 %collective-permute-start.3 = (bf16[1792,2048]{1,0:T(8,128)(2,1)}, bf16[1792,2048]{1,0:T(8,128)(2,1)}, u32[]{:S(2)}, u32[]{:S(2)}) collective-permute-start(bf16[1792,2048]{1,0:T(8,128)(2,1)} %head.7), channel_id=1, source_target_pairs={{0,1},{1,0},{2,3},{3,2},{4,5},{5,4},{6,7},{7,6},{8,9},{9,8},{10,11... | collective-permute-start | bytes 22020104 | tf_op jit(solution)/shard_map/ppermute | solution.py:30
  9.2 5.6 %collective-permute-start.1 = (bf16[24,896]{1,0:T(8,128)(2,1)S(1)}, bf16[24,896]{1,0:T(8,128)(2,1)S(1)}, u32[]{:S(2)}, u32[]{:S(2)}) collective-permute-start(bf16[24,896]{1,0:T(8,128)(2,1)S(1)} %convolution_convert_fusion.2), channel_id=1, source_target_pairs={{0,64},{64,0},{128,192},{192,128},{1,65},{65,1},{129,193},{193,129... | collective-permute-start | bytes 129032 | tf_op jit(solution)/shard_map/ppermute | solution.py:26
  11.4 4.0 %collective-permute-start.2 = (bf16[24,896]{1,0:T(8,128)(2,1)S(1)}, bf16[24,896]{1,0:T(8,128)(2,1)S(1)}, u32[]{:S(2)}, u32[]{:S(2)}) collective-permute-start(bf16[24,896]{1,0:T(8,128)(2,1)S(1)} %convolution_convert_fusion.2), channel_id=1, source_target_pairs={{0,192},{64,128},{128,64},{192,0},{1,193},{65,129},{129,65},{193,1... | collective-permute-start | bytes 129032 | tf_op jit(solution)/shard_map/ppermute | solution.py:26
  17.7 40.7 %copy-start.10 = (s32[384]{0:T(512)S(1)}, s32[384]{0:T(512)}, u32[]{:S(2)}) copy-start(s32[384]{0:T(512)} %param.6) | copy-start | bytes 4612
  17.7 40.9 %copy-start.11 = (s32[384]{0:T(512)S(1)}, s32[384]{0:T(512)}, u32[]{:S(2)}) copy-start(s32[384]{0:T(512)} %param.7) | copy-start | bytes 4612
  17.7 23.5 %collective-permute-start.7 = (bf16[1792,256]{1,0:T(8,128)(2,1)S(1)}, bf16[1792,256]{1,0:T(8,128)(2,1)}, u32[]{:S(2)}, u32[]{:S(2)}) collective-permute-start(bf16[1792,256]{1,0:T(8,128)(2,1)S(1)} %get-tuple-element.16), channel_id=1, source_target_pairs={{0,192},{64,128},{128,64},{192,0},{1,193},{65,129},{129,65},{193,1... | collective-permute-start | bytes 2752520 | tf_op jit(solution)/shard_map/ppermute | solution.py:26
  19.4 38.9 %collective-permute-start.4 = (bf16[1792,256]{1,0:T(8,128)(2,1)S(1)}, bf16[1792,256]{1,0:T(8,128)(2,1)}, u32[]{:S(2)}, u32[]{:S(2)}) collective-permute-start(bf16[1792,256]{1,0:T(8,128)(2,1)S(1)} %get-tuple-element.17), channel_id=1, source_target_pairs={{0,192},{64,128},{128,64},{192,0},{1,193},{65,129},{129,65},{193,1... | collective-permute-start | bytes 2752520 | tf_op jit(solution)/shard_map/ppermute | solution.py:26
  21.9 43.5 %collective-permute-start = (bf16[192,3584]{1,0:T(8,128)(2,1)}, bf16[192,3584]{1,0:T(8,128)(2,1)}, u32[]{:S(2)}, u32[]{:S(2)}) collective-permute-start(bf16[192,3584]{1,0:T(8,128)(2,1)} %convolution_convert_fusion.own), channel_id=1, source_target_pairs={{0,128},{64,192},{128,0},{192,64},{1,129},{65,193},{129,1},{193,65... | collective-permute-start | bytes 4128776 | tf_op jit(solution)/shard_map/ppermute | solution.py:26
  41.2 24.2 %collective-permute-start.8 = (bf16[1792,256]{1,0:T(8,128)(2,1)}, bf16[1792,256]{1,0:T(8,128)(2,1)}, u32[]{:S(2)}, u32[]{:S(2)}) collective-permute-start(bf16[1792,256]{1,0:T(8,128)(2,1)} %collective-permute-done.7.got_a), channel_id=1, source_target_pairs={{0,1},{1,0},{2,3},{3,2},{4,5},{5,4},{6,7},{7,6},{8,9},{9,8},{10,11... | collective-permute-start | bytes 2752520 | tf_op jit(solution)/shard_map/ppermute | solution.py:30
  58.3 49.7 %collective-permute-start.5 = (bf16[1792,256]{1,0:T(8,128)(2,1)}, bf16[1792,256]{1,0:T(8,128)(2,1)}, u32[]{:S(2)}, u32[]{:S(2)}) collective-permute-start(bf16[1792,256]{1,0:T(8,128)(2,1)} %collective-permute-done.4.got_a), channel_id=1, source_target_pairs={{0,1},{1,0},{2,3},{3,2},{4,5},{5,4},{6,7},{7,6},{8,9},{9,8},{10,11... | collective-permute-start | bytes 2752520 | tf_op jit(solution)/shard_map/ppermute | solution.py:30
  59.1 6.1 %collective-permute-start.6 = (s32[2,192]{1,0:T(2,128)S(1)}, s32[2,192]{1,0:T(2,128)S(1)}, u32[]{:S(2)}, u32[]{:S(2)}) collective-permute-start(s32[2,192]{1,0:T(2,128)S(1)} %reshape.201), channel_id=1, source_target_pairs={{0,64},{64,0},{128,192},{192,128},{1,65},{65,1},{129,193},{193,129... | collective-permute-start | bytes 4616 | tf_op jit(solution)/shard_map/ppermute | solution.py:26
  65.2 82.5 %copy-start.8 = (f32[1,2,192]{2,1,0:T(2,128)}, f32[1,2,192]{2,1,0:T(2,128)S(1)}, u32[]{:S(2)}) copy-start(f32[1,2,192]{2,1,0:T(2,128)S(1)} %get-tuple-element.34) | copy-start | bytes 4612
  117.4 4.1 %collective-permute-start.9 = (f32[4,8,256]{2,1,0:T(8,128)S(1)}, f32[4,8,256]{2,1,0:T(8,128)S(1)}, u32[]{:S(2)}, u32[]{:S(2)}) collective-permute-start(f32[4,8,256]{2,1,0:T(8,128)S(1)} %add.249), channel_id=1, source_target_pairs={{0,128},{64,192},{128,0},{192,64},{1,129},{65,193},{129,1},{193,65... | collective-permute-start | bytes 98312 | tf_op jit(solution)/shard_map/ppermute | solution.py:26
  121.5 5.5 %collective-permute-start.10 = (f32[4,8,256]{2,1,0:T(8,128)S(1)}, f32[4,8,256]{2,1,0:T(8,128)S(1)}, u32[]{:S(2)}, u32[]{:S(2)}) collective-permute-start(f32[4,8,256]{2,1,0:T(8,128)S(1)} %maximum_add_fusion), channel_id=1, source_target_pairs={{0,64},{64,0},{128,192},{192,128},{1,65},{65,1},{129,193},{193,129... | collective-permute-start | bytes 98312 | tf_op jit(solution)/shard_map/ppermute | solution.py:26
  127.0 4.0 %collective-permute-start.11 = (f32[4,8,256]{2,1,0:T(8,128)S(1)}, f32[4,8,256]{2,1,0:T(8,128)S(1)}, u32[]{:S(2)}, u32[]{:S(2)}) collective-permute-start(f32[4,8,256]{2,1,0:T(8,128)S(1)} %maximum_add_fusion.1), channel_id=1, source_target_pairs={{0,16},{16,0},{32,48},{48,32},{1,17},{17,1},{33,49},{49,33},{2,18}... | collective-permute-start | bytes 98312 | tf_op jit(solution)/shard_map/ppermute | solution.py:30
  131.0 5.4 %collective-permute-start.12 = (f32[4,8,256]{2,1,0:T(8,128)S(1)}, f32[4,8,256]{2,1,0:T(8,128)S(1)}, u32[]{:S(2)}, u32[]{:S(2)}) collective-permute-start(f32[4,8,256]{2,1,0:T(8,128)S(1)} %add.252), channel_id=1, source_target_pairs={{0,32},{16,48},{32,0},{48,16},{1,33},{17,49},{33,1},{49,17},{2,34}... | collective-permute-start | bytes 98312 | tf_op jit(solution)/shard_map/ppermute | solution.py:30
  136.4 4.3 %collective-permute-start.13 = (f32[4,8,256]{2,1,0:T(8,128)S(1)}, f32[4,8,256]{2,1,0:T(8,128)S(1)}, u32[]{:S(2)}, u32[]{:S(2)}) collective-permute-start(f32[4,8,256]{2,1,0:T(8,128)S(1)} %add.253), channel_id=1, source_target_pairs={{0,2},{2,0},{4,6},{6,4},{8,10},{10,8},{12,14},{14,12},{1,3},{3,1},... | collective-permute-start | bytes 98312 | tf_op jit(solution)/shard_map/ppermute | solution.py:30
  140.7 4.8 %collective-permute-start.14 = (f32[4,8,256]{2,1,0:T(8,128)S(1)}, f32[4,8,256]{2,1,0:T(8,128)S(1)}, u32[]{:S(2)}, u32[]{:S(2)}) collective-permute-start(f32[4,8,256]{2,1,0:T(8,128)S(1)} %add.254), channel_id=1, source_target_pairs={{0,4},{2,6},{4,0},{6,2},{8,12},{10,14},{12,8},{14,10},{1,5},{3,7},... | collective-permute-start | bytes 98312 | tf_op jit(solution)/shard_map/ppermute | solution.py:30
  145.5 7.8 %collective-permute-start.15 = (f32[4,8,256]{2,1,0:T(8,128)S(1)}, f32[4,8,256]{2,1,0:T(8,128)S(1)}, u32[]{:S(2)}, u32[]{:S(2)}) collective-permute-start(f32[4,8,256]{2,1,0:T(8,128)S(1)} %add.255), channel_id=1, source_target_pairs={{0,8},{2,10},{4,12},{6,14},{8,0},{10,2},{12,4},{14,6},{1,9},{3,11}... | collective-permute-start | bytes 98312 | tf_op jit(solution)/shard_map/ppermute | solution.py:30
  153.4 7.8 %copy-start.6 = (f32[4,8,256]{2,1,0:T(8,128)}, f32[4,8,256]{2,1,0:T(8,128)S(1)}, u32[]{:S(2)}) copy-start(f32[4,8,256]{2,1,0:T(8,128)S(1)} %add.256.stats) | copy-start | bytes 98308
  153.4 1.4 copy-start.5
  160.6 17.4 %collective-permute-start.18 = (bf16[2,192,1024]{2,1,0:T(8,128)(2,1)}, bf16[2,192,1024]{2,1,0:T(8,128)(2,1)}, u32[]{:S(2)}, u32[]{:S(2)}) collective-permute-start(bf16[2,192,1024]{2,1,0:T(8,128)(2,1)} %get-tuple-element.12), channel_id=1, source_target_pairs={{0,128},{64,192},{128,0},{192,64},{1,129},{65,193},{129,1},{193,65... | collective-permute-start | bytes 2359304 | tf_op jit(solution)/shard_map/ppermute | solution.py:26
  161.2 25.8 %collective-permute-start.17 = (bf16[2,192,1024]{2,1,0:T(8,128)(2,1)}, bf16[2,192,1024]{2,1,0:T(8,128)(2,1)}, u32[]{:S(2)}, u32[]{:S(2)}) collective-permute-start(bf16[2,192,1024]{2,1,0:T(8,128)(2,1)} %get-tuple-element.13.grad), channel_id=1, source_target_pairs={{0,64},{64,0},{128,192},{192,128},{1,65},{65,1},{129,193},{193,129... | collective-permute-start | bytes 2359304 | tf_op jit(solution)/shard_map/ppermute | solution.py:26
  163.3 32.5 %collective-permute-start.16 = (bf16[2,192,1024]{2,1,0:T(8,128)(2,1)}, bf16[2,192,1024]{2,1,0:T(8,128)(2,1)S(1)}, u32[]{:S(2)}, u32[]{:S(2)}) collective-permute-start(bf16[2,192,1024]{2,1,0:T(8,128)(2,1)} %get-tuple-element.12), channel_id=1, source_target_pairs={{0,192},{64,128},{128,64},{192,0},{1,193},{65,129},{129,65},{193,1... | collective-permute-start | bytes 2359304 | tf_op jit(solution)/shard_map/ppermute | solution.py:26
  170.8 1.6 copy-start.4
  185.3 1.6 copy-start.3
  194.3 1.5 copy-start.2
  202.9 1.8 copy-start.1
  203.0 21.5 %copy-start.9 = (f32[1,2,192]{2,1,0:T(2,128)S(1)}, f32[1,2,192]{2,1,0:T(2,128)}, u32[]{:S(2)}) copy-start(f32[1,2,192]{2,1,0:T(2,128)} %copy-done.8) | copy-start | bytes 4612
  204.6 7.5 %collective-permute-start.19 = (bf16[2,48,1792]{2,1,0:T(8,128)(2,1)}, bf16[2,48,1792]{2,1,0:T(8,128)(2,1)S(1)}, u32[]{:S(2)}, u32[]{:S(2)}) collective-permute-start(bf16[2,48,1792]{2,1,0:T(8,128)(2,1)} %get-tuple-element.18), channel_id=1, source_target_pairs={{0,16},{16,0},{32,48},{48,32},{1,17},{17,1},{33,49},{49,33},{2,18}... | collective-permute-start | bytes 1032200 | tf_op jit(solution)/shard_map/ppermute | solution.py:30
  205.1 11.2 %collective-permute-start.20 = (bf16[2,48,1792]{2,1,0:T(8,128)(2,1)}, bf16[2,48,1792]{2,1,0:T(8,128)(2,1)}, u32[]{:S(2)}, u32[]{:S(2)}) collective-permute-start(bf16[2,48,1792]{2,1,0:T(8,128)(2,1)} %get-tuple-element.20), channel_id=1, source_target_pairs={{0,32},{16,48},{32,0},{48,16},{1,33},{17,49},{33,1},{49,17},{2,34}... | collective-permute-start | bytes 1032200 | tf_op jit(solution)/shard_map/ppermute | solution.py:30
  207.0 12.3 %collective-permute-start.21 = (bf16[2,48,1792]{2,1,0:T(8,128)(2,1)S(1)}, bf16[2,48,1792]{2,1,0:T(8,128)(2,1)}, u32[]{:S(2)}, u32[]{:S(2)}) collective-permute-start(bf16[2,48,1792]{2,1,0:T(8,128)(2,1)S(1)} %get-tuple-element.19), channel_id=1, source_target_pairs={{0,48},{16,32},{32,16},{48,0},{1,49},{17,33},{33,17},{49,1},{2,50}... | collective-permute-start | bytes 1032200 | tf_op jit(solution)/shard_map/ppermute | solution.py:30
  221.9 12.2 %collective-permute-start.22 = (bf16[16,1792]{1,0:T(8,128)(2,1)S(1)}, bf16[16,1792]{1,0:T(8,128)(2,1)S(1)}, u32[]{:S(2)}, u32[]{:S(2)}) collective-permute-start(bf16[16,1792]{1,0:T(8,128)(2,1)S(1)} %get-tuple-element.21), channel_id=1, source_target_pairs={{0,2},{2,0},{4,6},{6,4},{8,10},{10,8},{12,14},{14,12},{1,3},{3,1},... | collective-permute-start | bytes 172040 | tf_op jit(solution)/shard_map/ppermute | solution.py:30
  222.1 16.6 %collective-permute-start.23 = (bf16[16,1792]{1,0:T(8,128)(2,1)}, bf16[16,1792]{1,0:T(8,128)(2,1)S(1)}, u32[]{:S(2)}, u32[]{:S(2)}) collective-permute-start(bf16[16,1792]{1,0:T(8,128)(2,1)} %get-tuple-element.27), channel_id=1, source_target_pairs={{0,4},{2,6},{4,0},{6,2},{8,12},{10,14},{12,8},{14,10},{1,5},{3,7},... | collective-permute-start | bytes 172040 | tf_op jit(solution)/shard_map/ppermute | solution.py:30
  226.0 1.2 collective-permute-start.30
  228.0 14.1 %collective-permute-start.24 = (bf16[16,1792]{1,0:T(8,128)(2,1)}, bf16[16,1792]{1,0:T(8,128)(2,1)S(1)}, u32[]{:S(2)}, u32[]{:S(2)}) collective-permute-start(bf16[16,1792]{1,0:T(8,128)(2,1)} %get-tuple-element.26), channel_id=1, source_target_pairs={{0,6},{2,4},{4,2},{6,0},{8,14},{10,12},{12,10},{14,8},{1,7},{3,5},... | collective-permute-start | bytes 172040 | tf_op jit(solution)/shard_map/ppermute | solution.py:30
  230.3 11.8 %collective-permute-start.25 = (bf16[16,1792]{1,0:T(8,128)(2,1)}, bf16[16,1792]{1,0:T(8,128)(2,1)S(1)}, u32[]{:S(2)}, u32[]{:S(2)}) collective-permute-start(bf16[16,1792]{1,0:T(8,128)(2,1)} %get-tuple-element.25), channel_id=1, source_target_pairs={{0,8},{2,10},{4,12},{6,14},{8,0},{10,2},{12,4},{14,6},{1,9},{3,11}... | collective-permute-start | bytes 172040 | tf_op jit(solution)/shard_map/ppermute | solution.py:30
  233.0 9.1 %collective-permute-start.26 = (bf16[16,1792]{1,0:T(8,128)(2,1)}, bf16[16,1792]{1,0:T(8,128)(2,1)S(1)}, u32[]{:S(2)}, u32[]{:S(2)}) collective-permute-start(bf16[16,1792]{1,0:T(8,128)(2,1)} %get-tuple-element.24), channel_id=1, source_target_pairs={{0,10},{2,8},{4,14},{6,12},{8,2},{10,0},{12,6},{14,4},{1,11},{3,9}... | collective-permute-start | bytes 172040 | tf_op jit(solution)/shard_map/ppermute | solution.py:30
  234.1 8.4 %collective-permute-start.27 = (bf16[16,1792]{1,0:T(8,128)(2,1)}, bf16[16,1792]{1,0:T(8,128)(2,1)S(1)}, u32[]{:S(2)}, u32[]{:S(2)}) collective-permute-start(bf16[16,1792]{1,0:T(8,128)(2,1)} %get-tuple-element.23), channel_id=1, source_target_pairs={{0,12},{2,14},{4,8},{6,10},{8,4},{10,6},{12,0},{14,2},{1,13},{3,15... | collective-permute-start | bytes 172040 | tf_op jit(solution)/shard_map/ppermute | solution.py:30
  238.8 7.0 %collective-permute-start.28 = (bf16[16,1792]{1,0:T(8,128)(2,1)}, bf16[16,1792]{1,0:T(8,128)(2,1)}, u32[]{:S(2)}, u32[]{:S(2)}) collective-permute-start(bf16[16,1792]{1,0:T(8,128)(2,1)} %get-tuple-element.22), channel_id=1, source_target_pairs={{0,14},{2,12},{4,10},{6,8},{8,6},{10,4},{12,2},{14,0},{1,15},{3,13... | collective-permute-start | bytes 172040 | tf_op jit(solution)/shard_map/ppermute | solution.py:30
  242.5 0.6 copy-start.7
  246.7 5.5 %collective-permute-start.29 = (bf16[8,1792]{1,0:T(8,128)(2,1)S(1)}, bf16[8,1792]{1,0:T(8,128)(2,1)S(1)}, u32[]{:S(2)}, u32[]{:S(2)}) collective-permute-start(bf16[8,1792]{1,0:T(8,128)(2,1)S(1)} %slice.81), channel_id=1, source_target_pairs={{0,64},{64,0},{128,192},{192,128},{1,65},{65,1},{129,193},{193,129... | collective-permute-start | bytes 86024 | tf_op jit(solution)/shard_map/ppermute | solution.py:26
Sparse Core Ops, SparseCore 0:
  16.2 82.3 all-gather.2

commit v3 on v0

v3 whole, which is shorter than its diff:
```python
import functools

import jax
import jax.numpy as jnp
from jax import lax
from jax.experimental import pallas as pl
from jax.experimental.pallas import tpu as pltpu
from jax.sharding import Mesh, PartitionSpec as P

softcap_limit = 30.0
kl_weight = 0.5
loss_scale = 16.0

N_Y, N_Z, N_C, N_X = 4, 8, 2, 4
LINE = ("rep", "tok")
ROWS = 192
QUARTER = 512
HALF_D = 1792
CHUNKS = (256, 256, 640, 640)
TILE = 256
VMEM = 50 * 1024 * 1024
F32, BF16 = jnp.float32, jnp.bfloat16


def line_xor(block, k):
    k = (k % 2) * 2 + k // 2
    return lax.ppermute(block, LINE, [(x, x ^ k) for x in range(N_X)])


def axis_xor(block, axis, k):
    return lax.ppermute(block, axis, [(i, i ^ k) for i in range(lax.axis_size(axis))])


def whole(*shape):
    return pl.BlockSpec(shape, lambda s, at: (0,) * len(shape))


def logits_kernel(at, own, nbr_a, nbr_b, *refs):
    far, head, mate, got, tgt = refs[:4], refs[4], refs[5], refs[6:14], refs[14]
    logits, stats, rows, raw, sums = refs[15:]
    step = pl.program_id(0)
    tok, y, z = at[0], at[2], at[3]

    @pl.when(step == 0)
    def _():
        for side in range(2):
            half = tok if side == 0 else 1 - tok
            begin = pl.multiple_of(half * HALF_D, 128)
            to = pl.ds(side * HALF_D, HALF_D)
            rows[0:ROWS, to] = own[:, pl.ds(begin, HALF_D)]
            rows[ROWS : ROWS + 96, to] = nbr_a[:, pl.ds(begin, HALF_D)]
            rows[ROWS + 96 : 2 * ROWS, to] = nbr_b[:, pl.ds(begin, HALF_D)]
        for k in range(4):
            d = y ^ k
            column = pl.multiple_of((d // 2 ^ tok) * HALF_D + d % 2 * 896, 128)
            for s in range(8):
                row = 2 * ROWS + (z ^ s) * 48
                rows[pl.ds(pl.multiple_of(row, 16), 48), pl.ds(column, 896)] = far[k][s]
        sums[...] = jnp.zeros_like(sums)

    lane = lax.broadcasted_iota(jnp.int32, (48, TILE), 1)

    def one(head, got, part, core):
        total = jnp.dot(rows[:, :HALF_D], head[...], preferred_element_type=F32)
        begin = HALF_D
        for count, chunk in zip(CHUNKS, got):
            total = total + jnp.dot(
                rows[:, begin : begin + count], chunk[...], preferred_element_type=F32
            )
            begin += count
        raw[...] = total
        column = lane + (at[4 + core] + part * TILE)
        for chunk in range(8):
            pair, g = chunk // 4, chunk % 4
            here = slice(g * 48, g * 48 + 48)
            if pair == 0:
                both = [raw[here], raw[ROWS + g * 48 : ROWS + g * 48 + 48]]
            else:
                begin = 2 * ROWS + g * 96
                pieces = [raw[begin + 24 * i : begin + 24 * i + 24] for i in range(4)]
                both = [jnp.concatenate(pieces[i::2], axis=0) for i in range(2)]
            both = [softcap_limit * jnp.tanh(v * (1.0 / softcap_limit)) for v in both]
            target = tgt[pair, here]
            hit = column == jnp.concatenate([target, target], axis=1)
            shared = [v.astype(BF16).astype(F32) for v in both]
            partner = [jnp.exp(v) for v in shared]
            for i in range(2):
                j = pair * 2 + i
                mine = both[i]
                logits[j, here] = mine
                terms = (
                    jnp.exp(mine),
                    partner[1 - i],
                    jnp.where(hit, mine, 0.0),
                    partner[1 - i] * (shared[1 - i] - mine),
                )
                for s, term in enumerate(terms):
                    sums[s, j, here] += term[:, :128] + term[:, 128:]

    for part in range(2):
        for core in range(2):
            @pl.when(step == part * 2 + core)
            def _(part=part, core=core):
                one((head, mate)[core], got[core * 4 : core * 4 + 4], part, core)

    @pl.when(step == 3)
    def _():
        lane = lax.broadcasted_iota(jnp.int32, (ROWS, 128), 1)
        for j in range(4):
            wide = jnp.zeros((ROWS, 128), F32)
            for s in range(4):
                wide = jnp.where(lane == s, jnp.sum(sums[s, j], axis=1, keepdims=True), wide)
            wide = jnp.concatenate([wide, jnp.zeros((256 - ROWS, 128), F32)], axis=0)
            stats[at[1] ^ j] = wide.T[:8]


def logits_call(at, own, nbr, far, head, mate, got, tgt):
    weights = pl.BlockSpec((HALF_D, TILE), lambda s, at: (0, at[1] * 2 + s // 2))
    return pl.pallas_call(
        logits_kernel,
        grid_spec=pltpu.PrefetchScalarGridSpec(
            num_scalar_prefetch=1,
            grid=(4,),
            in_specs=[whole(ROWS, 2 * HALF_D)]
            + [whole(ROWS // 2, 2 * HALF_D)] * 2
            + [whole(8, 48, 896)] * 4
            + [weights, pl.BlockSpec((HALF_D, TILE), lambda s, at: (0, s // 2))]
            + [pl.BlockSpec((c, TILE), lambda s, at: (0, s // 2)) for c in CHUNKS] * 2
            + [whole(2, ROWS, 128)],
            out_specs=[
                pl.BlockSpec((4, ROWS, TILE), lambda s, at: (0, 0, s % 2 * 2 + s // 2)),
                whole(4, 8, 256),
            ],
            scratch_shapes=[
                pltpu.VMEM((4 * ROWS, 2 * HALF_D), BF16),
                pltpu.VMEM((4 * ROWS, TILE), F32),
                pltpu.VMEM((4, 4, ROWS, 128), F32),
            ],
        ),
        out_shape=[
            jax.ShapeDtypeStruct((4, ROWS, 4 * TILE), F32),
            jax.ShapeDtypeStruct((4, 8, 256), F32),
        ],
        compiler_params=pltpu.CompilerParams(vmem_limit_bytes=VMEM),
        cost_estimate=pl.CostEstimate(
            flops=4 * ROWS * 4 * TILE * 2 * HALF_D * 2, bytes_accessed=16 << 20, transcendentals=1 << 21
        ),
        name="logits",
    )(at, own, *nbr, *far, head, mate, *got, tgt)


def grad_kernel(at, logits, stats, tgt, mask, mine, theirs, scales):
    step = pl.program_id(0)

    @pl.when(step == 0)
    def _():
        for j in range(4):
            total = stats[at[1] ^ j].T
            weight = loss_scale * mask[j // 2]
            scales[0, j] = (1.0 + kl_weight) * weight / total[:ROWS, 0:1]
            scales[1, j] = kl_weight * weight / total[:ROWS, 1:2]

    core, part = step // 2, step % 2
    column = lax.broadcasted_iota(jnp.int32, (48, TILE), 1)
    column = column + (jnp.where(core == 0, at[4], at[5]) + part * TILE)

    for pair in range(2):
        for g in range(4):
            here = slice(g * 48, g * 48 + 48)
            both = [logits[pair * 2, here], logits[pair * 2 + 1, here]]
            target, weight = tgt[pair, here], loss_scale * mask[pair, here]
            target = jnp.concatenate([target, target], axis=1)
            weight = jnp.concatenate([weight, weight], axis=1)
            hit = jnp.where(column == target, weight, 0.0)
            for i in range(2):
                own = both[i]
                shared = both[1 - i].astype(BF16).astype(F32)
                own_scale, partner_scale = (
                    jnp.concatenate([scales[n, pair * 2 + i, here]] * 2, axis=1) for n in range(2)
                )
                slope = own * (1.0 / softcap_limit)
                value = jnp.exp(own) * own_scale - hit - jnp.exp(shared) * partner_scale
                (mine, theirs)[i][pair, here] = (value * (1.0 - slope * slope)).astype(BF16)


def grad_call(at, logits, stats, tgt, mask):
    out = pl.BlockSpec((2, ROWS, TILE), lambda s, at: (0, 0, s))
    return pl.pallas_call(
        grad_kernel,
        grid_spec=pltpu.PrefetchScalarGridSpec(
            num_scalar_prefetch=1,
            grid=(4,),
            in_specs=[
                pl.BlockSpec((4, ROWS, TILE), lambda s, at: (0, 0, s)),
                whole(4, 8, 256),
                whole(2, ROWS, 128),
                whole(2, ROWS, 128),
            ],
            out_specs=[out, out],
            scratch_shapes=[pltpu.VMEM((2, 4, ROWS, 128), F32)],
        ),
        out_shape=[jax.ShapeDtypeStruct((2, ROWS, 4 * TILE), BF16)] * 2,
        compiler_params=pltpu.CompilerParams(vmem_limit_bytes=VMEM),
        name="logit_grad",
    )(at, logits, stats, tgt, mask)


def terms_kernel(at, *refs, ks, last):
    refs = list(refs)
    total = None
    for k in ks:
        grad, head, mate = refs[:3]
        refs = refs[3:]
        order = (0, 1) if k < 2 else (1, 0)
        for core, weight in enumerate((head, mate)):
            begin = core * QUARTER
            left = jnp.concatenate([grad[t, :, begin : begin + QUARTER] for t in order], axis=0)
            term = jnp.dot(left, weight[...], preferred_element_type=F32)
            total = term if total is None else total + term
    if not last:
        refs[0][...] = total
        return
    total = total + refs[0][...]
    outs, scratch = refs[1:5], refs[5]
    for tok in range(2):
        for y in range(4):
            begin = tok * ROWS + y * 48
            scratch[y, tok] = total[begin : begin + 48]
    for k in range(4):
        outs[k][...] = scratch[at[2] ^ k].astype(outs[k].dtype)


def terms_call(at, grads, head, mate, ks, acc=None):
    last = acc is not None
    tile = pl.BlockSpec((2 * ROWS, TILE), lambda s, at: (0, s))
    in_specs, args = [], []
    for k, grad in zip(ks, grads):
        weights = pl.BlockSpec((QUARTER, TILE), lambda s, at, k=k: (at[1] ^ k, s))
        in_specs += [pl.BlockSpec((2, ROWS, 4 * TILE), lambda s, at: (0, 0, 0)), weights, weights]
        args += [grad, head, mate]
    out_specs, scratch = tile, []
    out_shape = jax.ShapeDtypeStruct((2 * ROWS, HALF_D), F32)
    if last:
        in_specs.append(tile)
        args.append(acc)
        out_specs = [pl.BlockSpec((2, 48, TILE), lambda s, at: (0, 0, s))] * 4
        out_shape = [jax.ShapeDtypeStruct((2, 48, HALF_D), t) for t in (F32, BF16, BF16, BF16)]
        scratch = [pltpu.VMEM((4, 2, 48, TILE), F32)]
    return pl.pallas_call(
        functools.partial(terms_kernel, ks=ks, last=last),
        grid_spec=pltpu.PrefetchScalarGridSpec(
            num_scalar_prefetch=1,
            grid=(HALF_D // TILE,),
            in_specs=in_specs,
            out_specs=out_specs,
            scratch_shapes=scratch,
        ),
        out_shape=out_shape,
        compiler_params=pltpu.CompilerParams(vmem_limit_bytes=VMEM),
        cost_estimate=pl.CostEstimate(
            flops=2 * 2 * ROWS * HALF_D * 2 * QUARTER * len(ks),
            bytes_accessed=(6 << 20) * len(ks),
            transcendentals=0,
        ),
        name="gradient_terms",
    )(at, *args)


def rows_kernel(at, *refs):
    parts, outs = refs[:4], refs[4:]
    total = parts[0][...]
    for part in parts[1:]:
        total = total + part[...].astype(F32)
    z = at[3]
    out = lax.broadcasted_iota(jnp.int32, (128, 96), 0)
    src = lax.broadcasted_iota(jnp.int32, (128, 96), 1)
    owner = ((z >> 1) ^ ((out >> 3) & 3)) * 2 + ((z ^ (out >> 6)) & 1)
    i = out & 7
    wanted = ((out >> 5) & 1) * 48 + owner * 6 + i
    pick = jnp.where((src == wanted) & (i < 6), 1.0, 0.0).astype(BF16)
    low = jnp.dot(pick, total.reshape(96, 896).astype(BF16), preferred_element_type=F32)
    for n in range(4):
        outs[n][...] = low[n * 32 : n * 32 + 32].astype(BF16)


def rows_call(at, parts):
    return pl.pallas_call(
        rows_kernel,
        grid_spec=pltpu.PrefetchScalarGridSpec(
            num_scalar_prefetch=1,
            grid=(2,),
            in_specs=[pl.BlockSpec((2, 48, 896), lambda s, at: (0, 0, s))] * 4,
            out_specs=[pl.BlockSpec((32, 896), lambda s, at: (0, s))] * 4,
        ),
        out_shape=[jax.ShapeDtypeStruct((32, HALF_D), BF16)] * 4,
        compiler_params=pltpu.CompilerParams(vmem_limit_bytes=VMEM),
        name="rows",
    )(at, *parts)


def half_kernel(at, *refs):
    parts, first, others, scratch = refs[:4], refs[4], refs[5:8], refs[8]
    for side in range(2):
        half = parts[2 * side][...].astype(F32) + parts[2 * side + 1][...].astype(F32)
        begin = (at[0] ^ side) * HALF_D
        scratch[:, pl.ds(pl.multiple_of(begin, 128), HALF_D)] = half
    first[...] = scratch[0:8]
    for m in range(1, 4):
        others[m - 1][...] = scratch[m * 8 : m * 8 + 8].astype(BF16)


def half_call(at, parts):
    return pl.pallas_call(
        half_kernel,
        grid_spec=pltpu.PrefetchScalarGridSpec(
            num_scalar_prefetch=1,
            grid=(1,),
            in_specs=[whole(32, HALF_D)] * 4,
            out_specs=[whole(8, 2 * HALF_D)] * 4,
            scratch_shapes=[pltpu.VMEM((32, 2 * HALF_D), F32)],
        ),
        out_shape=[jax.ShapeDtypeStruct((8, 2 * HALF_D), t) for t in (F32, BF16, BF16, BF16)],
        name="half",
    )(at, *parts)


def tree_sum(values):
    values = list(values)
    while len(values) > 1:
        values = [a + b for a, b in zip(values[::2], values[1::2])]
    return values[0]


def add_over_slice(stats):
    stats = tree_sum([stats] + [line_xor(stats, k) for k in (1, 2, 3)])
    stats = tree_sum([stats] + [axis_xor(stats, "y", k) for k in (1, 2, 3)])
    return tree_sum([stats] + [axis_xor(stats, "z", k) for k in range(1, 8)])


def pick_rows(block, count, core):
    out = lax.broadcasted_iota(jnp.int32, (count, 2 * count), 0)
    src = lax.broadcasted_iota(jnp.int32, (count, 2 * count), 1)
    pick = (src == out // 6 * 12 + core * 6 + out % 6).astype(BF16)
    return jnp.dot(pick, block, preferred_element_type=F32).astype(BF16)


def shards(hidden, head, targets, loss_mask):
    rep, tok, y, z, core = (lax.axis_index(a) for a in ("rep", "tok", "y", "z", "core"))
    x = tok * 2 + rep
    states = hidden[0]

    sync = lax.optimization_barrier

    def chunk(n):
        return lax.dynamic_slice(head, (sum(CHUNKS[:n]), (3 - x) * QUARTER), (CHUNKS[n], QUARTER))

    got = []
    slab = pick_rows(lax.dynamic_slice(states, (z * 48, y * 896), (48, 896)), 24, core)
    got.append(line_xor(chunk(0), 3))
    slabs = [line_xor(slab, 2), line_xor(slab, 3)]
    piece = jnp.concatenate(slabs, axis=0)
    piece, got[0], head, states = sync((piece, got[0], head, states))

    got.append(line_xor(chunk(1), 3))
    far = jnp.concatenate([piece[None], axis_xor(piece[None], "z", 1)])
    own = pick_rows(states, ROWS, core)
    far, got[1], head, own = sync((far, got[1], head, own))

    voc = (y * 8 + z) * 2
    begin = [(voc + c) * 2048 + x * QUARTER for c in (core, 1 - core)]
    at = jnp.stack([tok, x, y, z, begin[0], begin[1]]).astype(jnp.int32)
    scal = jnp.stack([targets, loss_mask]).reshape(2, 32, 2, 6)
    scal = lax.dynamic_index_in_dim(scal, core, 2, keepdims=False).reshape(2, ROWS)

    got.append(line_xor(chunk(2), 3))
    nbr = [line_xor(own[:96], 1)]
    far = jnp.concatenate([far] + [axis_xor(far, "z", k) for k in (2, 4, 6)])
    mate = axis_xor(lax.dynamic_slice(head, (0, x * QUARTER), (HALF_D, QUARTER)), "core", 1)
    got_mate = [axis_xor(got[0], "core", 1)]
    scal = jnp.stack([scal, line_xor(scal, 2)], axis=1)
    mask = scal[1].astype(F32)
    tgt_wide = jnp.broadcast_to(scal[0][..., None], (2, ROWS, 128))
    mask_wide = jnp.broadcast_to(mask[..., None], (2, ROWS, 128))
    far, got[2], nbr[0], head, own, mate, got_mate[0], tgt_wide, mask_wide = sync(
        (far, got[2], nbr[0], head, own, mate, got_mate[0], tgt_wide, mask_wide)
    )

    got.append(line_xor(chunk(3), 3))
    nbr.append(line_xor(own[96:], 1))
    far = [far] + [axis_xor(far, "y", k) for k in (1, 2, 3)]
    got_mate += [axis_xor(got[n], "core", 1) for n in (1, 2)]
    head_t = head.T
    head_t, got[3], nbr[1], *far = sync((head_t, got[3], nbr[1], *far))
    got_mate.append(axis_xor(got[3], "core", 1))
    got = got + got_mate

    logits, stats = logits_call(at, own, nbr, far, head, mate, got, tgt_wide)
    head_t, stats = sync((head_t, stats))
    mate_t = axis_xor(head_t, "core", 1)
    stats = add_over_slice(stats)

    mine, theirs = grad_call(at, logits, stats, tgt_wide, mask_wide)
    grads = [mine, line_xor(theirs, 1), line_xor(mine, 2), line_xor(theirs, 3)]
    terms = terms_call(at, grads[:1], head_t, mate_t, (0,))
    parts = list(terms_call(at, grads[1:], head_t, mate_t, (1, 2, 3), terms))

    stats, parts[0] = sync((stats, parts[0]))
    stats = lax.dynamic_index_in_dim(stats, x, 0, keepdims=False)
    own_total, partner_total, picked, cross = (stats[s, :ROWS] for s in range(4))
    own_lse, partner_lse = jnp.log(own_total), jnp.log(partner_total)
    loss = mask[0] * (
        own_lse - picked + kl_weight * (cross / partner_total - partner_lse + own_lse)
    )
    pair = jnp.stack([loss, axis_xor(loss, "core", 1)]).reshape(2, 32, 6)
    pair = jnp.where(core == 0, pair, pair[::-1])
    token_loss = pair.transpose(1, 0, 2).reshape(1, 384)

    parts = [parts[0]] + [axis_xor(parts[k], "y", k) for k in (1, 2, 3)]
    token_loss, parts[0] = sync((token_loss, parts[0]))
    parts = rows_call(at, parts)
    parts = [
        parts[0],
        axis_xor(parts[2], "z", 1),
        line_xor(parts[1], 2),
        lax.ppermute(parts[3], ("tok", "z"), [(i, i ^ 9) for i in range(16)]),
    ]
    parts = half_call(at, parts)
    total = parts[0]
    for m in (1, 2, 3):
        total = total + axis_xor(parts[m], "z", 2 * m).astype(F32)
    return total[:6].astype(BF16)[None], token_loss


def solution(mesh):
    fine = Mesh(
        mesh.devices.reshape(2, 2, N_Y, N_Z, N_C), ("rep", "tok", "y", "z", "core")
    )
    voc = ("y", "z", "core")
    placed = (P("rep", "tok", None), P("tok", voc), P("tok"), P("tok"))
    return jax.shard_map(
        shards,
        mesh=fine,
        in_specs=placed,
        out_specs=(P("rep", ("tok", *voc), None), P("rep", "tok")),
        check_vma=False,
    )
```

time: 632 us -> 279 us (0.44)
  blocking collectives: 277 us -> 0 us
  waiting for transfers between devices: 222 us -> 107 us
  Pallas kernels: 0 us -> 42.7 us
  starting transfers between devices: 50.3 us -> 84.2 us
  matrix products: 29.8 us -> 1.2 us
  between operations: 14.9 us -> 1.17 us
    all_gather x1 -> x0, waiting for transfers between devices: 186 us -> none  [shards(): full_head = lax.all_gather(head, 'tok', axis=0, tiled=True)]
    unnamed x1 -> x0, blocking collectives: 147 us -> none
    psum x1 -> x0, blocking collectives: 130 us -> none  [shards(): partner_total, cross = lax.psum((partner_part, cross_part), 'voc')]
    ppermute x1 -> x48, starting transfers between devices: 1.46 us -> 84.2 us  [the longest x31 59.5 us: axis_xor(): lax.ppermute(block, axis, [(i, i ^ k) for i in range(lax.axis_size(axis))])]
    ppermute x1 -> x48, waiting for transfers between devices: 35 us -> 107 us  [the longest x16 54 us: line_xor(): return lax.ppermute(block, LINE, [(x, x ^ k) for x in range(N_X)])]
    unnamed x16 -> x0, starting transfers between devices: 48.8 us -> none
    pallas_call x0 -> x6, Pallas kernels: none -> 42.7 us  [the longest x2 18.1 us: terms_call(): pl.pallas_call(functools.partial(terms_kernel, ks=ks, last=last), grid_sp...]
    dot_general x2, matrix products: 29.8 us -> 1.2 us  [pick_rows(): return jnp.dot(pick, block, preferred_element_type=F32).astype(BF16)]
  transfers between devices with their start and end apart: 18 -> 48, of which waited for: 2 -> 27; matrix products, arithmetic and copies ran while one was open for 0% -> 9% of each run, Pallas kernels for 0% -> 4%
where the time goes in v3:
time: 279 us; the launch traced here: 274 us
  waiting for transfers between devices  107 us (38%)
  starting transfers between devices  84.2 us (30%)
  Pallas kernels  42.7 us (15%)
  local copies, waits for them, and re-layouts  33.1 us (12%)
  other arithmetic  4.66 us (2%)
    ppermute x31, starting transfers between devices, axis_xor(): lax.ppermute(block, axis, [(i, i ^ k) for i in range(lax.axis_size(axis))])  59.5 us
    ppermute x16, waiting for transfers between devices, line_xor(): return lax.ppermute(block, LINE, [(x, x ^ k) for x in range(N_X)])  54 us
    ppermute x31, waiting for transfers between devices, axis_xor(): lax.ppermute(block, axis, [(i, i ^ k) for i in range(lax.axis_size(axis))])  47.8 us
    ppermute x16, starting transfers between devices, line_xor(): return lax.ppermute(block, LINE, [(x, x ^ k) for x in range(N_X)])  24.7 us
    pallas_call x2, Pallas kernels, terms_call(): pl.pallas_call(functools.partial(terms_kernel, ks=ks, last=last), grid_sp...  18.1 us
    pallas_call x1, Pallas kernels, logits_call(): pl.pallas_call(logits_kernel, grid_spec=pltpu.PrefetchScalarGridSpec(num_...  14.3 us
    optimization_barrier x1, local copies, waits for them, and re-layouts, shards(): sync((far, got[2], nbr[0], head, own, mate, got_mate[0], tgt_wide, mask_w...  10 us
    unnamed x36, local copies, waits for them, and re-layouts  8.44 us
  transfers between devices with their start and end apart: 48, of which 27 were waited for; matrix products, arithmetic and copies ran while one was open for 9% of the time, Pallas kernels for 4%

profile of v3, /device:TPU:2, one launch (start us, length us, event | category | flops | bytes accessed | tf_op | source)
XLA Modules:
  0.0 273.7 jit_solution(15666656519169375788)
XLA Ops:
  2.6 2.2 collective-permute-start.1
  9.3 5.0 %collective-permute-done.3.refs_6_ = bf16[256,512]{1,0:T(8,128)(2,1)S(1)} collective-permute-done((bf16[256,512]{1,0:T(8,128)(2,1)S(1)}, bf16[256,512]{1,0:T(8,128)(2,1)S(1)}, u32[]{:S(2)}, u32[]{:S(2)}) %collective-permute-start.3) | collective-permute-done | bytes 262176 | tf_op jit(solution)/shard_map/ppermute | solution.py:27
  20.2 4.4 %collective-permute-done.5.refs_7_ = bf16[256,512]{1,0:T(8,128)(2,1)} collective-permute-done((bf16[256,512]{1,0:T(8,128)(2,1)S(1)}, bf16[256,512]{1,0:T(8,128)(2,1)}, u32[]{:S(2)}, u32[]{:S(2)}) %collective-permute-start.5) | collective-permute-done | bytes 262176 | tf_op jit(solution)/shard_map/ppermute | solution.py:27
  24.6 2.9 %constant_dynamic-slice_fusion = bf16[1792,512]{1,0:T(8,128)(2,1)} fusion(bf16[1792,2048]{1,0:T(8,128)(2,1)} %refs_4_, s32[]{:T(128)S(6)} %select_n.63), kind=kLoop, calls=%fused_computation.53 | loop fusion | bytes 3670020 | tf_op jit(solution)/shard_map/dynamic_slice | solution.py:378
  28.4 3.2 %collective-permute-start.10 = (bf16[96,3584]{1,0:T(8,128)(2,1)}, bf16[96,3584]{1,0:T(8,128)(2,1)}, u32[]{:S(2)}, u32[]{:S(2)}) collective-permute-start(bf16[96,3584]{1,0:T(8,128)(2,1)} %slice.37), channel_id=1, source_target_pairs={{0,128},{64,192},{128,0},{192,64},{1,129},{65,193},{129,1},{193,65... | collective-permute-start | bytes 2064392 | tf_op jit(solution)/shard_map/ppermute | solution.py:27
  31.6 2.0 constant_dynamic-slice_fusion.4
  35.6 3.3 %collective-permute-start.6 = (bf16[2,48,896]{2,1,0:T(8,128)(2,1)}, bf16[2,48,896]{2,1,0:T(8,128)(2,1)}, u32[]{:S(2)}, u32[]{:S(2)}) collective-permute-start(bf16[2,48,896]{2,1,0:T(8,128)(2,1)} %pad_maximum_fusion.1), channel_id=1, source_target_pairs={{0,4},{2,6},{4,0},{6,2},{8,12},{10,14},{12,8},{14,10},{1,5},{3,7},... | collective-permute-start | bytes 516104 | tf_op jit(solution)/shard_map/ppermute | solution.py:31
  39.8 9.2 %collective-permute-done = s32[2,192]{1,0:T(2,128)S(1)} collective-permute-done((s32[2,192]{1,0:T(2,128)S(1)}, s32[2,192]{1,0:T(2,128)S(1)}, u32[]{:S(2)}, u32[]{:S(2)}) %collective-permute-start) | collective-permute-done | bytes 1568 | tf_op jit(solution)/shard_map/ppermute | solution.py:27
  49.0 6.3 %collective-permute-start.7 = (bf16[2,48,896]{2,1,0:T(8,128)(2,1)}, bf16[2,48,896]{2,1,0:T(8,128)(2,1)}, u32[]{:S(2)}, u32[]{:S(2)}) collective-permute-start(bf16[2,48,896]{2,1,0:T(8,128)(2,1)} %pad_maximum_fusion.1), channel_id=1, source_target_pairs={{0,8},{2,10},{4,12},{6,14},{8,0},{10,2},{12,4},{14,6},{1,9},{3,11}... | collective-permute-start | bytes 516104 | tf_op jit(solution)/shard_map/ppermute | solution.py:31
  55.8 6.9 %collective-permute-done.7 = bf16[2,48,896]{2,1,0:T(8,128)(2,1)} collective-permute-done((bf16[2,48,896]{2,1,0:T(8,128)(2,1)}, bf16[2,48,896]{2,1,0:T(8,128)(2,1)}, u32[]{:S(2)}, u32[]{:S(2)}) %collective-permute-start.7) | collective-permute-done | bytes 172064 | tf_op jit(solution)/shard_map/ppermute | solution.py:31
  62.9 7.4 %collective-permute-done.8 = bf16[2,48,896]{2,1,0:T(8,128)(2,1)} collective-permute-done((bf16[2,48,896]{2,1,0:T(8,128)(2,1)}, bf16[2,48,896]{2,1,0:T(8,128)(2,1)}, u32[]{:S(2)}, u32[]{:S(2)}) %collective-permute-start.8) | collective-permute-done | bytes 172064 | tf_op jit(solution)/shard_map/ppermute | solution.py:31
  70.3 2.1 pad_maximum_fusion.refs_0_
  75.2 2.9 %collective-permute-start.16 = (bf16[8,48,896]{2,1,0:T(8,128)(2,1)}, bf16[8,48,896]{2,1,0:T(8,128)(2,1)}, u32[]{:S(2)}, u32[]{:S(2)}) collective-permute-start(bf16[8,48,896]{2,1,0:T(8,128)(2,1)} %pad_maximum_fusion.refs_0_), channel_id=1, source_target_pairs={{0,32},{16,48},{32,0},{48,16},{1,33},{17,49},{33,1},{49,17},{2,34}... | collective-permute-start | bytes 2064392 | tf_op jit(solution)/shard_map/ppermute | solution.py:31
  78.3 2.0 slice.39
  80.3 2.1 collective-permute-start.14
  82.4 2.0 constant_dynamic-slice_fusion.2
  85.2 10.0 %copy.13 = bf16[1792,2048]{0,1:T(8,128)(2,1)} copy(bf16[1792,2048]{1,0:T(8,128)(2,1)} %refs_4_) | data formatting | bytes 14680064 | tf_op jit(solution)/shard_map/optimization_barrier | solution.py:384
  95.2 5.2 %collective-permute-done.13.refs_9_ = bf16[640,512]{1,0:T(8,128)(2,1)} collective-permute-done((bf16[640,512]{1,0:T(8,128)(2,1)}, bf16[640,512]{1,0:T(8,128)(2,1)}, u32[]{:S(2)}, u32[]{:S(2)}) %collective-permute-start.13) | collective-permute-done | bytes 655392 | tf_op jit(solution)/shard_map/ppermute | solution.py:27
  100.4 8.0 %collective-permute-done.16.refs_2_ = bf16[8,48,896]{2,1,0:T(8,128)(2,1)} collective-permute-done((bf16[8,48,896]{2,1,0:T(8,128)(2,1)}, bf16[8,48,896]{2,1,0:T(8,128)(2,1)}, u32[]{:S(2)}, u32[]{:S(2)}) %collective-permute-start.16) | collective-permute-done | bytes 688160 | tf_op jit(solution)/shard_map/ppermute | solution.py:31
  108.4 2.6 collective-permute-done.17.refs_3_
  111.6 2.2 collective-permute-done.18.refs_11_
  114.9 14.3 %logits.1 = (f32[4,192,1024]{2,1,0:T(8,128)}, f32[4,8,256]{2,1,0:T(8,128)S(1)}) custom-call(s32[6]{0:T(128)S(1)} %stack.51.at, bf16[192,3584]{1,0:T(8,128)(2,1)} %copy-done.11, bf16[96,3584]{1,0:T(8,128)(2,1)} %collective-permute-done.10.nbr_a, bf16[96,3584]{1,0:T(8,128)(2,1)} %collective-permute-done.14.nbr_b, bf16[8,48,896]{2,1,0:T(8,128)(2,1)} %pad_maximum_fusion.refs_0_, ...), custom_call_target="tpu_custom_call" | custom-call | flops 5637144576 | bytes 16777216 | tf_op jit(solution)/shard_map/logits/pallas_call | solution.py:119
  129.4 2.2 collective-permute-start.21
  133.5 3.5 %collective-permute-done.22 = f32[4,8,256]{2,1,0:T(8,128)S(1)} collective-permute-done((f32[4,8,256]{2,1,0:T(8,128)S(1)}, f32[4,8,256]{2,1,0:T(8,128)S(1)}, u32[]{:S(2)}, u32[]{:S(2)}) %collective-permute-start.22) | collective-permute-done | bytes 32800 | tf_op jit(solution)/shard_map/ppermute | solution.py:27
  138.8 12.4 %collective-permute-start.26 = (f32[4,8,256]{2,1,0:T(8,128)S(1)}, f32[4,8,256]{2,1,0:T(8,128)S(1)}, u32[]{:S(2)}, u32[]{:S(2)}) collective-permute-start(f32[4,8,256]{2,1,0:T(8,128)S(1)} %add_add_fusion.2), channel_id=1, source_target_pairs={{0,48},{16,32},{32,16},{48,0},{1,49},{17,33},{33,17},{49,1},{2,50}... | collective-permute-start | bytes 98312 | tf_op jit(solution)/shard_map/ppermute | solution.py:31
  151.2 2.2 collective-permute-done.26
  153.4 2.2 collective-permute-start.27
  155.7 2.5 collective-permute-start.29
  158.1 3.8 %collective-permute-start.30 = (f32[4,8,256]{2,1,0:T(8,128)S(1)}, f32[4,8,256]{2,1,0:T(8,128)S(1)}, u32[]{:S(2)}, u32[]{:S(2)}) collective-permute-start(f32[4,8,256]{2,1,0:T(8,128)S(1)} %add_add_fusion.1), channel_id=1, source_target_pairs={{0,8},{2,10},{4,12},{6,14},{8,0},{10,2},{12,4},{14,6},{1,9},{3,11}... | collective-permute-start | bytes 98312 | tf_op jit(solution)/shard_map/ppermute | solution.py:31
  163.6 3.5 %collective-permute-start.32 = (f32[4,8,256]{2,1,0:T(8,128)S(1)}, f32[4,8,256]{2,1,0:T(8,128)S(1)}, u32[]{:S(2)}, u32[]{:S(2)}) collective-permute-start(f32[4,8,256]{2,1,0:T(8,128)S(1)} %add_add_fusion.1), channel_id=1, source_target_pairs={{0,12},{2,14},{4,8},{6,10},{8,4},{10,6},{12,0},{14,2},{1,13},{3,15... | collective-permute-start | bytes 98312 | tf_op jit(solution)/shard_map/ppermute | solution.py:31
  169.7 2.6 collective-permute-done.33
  172.2 5.7 %logit_grad.1 = (bf16[2,192,1024]{2,1,0:T(8,128)(2,1)}, bf16[2,192,1024]{2,1,0:T(8,128)(2,1)}) custom-call(s32[6]{0:T(128)S(1)} %stack.51.at, f32[4,192,1024]{2,1,0:T(8,128)} %get-tuple-element.73.logits, f32[4,8,256]{2,1,0:T(8,128)S(1)} %add_add_fusion.stats, s32[2,192,128]{2,1,0:T(8,128)S(1)} %broadcast_in_dim.22.refs_14_.tgt, ...), custom_call_target="tpu_custom_call" | custom-call | tf_op jit(solution)/shard_map/logit_grad/pallas_call | solution.py:188
  177.9 2.3 collective-permute-start.34
  181.8 6.6 %gradient_terms.2.refs_9_ = f32[384,1792]{1,0:T(8,128)S(1)} custom-call(s32[6]{0:T(128)S(1)} %stack.51.at, bf16[2,192,1024]{2,1,0:T(8,128)(2,1)} %get-tuple-element.77.refs_0_, bf16[2048,1792]{1,0:T(8,128)(2,1)} %bitcast.11.refs_1_.refs_4_.refs_7_, bf16[2048,1792]{1,0:T(8,128)(2,1)} %collective-permute-done.35.refs_2_.refs_5_.refs_8_), custom_call_target="tpu_custom_call" | custom-call | flops 1409286144 | bytes 6291456 | tf_op jit(solution)/shard_map/gradient_terms/pallas_call | solution.py:249
  190.0 8.9 %collective-permute-done.34.refs_0_ = bf16[2,192,1024]{2,1,0:T(8,128)(2,1)S(1)} collective-permute-done((bf16[2,192,1024]{2,1,0:T(8,128)(2,1)}, bf16[2,192,1024]{2,1,0:T(8,128)(2,1)S(1)}, u32[]{:S(2)}, u32[]{:S(2)}) %collective-permute-start.34) | collective-permute-done | bytes 786464 | tf_op jit(solution)/shard_map/ppermute | solution.py:27
  198.9 11.6 %collective-permute-done.36.refs_3_ = bf16[2,192,1024]{2,1,0:T(8,128)(2,1)} collective-permute-done((bf16[2,192,1024]{2,1,0:T(8,128)(2,1)}, bf16[2,192,1024]{2,1,0:T(8,128)(2,1)}, u32[]{:S(2)}, u32[]{:S(2)}) %collective-permute-start.36) | collective-permute-done | bytes 786464 | tf_op jit(solution)/shard_map/ppermute | solution.py:27
  212.0 11.5 %gradient_terms.3 = (f32[2,48,1792]{2,1,0:T(8,128)S(1)}, bf16[2,48,1792]{2,1,0:T(8,128)(2,1)}, bf16[2,48,1792]{2,1,0:T(8,128)(2,1)}, bf16[2,48,1792]{2,1,0:T(8,128)(2,1)}) custom-call(s32[6]{0:T(128)S(1)} %stack.51.at, bf16[2,192,1024]{2,1,0:T(8,128)(2,1)S(1)} %collective-permute-done.34.refs_0_, bf16[2048,1792]{1,0:T(8,128)(2,1)} %bitcast.11.refs_1_.refs_4_.refs_7_, ...), custom_call_target="tpu_custom_call" | custom-call | flops 4227858432 | bytes 18874368 | tf_op jit(solution)/shard_map/gradient_terms/pallas_call | solution.py:249
  224.4 4.4 %collective-permute-start.40 = (bf16[2,48,1792]{2,1,0:T(8,128)(2,1)}, bf16[2,48,1792]{2,1,0:T(8,128)(2,1)S(1)}, u32[]{:S(2)}, u32[]{:S(2)}) collective-permute-start(bf16[2,48,1792]{2,1,0:T(8,128)(2,1)} %get-tuple-element.83), channel_id=1, source_target_pairs={{0,32},{16,48},{32,0},{48,16},{1,33},{17,49},{33,1},{49,17},{2,34}... | collective-permute-start | bytes 1032200 | tf_op jit(solution)/shard_map/ppermute | solution.py:31
  232.2 5.9 %collective-permute-done.40.refs_2_ = bf16[2,48,1792]{2,1,0:T(8,128)(2,1)S(1)} collective-permute-done((bf16[2,48,1792]{2,1,0:T(8,128)(2,1)}, bf16[2,48,1792]{2,1,0:T(8,128)(2,1)S(1)}, u32[]{:S(2)}, u32[]{:S(2)}) %collective-permute-start.40) | collective-permute-done | bytes 344096 | tf_op jit(solution)/shard_map/ppermute | solution.py:31
  238.0 3.2 %collective-permute-done.41.refs_3_ = bf16[2,48,1792]{2,1,0:T(8,128)(2,1)} collective-permute-done((bf16[2,48,1792]{2,1,0:T(8,128)(2,1)}, bf16[2,48,1792]{2,1,0:T(8,128)(2,1)}, u32[]{:S(2)}, u32[]{:S(2)}) %collective-permute-start.41) | collective-permute-done | bytes 344096 | tf_op jit(solution)/shard_map/ppermute | solution.py:31
  242.4 2.1 rows.1
  245.2 2.5 collective-permute-start.42
  247.7 3.4 %collective-permute-start.43 = (bf16[32,1792]{1,0:T(8,128)(2,1)S(1)}, bf16[32,1792]{1,0:T(8,128)(2,1)S(1)}, u32[]{:S(2)}, u32[]{:S(2)}) collective-permute-start(bf16[32,1792]{1,0:T(8,128)(2,1)S(1)} %get-tuple-element.87), channel_id=1, source_target_pairs={{0,64},{64,0},{128,192},{192,128},{1,65},{65,1},{129,193},{193,129... | collective-permute-start | bytes 344072 | tf_op jit(solution)/shard_map/ppermute | solution.py:27
  251.1 2.8 %collective-permute-done.43.refs_2_ = bf16[32,1792]{1,0:T(8,128)(2,1)S(1)} collective-permute-done((bf16[32,1792]{1,0:T(8,128)(2,1)S(1)}, bf16[32,1792]{1,0:T(8,128)(2,1)S(1)}, u32[]{:S(2)}, u32[]{:S(2)}) %collective-permute-start.43) | collective-permute-done | bytes 114720 | tf_op jit(solution)/shard_map/ppermute | solution.py:27
  254.0 4.8 %collective-permute-done.44.refs_3_ = bf16[32,1792]{1,0:T(8,128)(2,1)S(1)} collective-permute-done((bf16[32,1792]{1,0:T(8,128)(2,1)S(1)}, bf16[32,1792]{1,0:T(8,128)(2,1)S(1)}, u32[]{:S(2)}, u32[]{:S(2)}) %collective-permute-start.44) | collective-permute-done | bytes 114720 | tf_op jit(solution)/shard_map/ppermute | solution.py:425
  259.4 2.5 half.1
  261.9 3.4 %collective-permute-start.46 = (bf16[8,3584]{1,0:T(8,128)(2,1)}, bf16[8,3584]{1,0:T(8,128)(2,1)S(1)}, u32[]{:S(2)}, u32[]{:S(2)}) collective-permute-start(bf16[8,3584]{1,0:T(8,128)(2,1)} %get-tuple-element.91), channel_id=1, source_target_pairs={{0,8},{2,10},{4,12},{6,14},{8,0},{10,2},{12,4},{14,6},{1,9},{3,11}... | collective-permute-start | bytes 172040 | tf_op jit(solution)/shard_map/ppermute | solution.py:31
  265.4 3.0 %collective-permute-start.47 = (bf16[8,3584]{1,0:T(8,128)(2,1)}, bf16[8,3584]{1,0:T(8,128)(2,1)S(1)}, u32[]{:S(2)}, u32[]{:S(2)}) collective-permute-start(bf16[8,3584]{1,0:T(8,128)(2,1)} %get-tuple-element.92), channel_id=1, source_target_pairs={{0,12},{2,14},{4,8},{6,10},{8,4},{10,6},{12,0},{14,2},{1,13},{3,15... | collective-permute-start | bytes 172040 | tf_op jit(solution)/shard_map/ppermute | solution.py:31
  (138 shorter events, 46.6 us)
Async XLA Ops:
  2.6 5.6 %collective-permute-start.1 = (bf16[24,896]{1,0:T(8,128)(2,1)S(1)}, bf16[24,896]{1,0:T(8,128)(2,1)S(1)}, u32[]{:S(2)}, u32[]{:S(2)}) collective-permute-start(bf16[24,896]{1,0:T(8,128)(2,1)S(1)} %convolution_convert_fusion.1), channel_id=1, source_target_pairs={{0,64},{64,0},{128,192},{192,128},{1,65},{65,1},{129,193},{193,129... | collective-permute-start | bytes 129032 | tf_op jit(solution)/shard_map/ppermute | solution.py:27
  4.8 4.5 %collective-permute-start.2 = (bf16[24,896]{1,0:T(8,128)(2,1)S(1)}, bf16[24,896]{1,0:T(8,128)(2,1)S(1)}, u32[]{:S(2)}, u32[]{:S(2)}) collective-permute-start(bf16[24,896]{1,0:T(8,128)(2,1)S(1)} %convolution_convert_fusion.1), channel_id=1, source_target_pairs={{0,192},{64,128},{128,64},{192,0},{1,193},{65,129},{129,65},{193,1... | collective-permute-start | bytes 129032 | tf_op jit(solution)/shard_map/ppermute | solution.py:27
  7.4 6.9 %collective-permute-start.3 = (bf16[256,512]{1,0:T(8,128)(2,1)S(1)}, bf16[256,512]{1,0:T(8,128)(2,1)S(1)}, u32[]{:S(2)}, u32[]{:S(2)}) collective-permute-start(bf16[256,512]{1,0:T(8,128)(2,1)S(1)} %constant_dynamic-slice_fusion.1), channel_id=1, source_target_pairs={{0,192},{64,128},{128,64},{192,0},{1,193},{65,129},{129,65},{193,1... | collective-permute-start | bytes 786440 | tf_op jit(solution)/shard_map/ppermute | solution.py:27
  14.3 5.1 %collective-permute-start.4 = (bf16[1,48,896]{2,1,0:T(8,128)(2,1)S(1)}, bf16[1,48,896]{2,1,0:T(8,128)(2,1)S(1)}, u32[]{:S(2)}, u32[]{:S(2)}) collective-permute-start(bf16[1,48,896]{2,1,0:T(8,128)(2,1)S(1)} %bitcast.41), channel_id=1, source_target_pairs={{0,2},{2,0},{4,6},{6,4},{8,10},{10,8},{12,14},{14,12},{1,3},{3,1},... | collective-permute-start | bytes 258056 | tf_op jit(solution)/shard_map/ppermute | solution.py:31
  17.2 7.4 %collective-permute-start.5 = (bf16[256,512]{1,0:T(8,128)(2,1)S(1)}, bf16[256,512]{1,0:T(8,128)(2,1)}, u32[]{:S(2)}, u32[]{:S(2)}) collective-permute-start(bf16[256,512]{1,0:T(8,128)(2,1)S(1)} %constant_dynamic-slice_fusion.3), channel_id=1, source_target_pairs={{0,192},{64,128},{128,64},{192,0},{1,193},{65,129},{129,65},{193,1... | collective-permute-start | bytes 786440 | tf_op jit(solution)/shard_map/ppermute | solution.py:27
  27.5 44.9 %collective-permute-start.11 = (bf16[1792,512]{1,0:T(8,128)(2,1)}, bf16[1792,512]{1,0:T(8,128)(2,1)}, u32[]{:S(2)}, u32[]{:S(2)}) collective-permute-start(bf16[1792,512]{1,0:T(8,128)(2,1)} %constant_dynamic-slice_fusion), channel_id=1, source_target_pairs={{0,1},{1,0},{2,3},{3,2},{4,5},{5,4},{6,7},{7,6},{8,9},{9,8},{10,11... | collective-permute-start | bytes 5505032 | tf_op jit(solution)/shard_map/ppermute | solution.py:31
  28.4 44.0 %collective-permute-start.10 = (bf16[96,3584]{1,0:T(8,128)(2,1)}, bf16[96,3584]{1,0:T(8,128)(2,1)}, u32[]{:S(2)}, u32[]{:S(2)}) collective-permute-start(bf16[96,3584]{1,0:T(8,128)(2,1)} %slice.37), channel_id=1, source_target_pairs={{0,128},{64,192},{128,0},{192,64},{1,129},{65,193},{129,1},{193,65... | collective-permute-start | bytes 2064392 | tf_op jit(solution)/shard_map/ppermute | solution.py:27
  33.6 38.9 %collective-permute-start.9 = (bf16[640,512]{1,0:T(8,128)(2,1)}, bf16[640,512]{1,0:T(8,128)(2,1)S(1)}, u32[]{:S(2)}, u32[]{:S(2)}) collective-permute-start(bf16[640,512]{1,0:T(8,128)(2,1)} %constant_dynamic-slice_fusion.4), channel_id=1, source_target_pairs={{0,192},{64,128},{128,64},{192,0},{1,193},{65,129},{129,65},{193,1... | collective-permute-start | bytes 1966088 | tf_op jit(solution)/shard_map/ppermute | solution.py:27
  35.6 19.7 %collective-permute-start.6 = (bf16[2,48,896]{2,1,0:T(8,128)(2,1)}, bf16[2,48,896]{2,1,0:T(8,128)(2,1)}, u32[]{:S(2)}, u32[]{:S(2)}) collective-permute-start(bf16[2,48,896]{2,1,0:T(8,128)(2,1)} %pad_maximum_fusion.1), channel_id=1, source_target_pairs={{0,4},{2,6},{4,0},{6,2},{8,12},{10,14},{12,8},{14,10},{1,5},{3,7},... | collective-permute-start | bytes 516104 | tf_op jit(solution)/shard_map/ppermute | solution.py:31
  39.1 9.9 %collective-permute-start = (s32[2,192]{1,0:T(2,128)S(1)}, s32[2,192]{1,0:T(2,128)S(1)}, u32[]{:S(2)}, u32[]{:S(2)}) collective-permute-start(s32[2,192]{1,0:T(2,128)S(1)} %reshape.39), channel_id=1, source_target_pairs={{0,64},{64,0},{128,192},{192,128},{1,65},{65,1},{129,193},{193,129... | collective-permute-start | bytes 4616 | tf_op jit(solution)/shard_map/ppermute | solution.py:27
  49.0 13.7 %collective-permute-start.7 = (bf16[2,48,896]{2,1,0:T(8,128)(2,1)}, bf16[2,48,896]{2,1,0:T(8,128)(2,1)}, u32[]{:S(2)}, u32[]{:S(2)}) collective-permute-start(bf16[2,48,896]{2,1,0:T(8,128)(2,1)} %pad_maximum_fusion.1), channel_id=1, source_target_pairs={{0,8},{2,10},{4,12},{6,14},{8,0},{10,2},{12,4},{14,6},{1,9},{3,11}... | collective-permute-start | bytes 516104 | tf_op jit(solution)/shard_map/ppermute | solution.py:31
  55.3 15.0 %collective-permute-start.8 = (bf16[2,48,896]{2,1,0:T(8,128)(2,1)}, bf16[2,48,896]{2,1,0:T(8,128)(2,1)}, u32[]{:S(2)}, u32[]{:S(2)}) collective-permute-start(bf16[2,48,896]{2,1,0:T(8,128)(2,1)} %pad_maximum_fusion.1), channel_id=1, source_target_pairs={{0,12},{2,14},{4,8},{6,10},{8,4},{10,6},{12,0},{14,2},{1,13},{3,15... | collective-permute-start | bytes 516104 | tf_op jit(solution)/shard_map/ppermute | solution.py:31
  62.7 9.7 %collective-permute-start.12 = (bf16[256,512]{1,0:T(8,128)(2,1)}, bf16[256,512]{1,0:T(8,128)(2,1)}, u32[]{:S(2)}, u32[]{:S(2)}) collective-permute-start(bf16[256,512]{1,0:T(8,128)(2,1)} %copy-done.9), channel_id=1, source_target_pairs={{0,1},{1,0},{2,3},{3,2},{4,5},{5,4},{6,7},{7,6},{8,9},{9,8},{10,11... | collective-permute-start | bytes 786440 | tf_op jit(solution)/shard_map/ppermute | solution.py:31
  73.5 26.9 %collective-permute-start.15 = (bf16[8,48,896]{2,1,0:T(8,128)(2,1)}, bf16[8,48,896]{2,1,0:T(8,128)(2,1)}, u32[]{:S(2)}, u32[]{:S(2)}) collective-permute-start(bf16[8,48,896]{2,1,0:T(8,128)(2,1)} %pad_maximum_fusion.refs_0_), channel_id=1, source_target_pairs={{0,16},{16,0},{32,48},{48,32},{1,17},{17,1},{33,49},{49,33},{2,18}... | collective-permute-start | bytes 2064392 | tf_op jit(solution)/shard_map/ppermute | solution.py:31
  75.2 33.2 %collective-permute-start.16 = (bf16[8,48,896]{2,1,0:T(8,128)(2,1)}, bf16[8,48,896]{2,1,0:T(8,128)(2,1)}, u32[]{:S(2)}, u32[]{:S(2)}) collective-permute-start(bf16[8,48,896]{2,1,0:T(8,128)(2,1)} %pad_maximum_fusion.refs_0_), channel_id=1, source_target_pairs={{0,32},{16,48},{32,0},{48,16},{1,33},{17,49},{33,1},{49,17},{2,34}... | collective-permute-start | bytes 2064392 | tf_op jit(solution)/shard_map/ppermute | solution.py:31
  78.1 32.9 %collective-permute-start.17 = (bf16[8,48,896]{2,1,0:T(8,128)(2,1)}, bf16[8,48,896]{2,1,0:T(8,128)(2,1)}, u32[]{:S(2)}, u32[]{:S(2)}) collective-permute-start(bf16[8,48,896]{2,1,0:T(8,128)(2,1)} %pad_maximum_fusion.refs_0_), channel_id=1, source_target_pairs={{0,48},{16,32},{32,16},{48,0},{1,49},{17,33},{33,17},{49,1},{2,50}... | collective-permute-start | bytes 2064392 | tf_op jit(solution)/shard_map/ppermute | solution.py:31
  80.3 20.1 %collective-permute-start.14 = (bf16[96,3584]{1,0:T(8,128)(2,1)}, bf16[96,3584]{1,0:T(8,128)(2,1)}, u32[]{:S(2)}, u32[]{:S(2)}) collective-permute-start(bf16[96,3584]{1,0:T(8,128)(2,1)} %slice.39), channel_id=1, source_target_pairs={{0,128},{64,192},{128,0},{192,64},{1,129},{65,193},{129,1},{193,65... | collective-permute-start | bytes 2064392 | tf_op jit(solution)/shard_map/ppermute | solution.py:27
  84.4 16.0 %collective-permute-start.13 = (bf16[640,512]{1,0:T(8,128)(2,1)}, bf16[640,512]{1,0:T(8,128)(2,1)}, u32[]{:S(2)}, u32[]{:S(2)}) collective-permute-start(bf16[640,512]{1,0:T(8,128)(2,1)} %constant_dynamic-slice_fusion.2), channel_id=1, source_target_pairs={{0,192},{64,128},{128,64},{192,0},{1,193},{65,129},{129,65},{193,1... | collective-permute-start | bytes 1966088 | tf_op jit(solution)/shard_map/ppermute | solution.py:27
  100.4 13.4 %collective-permute-start.19 = (bf16[640,512]{1,0:T(8,128)(2,1)}, bf16[640,512]{1,0:T(8,128)(2,1)}, u32[]{:S(2)}, u32[]{:S(2)}) collective-permute-start(bf16[640,512]{1,0:T(8,128)(2,1)} %copy-done.7), channel_id=1, source_target_pairs={{0,1},{1,0},{2,3},{3,2},{4,5},{5,4},{6,7},{7,6},{8,9},{9,8},{10,11... | collective-permute-start | bytes 1966088 | tf_op jit(solution)/shard_map/ppermute | solution.py:31
  111.0 2.8 %collective-permute-start.20 = (bf16[640,512]{1,0:T(8,128)(2,1)}, bf16[640,512]{1,0:T(8,128)(2,1)}, u32[]{:S(2)}, u32[]{:S(2)}) collective-permute-start(bf16[640,512]{1,0:T(8,128)(2,1)} %collective-permute-done.13.refs_9_), channel_id=1, source_target_pairs={{0,1},{1,0},{2,3},{3,2},{4,5},{5,4},{6,7},{7,6},{8,9},{9,8},{10,11... | collective-permute-start | bytes 1966088 | tf_op jit(solution)/shard_map/ppermute | solution.py:31
  111.0 2.8 %collective-permute-start.18 = (bf16[256,512]{1,0:T(8,128)(2,1)}, bf16[256,512]{1,0:T(8,128)(2,1)}, u32[]{:S(2)}, u32[]{:S(2)}) collective-permute-start(bf16[256,512]{1,0:T(8,128)(2,1)} %collective-permute-done.5.refs_7_), channel_id=1, source_target_pairs={{0,1},{1,0},{2,3},{3,2},{4,5},{5,4},{6,7},{7,6},{8,9},{9,8},{10,11... | collective-permute-start | bytes 786440 | tf_op jit(solution)/shard_map/ppermute | solution.py:31
  129.2 52.7 %collective-permute-start.35 = (bf16[2048,1792]{1,0:T(8,128)(2,1)}, bf16[2048,1792]{1,0:T(8,128)(2,1)}, u32[]{:S(2)}, u32[]{:S(2)}) collective-permute-start(bf16[2048,1792]{1,0:T(8,128)(2,1)} %bitcast.11.refs_1_.refs_4_.refs_7_), channel_id=1, source_target_pairs={{0,1},{1,0},{2,3},{3,2},{4,5},{5,4},{6,7},{7,6},{8,9},{9,8},{10,11... | collective-permute-start | bytes 22020104 | tf_op jit(solution)/shard_map/ppermute | solution.py:31
  129.4 4.1 %collective-permute-start.21 = (f32[4,8,256]{2,1,0:T(8,128)S(1)}, f32[4,8,256]{2,1,0:T(8,128)S(1)}, u32[]{:S(2)}, u32[]{:S(2)}) collective-permute-start(f32[4,8,256]{2,1,0:T(8,128)S(1)} %get-tuple-element.72), channel_id=1, source_target_pairs={{0,128},{64,192},{128,0},{192,64},{1,129},{65,193},{129,1},{193,65... | collective-permute-start | bytes 98312 | tf_op jit(solution)/shard_map/ppermute | solution.py:27
  131.5 5.4 %collective-permute-start.22 = (f32[4,8,256]{2,1,0:T(8,128)S(1)}, f32[4,8,256]{2,1,0:T(8,128)S(1)}, u32[]{:S(2)}, u32[]{:S(2)}) collective-permute-start(f32[4,8,256]{2,1,0:T(8,128)S(1)} %get-tuple-element.72), channel_id=1, source_target_pairs={{0,64},{64,0},{128,192},{192,128},{1,65},{65,1},{129,193},{193,129... | collective-permute-start | bytes 98312 | tf_op jit(solution)/shard_map/ppermute | solution.py:27
  131.6 5.4 %collective-permute-start.23 = (f32[4,8,256]{2,1,0:T(8,128)S(1)}, f32[4,8,256]{2,1,0:T(8,128)S(1)}, u32[]{:S(2)}, u32[]{:S(2)}) collective-permute-start(f32[4,8,256]{2,1,0:T(8,128)S(1)} %get-tuple-element.72), channel_id=1, source_target_pairs={{0,192},{64,128},{128,64},{192,0},{1,193},{65,129},{129,65},{193,1... | collective-permute-start | bytes 98312 | tf_op jit(solution)/shard_map/ppermute | solution.py:27
  137.0 14.3 %collective-permute-start.24 = (f32[4,8,256]{2,1,0:T(8,128)S(1)}, f32[4,8,256]{2,1,0:T(8,128)S(1)}, u32[]{:S(2)}, u32[]{:S(2)}) collective-permute-start(f32[4,8,256]{2,1,0:T(8,128)S(1)} %add_add_fusion.2), channel_id=1, source_target_pairs={{0,16},{16,0},{32,48},{48,32},{1,17},{17,1},{33,49},{49,33},{2,18}... | collective-permute-start | bytes 98312 | tf_op jit(solution)/shard_map/ppermute | solution.py:31
  137.1 14.2 %collective-permute-start.25 = (f32[4,8,256]{2,1,0:T(8,128)S(1)}, f32[4,8,256]{2,1,0:T(8,128)S(1)}, u32[]{:S(2)}, u32[]{:S(2)}) collective-permute-start(f32[4,8,256]{2,1,0:T(8,128)S(1)} %add_add_fusion.2), channel_id=1, source_target_pairs={{0,32},{16,48},{32,0},{48,16},{1,33},{17,49},{33,1},{49,17},{2,34}... | collective-permute-start | bytes 98312 | tf_op jit(solution)/shard_map/ppermute | solution.py:31
  138.8 14.6 %collective-permute-start.26 = (f32[4,8,256]{2,1,0:T(8,128)S(1)}, f32[4,8,256]{2,1,0:T(8,128)S(1)}, u32[]{:S(2)}, u32[]{:S(2)}) collective-permute-start(f32[4,8,256]{2,1,0:T(8,128)S(1)} %add_add_fusion.2), channel_id=1, source_target_pairs={{0,48},{16,32},{32,16},{48,0},{1,49},{17,33},{33,17},{49,1},{2,50}... | collective-permute-start | bytes 98312 | tf_op jit(solution)/shard_map/ppermute | solution.py:31
  153.4 8.5 %collective-permute-start.27 = (f32[4,8,256]{2,1,0:T(8,128)S(1)}, f32[4,8,256]{2,1,0:T(8,128)S(1)}, u32[]{:S(2)}, u32[]{:S(2)}) collective-permute-start(f32[4,8,256]{2,1,0:T(8,128)S(1)} %add_add_fusion.1), channel_id=1, source_target_pairs={{0,2},{2,0},{4,6},{6,4},{8,10},{10,8},{12,14},{14,12},{1,3},{3,1},... | collective-permute-start | bytes 98312 | tf_op jit(solution)/shard_map/ppermute | solution.py:31
  155.7 8.0 %collective-permute-start.28 = (f32[4,8,256]{2,1,0:T(8,128)S(1)}, f32[4,8,256]{2,1,0:T(8,128)S(1)}, u32[]{:S(2)}, u32[]{:S(2)}) collective-permute-start(f32[4,8,256]{2,1,0:T(8,128)S(1)} %add_add_fusion.1), channel_id=1, source_target_pairs={{0,4},{2,6},{4,0},{6,2},{8,12},{10,14},{12,8},{14,10},{1,5},{3,7},... | collective-permute-start | bytes 98312 | tf_op jit(solution)/shard_map/ppermute | solution.py:31
  155.7 11.4 %collective-permute-start.29 = (f32[4,8,256]{2,1,0:T(8,128)S(1)}, f32[4,8,256]{2,1,0:T(8,128)S(1)}, u32[]{:S(2)}, u32[]{:S(2)}) collective-permute-start(f32[4,8,256]{2,1,0:T(8,128)S(1)} %add_add_fusion.1), channel_id=1, source_target_pairs={{0,6},{2,4},{4,2},{6,0},{8,14},{10,12},{12,10},{14,8},{1,7},{3,5},... | collective-permute-start | bytes 98312 | tf_op jit(solution)/shard_map/ppermute | solution.py:31
  158.1 9.2 %collective-permute-start.30 = (f32[4,8,256]{2,1,0:T(8,128)S(1)}, f32[4,8,256]{2,1,0:T(8,128)S(1)}, u32[]{:S(2)}, u32[]{:S(2)}) collective-permute-start(f32[4,8,256]{2,1,0:T(8,128)S(1)} %add_add_fusion.1), channel_id=1, source_target_pairs={{0,8},{2,10},{4,12},{6,14},{8,0},{10,2},{12,4},{14,6},{1,9},{3,11}... | collective-permute-start | bytes 98312 | tf_op jit(solution)/shard_map/ppermute | solution.py:31
  161.9 7.3 %collective-permute-start.31 = (f32[4,8,256]{2,1,0:T(8,128)S(1)}, f32[4,8,256]{2,1,0:T(8,128)S(1)}, u32[]{:S(2)}, u32[]{:S(2)}) collective-permute-start(f32[4,8,256]{2,1,0:T(8,128)S(1)} %add_add_fusion.1), channel_id=1, source_target_pairs={{0,10},{2,8},{4,14},{6,12},{8,2},{10,0},{12,6},{14,4},{1,11},{3,9}... | collective-permute-start | bytes 98312 | tf_op jit(solution)/shard_map/ppermute | solution.py:31
  163.6 6.0 %collective-permute-start.32 = (f32[4,8,256]{2,1,0:T(8,128)S(1)}, f32[4,8,256]{2,1,0:T(8,128)S(1)}, u32[]{:S(2)}, u32[]{:S(2)}) collective-permute-start(f32[4,8,256]{2,1,0:T(8,128)S(1)} %add_add_fusion.1), channel_id=1, source_target_pairs={{0,12},{2,14},{4,8},{6,10},{8,4},{10,6},{12,0},{14,2},{1,13},{3,15... | collective-permute-start | bytes 98312 | tf_op jit(solution)/shard_map/ppermute | solution.py:31
  167.1 5.1 %collective-permute-start.33 = (f32[4,8,256]{2,1,0:T(8,128)S(1)}, f32[4,8,256]{2,1,0:T(8,128)S(1)}, u32[]{:S(2)}, u32[]{:S(2)}) collective-permute-start(f32[4,8,256]{2,1,0:T(8,128)S(1)} %add_add_fusion.1), channel_id=1, source_target_pairs={{0,14},{2,12},{4,10},{6,8},{8,6},{10,4},{12,2},{14,0},{1,15},{3,13... | collective-permute-start | bytes 98312 | tf_op jit(solution)/shard_map/ppermute | solution.py:31
  177.9 21.0 %collective-permute-start.34 = (bf16[2,192,1024]{2,1,0:T(8,128)(2,1)}, bf16[2,192,1024]{2,1,0:T(8,128)(2,1)S(1)}, u32[]{:S(2)}, u32[]{:S(2)}) collective-permute-start(bf16[2,192,1024]{2,1,0:T(8,128)(2,1)} %get-tuple-element.75), channel_id=1, source_target_pairs={{0,128},{64,192},{128,0},{192,64},{1,129},{65,193},{129,1},{193,65... | collective-permute-start | bytes 2359304 | tf_op jit(solution)/shard_map/ppermute | solution.py:27
  180.3 30.3 %collective-permute-start.36 = (bf16[2,192,1024]{2,1,0:T(8,128)(2,1)}, bf16[2,192,1024]{2,1,0:T(8,128)(2,1)}, u32[]{:S(2)}, u32[]{:S(2)}) collective-permute-start(bf16[2,192,1024]{2,1,0:T(8,128)(2,1)} %get-tuple-element.77.refs_0_), channel_id=1, source_target_pairs={{0,64},{64,0},{128,192},{192,128},{1,65},{65,1},{129,193},{193,129... | collective-permute-start | bytes 2359304 | tf_op jit(solution)/shard_map/ppermute | solution.py:27
  181.3 30.7 %collective-permute-start.37 = (bf16[2,192,1024]{2,1,0:T(8,128)(2,1)}, bf16[2,192,1024]{2,1,0:T(8,128)(2,1)}, u32[]{:S(2)}, u32[]{:S(2)}) collective-permute-start(bf16[2,192,1024]{2,1,0:T(8,128)(2,1)} %get-tuple-element.75), channel_id=1, source_target_pairs={{0,192},{64,128},{128,64},{192,0},{1,193},{65,129},{129,65},{193,1... | collective-permute-start | bytes 2359304 | tf_op jit(solution)/shard_map/ppermute | solution.py:27
  224.4 7.7 %collective-permute-start.39 = (bf16[2,48,1792]{2,1,0:T(8,128)(2,1)}, bf16[2,48,1792]{2,1,0:T(8,128)(2,1)S(1)}, u32[]{:S(2)}, u32[]{:S(2)}) collective-permute-start(bf16[2,48,1792]{2,1,0:T(8,128)(2,1)} %get-tuple-element.82), channel_id=1, source_target_pairs={{0,16},{16,0},{32,48},{48,32},{1,17},{17,1},{33,49},{49,33},{2,18}... | collective-permute-start | bytes 1032200 | tf_op jit(solution)/shard_map/ppermute | solution.py:31
  224.4 13.6 %collective-permute-start.40 = (bf16[2,48,1792]{2,1,0:T(8,128)(2,1)}, bf16[2,48,1792]{2,1,0:T(8,128)(2,1)S(1)}, u32[]{:S(2)}, u32[]{:S(2)}) collective-permute-start(bf16[2,48,1792]{2,1,0:T(8,128)(2,1)} %get-tuple-element.83), channel_id=1, source_target_pairs={{0,32},{16,48},{32,0},{48,16},{1,33},{17,49},{33,1},{49,17},{2,34}... | collective-permute-start | bytes 1032200 | tf_op jit(solution)/shard_map/ppermute | solution.py:31
  228.8 12.5 %collective-permute-start.41 = (bf16[2,48,1792]{2,1,0:T(8,128)(2,1)}, bf16[2,48,1792]{2,1,0:T(8,128)(2,1)}, u32[]{:S(2)}, u32[]{:S(2)}) collective-permute-start(bf16[2,48,1792]{2,1,0:T(8,128)(2,1)} %get-tuple-element.84), channel_id=1, source_target_pairs={{0,48},{16,32},{32,16},{48,0},{1,49},{17,33},{33,17},{49,1},{2,50}... | collective-permute-start | bytes 1032200 | tf_op jit(solution)/shard_map/ppermute | solution.py:31
  229.9 1.2 collective-permute-start.38
  245.2 6.0 %collective-permute-start.42 = (bf16[32,1792]{1,0:T(8,128)(2,1)S(1)}, bf16[32,1792]{1,0:T(8,128)(2,1)S(1)}, u32[]{:S(2)}, u32[]{:S(2)}) collective-permute-start(bf16[32,1792]{1,0:T(8,128)(2,1)S(1)} %get-tuple-element.86), channel_id=1, source_target_pairs={{0,2},{2,0},{4,6},{6,4},{8,10},{10,8},{12,14},{14,12},{1,3},{3,1},... | collective-permute-start | bytes 344072 | tf_op jit(solution)/shard_map/ppermute | solution.py:31
  247.7 6.3 %collective-permute-start.43 = (bf16[32,1792]{1,0:T(8,128)(2,1)S(1)}, bf16[32,1792]{1,0:T(8,128)(2,1)S(1)}, u32[]{:S(2)}, u32[]{:S(2)}) collective-permute-start(bf16[32,1792]{1,0:T(8,128)(2,1)S(1)} %get-tuple-element.87), channel_id=1, source_target_pairs={{0,64},{64,0},{128,192},{192,128},{1,65},{65,1},{129,193},{193,129... | collective-permute-start | bytes 344072 | tf_op jit(solution)/shard_map/ppermute | solution.py:27
  251.1 7.7 %collective-permute-start.44 = (bf16[32,1792]{1,0:T(8,128)(2,1)S(1)}, bf16[32,1792]{1,0:T(8,128)(2,1)S(1)}, u32[]{:S(2)}, u32[]{:S(2)}) collective-permute-start(bf16[32,1792]{1,0:T(8,128)(2,1)S(1)} %get-tuple-element.88), channel_id=1, source_target_pairs={{0,66},{2,64},{4,70},{6,68},{8,74},{10,72},{12,78},{14,76},{64,2},... | collective-permute-start | bytes 344072 | tf_op jit(solution)/shard_map/ppermute | solution.py:425
  261.9 6.5 %collective-permute-start.45 = (bf16[8,3584]{1,0:T(8,128)(2,1)}, bf16[8,3584]{1,0:T(8,128)(2,1)S(1)}, u32[]{:S(2)}, u32[]{:S(2)}) collective-permute-start(bf16[8,3584]{1,0:T(8,128)(2,1)} %get-tuple-element.90), channel_id=1, source_target_pairs={{0,4},{2,6},{4,0},{6,2},{8,12},{10,14},{12,8},{14,10},{1,5},{3,7},... | collective-permute-start | bytes 172040 | tf_op jit(solution)/shard_map/ppermute | solution.py:31
  261.9 8.4 %collective-permute-start.46 = (bf16[8,3584]{1,0:T(8,128)(2,1)}, bf16[8,3584]{1,0:T(8,128)(2,1)S(1)}, u32[]{:S(2)}, u32[]{:S(2)}) collective-permute-start(bf16[8,3584]{1,0:T(8,128)(2,1)} %get-tuple-element.91), channel_id=1, source_target_pairs={{0,8},{2,10},{4,12},{6,14},{8,0},{10,2},{12,4},{14,6},{1,9},{3,11}... | collective-permute-start | bytes 172040 | tf_op jit(solution)/shard_map/ppermute | solution.py:31
  265.4 6.5 %collective-permute-start.47 = (bf16[8,3584]{1,0:T(8,128)(2,1)}, bf16[8,3584]{1,0:T(8,128)(2,1)S(1)}, u32[]{:S(2)}, u32[]{:S(2)}) collective-permute-start(bf16[8,3584]{1,0:T(8,128)(2,1)} %get-tuple-element.92), channel_id=1, source_target_pairs={{0,12},{2,14},{4,8},{6,10},{8,4},{10,6},{12,0},{14,2},{1,13},{3,15... | collective-permute-start | bytes 172040 | tf_op jit(solution)/shard_map/ppermute | solution.py:31
  (17 other events, 243.2 us)

commit v4 on v3

--- a/solution.py
+++ b/solution.py
@@ -16,7 +16,7 @@
 ROWS = 192
 QUARTER = 512
 HALF_D = 1792
-CHUNKS = (256, 256, 640, 640)
+CHUNKS = (896, 896)
 TILE = 256
 VMEM = 50 * 1024 * 1024
 F32, BF16 = jnp.float32, jnp.bfloat16
@@ -36,10 +36,10 @@
 
 
 def logits_kernel(at, own, nbr_a, nbr_b, *refs):
-    far, head, mate, got, tgt = refs[:4], refs[4], refs[5], refs[6:14], refs[14]
-    logits, stats, rows, raw, sums = refs[15:]
+    far, head, mate, got, tgt = refs[0], refs[1], refs[2], refs[3:7], refs[7]
+    logits, stats, rows, raw, sums = refs[8:]
     step = pl.program_id(0)
-    tok, y, z = at[0], at[2], at[3]
+    tok, y = at[0], at[2]
 
     @pl.when(step == 0)
     def _():
@@ -53,22 +53,14 @@
         for k in range(4):
             d = y ^ k
             column = pl.multiple_of((d // 2 ^ tok) * HALF_D + d % 2 * 896, 128)
-            for s in range(8):
-                row = 2 * ROWS + (z ^ s) * 48
-                rows[pl.ds(pl.multiple_of(row, 16), 48), pl.ds(column, 896)] = far[k][s]
+            rows[2 * ROWS :, pl.ds(column, 896)] = far[:, k].reshape(2 * ROWS, 896)
         sums[...] = jnp.zeros_like(sums)
 
     lane = lax.broadcasted_iota(jnp.int32, (48, TILE), 1)
 
     def one(head, got, part, core):
-        total = jnp.dot(rows[:, :HALF_D], head[...], preferred_element_type=F32)
-        begin = HALF_D
-        for count, chunk in zip(CHUNKS, got):
-            total = total + jnp.dot(
-                rows[:, begin : begin + count], chunk[...], preferred_element_type=F32
-            )
-            begin += count
-        raw[...] = total
+        weights = jnp.concatenate([head[...]] + [chunk[...] for chunk in got], axis=0)
+        raw[...] = jnp.dot(rows[...], weights, preferred_element_type=F32)
         column = lane + (at[4 + core] + part * TILE)
         for chunk in range(8):
             pair, g = chunk // 4, chunk % 4
@@ -101,7 +93,7 @@
         for core in range(2):
             @pl.when(step == part * 2 + core)
             def _(part=part, core=core):
-                one((head, mate)[core], got[core * 4 : core * 4 + 4], part, core)
+                one((head, mate)[core], got[core * 2 : core * 2 + 2], part, core)
 
     @pl.when(step == 3)
     def _():
@@ -123,7 +115,7 @@
             grid=(4,),
             in_specs=[whole(ROWS, 2 * HALF_D)]
             + [whole(ROWS // 2, 2 * HALF_D)] * 2
-            + [whole(8, 48, 896)] * 4
+            + [whole(8, 4, 48, 896)]
             + [weights, pl.BlockSpec((HALF_D, TILE), lambda s, at: (0, s // 2))]
             + [pl.BlockSpec((c, TILE), lambda s, at: (0, s // 2)) for c in CHUNKS] * 2
             + [whole(2, ROWS, 128)],
@@ -146,7 +138,7 @@
             flops=4 * ROWS * 4 * TILE * 2 * HALF_D * 2, bytes_accessed=16 << 20, transcendentals=1 << 21
         ),
         name="logits",
-    )(at, own, *nbr, *far, head, mate, *got, tgt)
+    )(at, own, *nbr, far, head, mate, *got, tgt)
 
 
 def grad_kernel(at, logits, stats, tgt, mask, mine, theirs, scales):
@@ -205,23 +197,26 @@
     )(at, logits, stats, tgt, mask)
 
 
-def terms_kernel(at, *refs, ks, last):
+def terms_kernel(at, *refs, ks, add, last):
     refs = list(refs)
-    total = None
+    left, right = [], []
     for k in ks:
         grad, head, mate = refs[:3]
         refs = refs[3:]
         order = (0, 1) if k < 2 else (1, 0)
-        for core, weight in enumerate((head, mate)):
-            begin = core * QUARTER
-            left = jnp.concatenate([grad[t, :, begin : begin + QUARTER] for t in order], axis=0)
-            term = jnp.dot(left, weight[...], preferred_element_type=F32)
-            total = term if total is None else total + term
+        left.append(jnp.concatenate([grad[t] for t in order], axis=0))
+        right += [head[...], mate[...]]
+    total = jnp.dot(
+        jnp.concatenate(left, axis=1),
+        jnp.concatenate(right, axis=0),
+        preferred_element_type=F32,
+    )
+    if add:
+        total = total + refs.pop(0)[...]
     if not last:
         refs[0][...] = total
         return
-    total = total + refs[0][...]
-    outs, scratch = refs[1:5], refs[5]
+    outs, scratch = refs[:4], refs[4]
     for tok in range(2):
         for y in range(4):
             begin = tok * ROWS + y * 48
@@ -230,8 +225,7 @@
         outs[k][...] = scratch[at[2] ^ k].astype(outs[k].dtype)
 
 
-def terms_call(at, grads, head, mate, ks, acc=None):
-    last = acc is not None
+def terms_call(at, grads, head, mate, ks, acc=None, last=False):
     tile = pl.BlockSpec((2 * ROWS, TILE), lambda s, at: (0, s))
     in_specs, args = [], []
     for k, grad in zip(ks, grads):
@@ -240,14 +234,15 @@
         args += [grad, head, mate]
     out_specs, scratch = tile, []
     out_shape = jax.ShapeDtypeStruct((2 * ROWS, HALF_D), F32)
-    if last:
+    if acc is not None:
         in_specs.append(tile)
         args.append(acc)
+    if last:
         out_specs = [pl.BlockSpec((2, 48, TILE), lambda s, at: (0, 0, s))] * 4
         out_shape = [jax.ShapeDtypeStruct((2, 48, HALF_D), t) for t in (F32, BF16, BF16, BF16)]
         scratch = [pltpu.VMEM((4, 2, 48, TILE), F32)]
     return pl.pallas_call(
-        functools.partial(terms_kernel, ks=ks, last=last),
+        functools.partial(terms_kernel, ks=ks, add=acc is not None, last=last),
         grid_spec=pltpu.PrefetchScalarGridSpec(
             num_scalar_prefetch=1,
             grid=(HALF_D // TILE,),
@@ -267,20 +262,17 @@
 
 
 def rows_kernel(at, *refs):
-    parts, outs = refs[:4], refs[4:]
+    parts, out_ref = refs[:4], refs[4]
     total = parts[0][...]
     for part in parts[1:]:
         total = total + part[...].astype(F32)
-    z = at[3]
     out = lax.broadcasted_iota(jnp.int32, (128, 96), 0)
     src = lax.broadcasted_iota(jnp.int32, (128, 96), 1)
-    owner = ((z >> 1) ^ ((out >> 3) & 3)) * 2 + ((z ^ (out >> 6)) & 1)
     i = out & 7
-    wanted = ((out >> 5) & 1) * 48 + owner * 6 + i
+    wanted = ((out >> 6) ^ at[0]) * 48 + ((out >> 3) & 7) * 6 + i
     pick = jnp.where((src == wanted) & (i < 6), 1.0, 0.0).astype(BF16)
     low = jnp.dot(pick, total.reshape(96, 896).astype(BF16), preferred_element_type=F32)
-    for n in range(4):
-        outs[n][...] = low[n * 32 : n * 32 + 32].astype(BF16)
+    out_ref[...] = low.reshape(16, 8, 896).astype(BF16)
 
 
 def rows_call(at, parts):
@@ -290,51 +282,19 @@
             num_scalar_prefetch=1,
             grid=(2,),
             in_specs=[pl.BlockSpec((2, 48, 896), lambda s, at: (0, 0, s))] * 4,
-            out_specs=[pl.BlockSpec((32, 896), lambda s, at: (0, s))] * 4,
-        ),
-        out_shape=[jax.ShapeDtypeStruct((32, HALF_D), BF16)] * 4,
+            out_specs=pl.BlockSpec((16, 8, 896), lambda s, at: (0, 0, s)),
+        ),
+        out_shape=jax.ShapeDtypeStruct((16, 8, HALF_D), BF16),
         compiler_params=pltpu.CompilerParams(vmem_limit_bytes=VMEM),
         name="rows",
     )(at, *parts)
 
 
-def half_kernel(at, *refs):
-    parts, first, others, scratch = refs[:4], refs[4], refs[5:8], refs[8]
-    for side in range(2):
-        half = parts[2 * side][...].astype(F32) + parts[2 * side + 1][...].astype(F32)
-        begin = (at[0] ^ side) * HALF_D
-        scratch[:, pl.ds(pl.multiple_of(begin, 128), HALF_D)] = half
-    first[...] = scratch[0:8]
-    for m in range(1, 4):
-        others[m - 1][...] = scratch[m * 8 : m * 8 + 8].astype(BF16)
-
-
-def half_call(at, parts):
-    return pl.pallas_call(
-        half_kernel,
-        grid_spec=pltpu.PrefetchScalarGridSpec(
-            num_scalar_prefetch=1,
-            grid=(1,),
-            in_specs=[whole(32, HALF_D)] * 4,
-            out_specs=[whole(8, 2 * HALF_D)] * 4,
-            scratch_shapes=[pltpu.VMEM((32, 2 * HALF_D), F32)],
-        ),
-        out_shape=[jax.ShapeDtypeStruct((8, 2 * HALF_D), t) for t in (F32, BF16, BF16, BF16)],
-        name="half",
-    )(at, *parts)
-
-
-def tree_sum(values):
-    values = list(values)
-    while len(values) > 1:
-        values = [a + b for a, b in zip(values[::2], values[1::2])]
-    return values[0]
-
-
 def add_over_slice(stats):
-    stats = tree_sum([stats] + [line_xor(stats, k) for k in (1, 2, 3)])
-    stats = tree_sum([stats] + [axis_xor(stats, "y", k) for k in (1, 2, 3)])
-    return tree_sum([stats] + [axis_xor(stats, "z", k) for k in range(1, 8)])
+    for axis in (LINE, "y", "z"):
+        spread = jnp.broadcast_to(stats[None], (lax.axis_size(axis), *stats.shape))
+        stats = jnp.sum(lax.all_to_all(spread, axis, 0, 0, tiled=True), axis=0)
+    return stats
 
 
 def pick_rows(block, count, core):
@@ -351,47 +311,38 @@
 
     sync = lax.optimization_barrier
 
-    def chunk(n):
-        return lax.dynamic_slice(head, (sum(CHUNKS[:n]), (3 - x) * QUARTER), (CHUNKS[n], QUARTER))
+    slab = pick_rows(lax.dynamic_slice(states, (z * 48, y * 896), (48, 896)), 24, core)
+    piece = jnp.concatenate([line_xor(slab, 2), line_xor(slab, 3)], axis=0)[None]
+    piece = jnp.concatenate([piece] + [axis_xor(piece, "y", k) for k in (1, 2, 3)])
+    piece, head, states = sync((piece, head, states))
+    far = lax.all_gather(piece[None], "z", axis=0, tiled=True)
 
     got = []
-    slab = pick_rows(lax.dynamic_slice(states, (z * 48, y * 896), (48, 896)), 24, core)
-    got.append(line_xor(chunk(0), 3))
-    slabs = [line_xor(slab, 2), line_xor(slab, 3)]
-    piece = jnp.concatenate(slabs, axis=0)
-    piece, got[0], head, states = sync((piece, got[0], head, states))
-
-    got.append(line_xor(chunk(1), 3))
-    far = jnp.concatenate([piece[None], axis_xor(piece[None], "z", 1)])
+    for n in range(2):
+        sent = lax.dynamic_slice(head, (n * 896, (3 - x) * QUARTER), (896, QUARTER))
+        got.append(line_xor(sent, 3))
     own = pick_rows(states, ROWS, core)
-    far, got[1], head, own = sync((far, got[1], head, own))
+    nbr = [line_xor(own[:96], 1)]
+    mate = axis_xor(lax.dynamic_slice(head, (0, x * QUARTER), (HALF_D, QUARTER)), "core", 1)
 
     voc = (y * 8 + z) * 2
     begin = [(voc + c) * 2048 + x * QUARTER for c in (core, 1 - core)]
     at = jnp.stack([tok, x, y, z, begin[0], begin[1]]).astype(jnp.int32)
     scal = jnp.stack([targets, loss_mask]).reshape(2, 32, 2, 6)
     scal = lax.dynamic_index_in_dim(scal, core, 2, keepdims=False).reshape(2, ROWS)
-
-    got.append(line_xor(chunk(2), 3))
-    nbr = [line_xor(own[:96], 1)]
-    far = jnp.concatenate([far] + [axis_xor(far, "z", k) for k in (2, 4, 6)])
-    mate = axis_xor(lax.dynamic_slice(head, (0, x * QUARTER), (HALF_D, QUARTER)), "core", 1)
-    got_mate = [axis_xor(got[0], "core", 1)]
     scal = jnp.stack([scal, line_xor(scal, 2)], axis=1)
     mask = scal[1].astype(F32)
     tgt_wide = jnp.broadcast_to(scal[0][..., None], (2, ROWS, 128))
     mask_wide = jnp.broadcast_to(mask[..., None], (2, ROWS, 128))
-    far, got[2], nbr[0], head, own, mate, got_mate[0], tgt_wide, mask_wide = sync(
-        (far, got[2], nbr[0], head, own, mate, got_mate[0], tgt_wide, mask_wide)
-    )
-
-    got.append(line_xor(chunk(3), 3))
+
+    head, tgt_wide, mask_wide, mate, got[0], nbr[0], own = sync(
+        (head, tgt_wide, mask_wide, mate, got[0], nbr[0], own)
+    )
     nbr.append(line_xor(own[96:], 1))
-    far = [far] + [axis_xor(far, "y", k) for k in (1, 2, 3)]
-    got_mate += [axis_xor(got[n], "core", 1) for n in (1, 2)]
+    got_mate = [axis_xor(got[0], "core", 1)]
     head_t = head.T
-    head_t, got[3], nbr[1], *far = sync((head_t, got[3], nbr[1], *far))
-    got_mate.append(axis_xor(got[3], "core", 1))
+    head_t, got[1], got_mate[0] = sync((head_t, got[1], got_mate[0]))
+    got_mate.append(axis_xor(got[1], "core", 1))
     got = got + got_mate
 
     logits, stats = logits_call(at, own, nbr, far, head, mate, got, tgt_wide)
@@ -402,7 +353,8 @@
     mine, theirs = grad_call(at, logits, stats, tgt_wide, mask_wide)
     grads = [mine, line_xor(theirs, 1), line_xor(mine, 2), line_xor(theirs, 3)]
     terms = terms_call(at, grads[:1], head_t, mate_t, (0,))
-    parts = list(terms_call(at, grads[1:], head_t, mate_t, (1, 2, 3), terms))
+    terms = terms_call(at, grads[1:2], head_t, mate_t, (1,), terms)
+    parts = list(terms_call(at, grads[2:], head_t, mate_t, (2, 3), terms, last=True))
 
     stats, parts[0] = sync((stats, parts[0]))
     stats = lax.dynamic_index_in_dim(stats, x, 0, keepdims=False)
@@ -417,18 +369,10 @@
 
     parts = [parts[0]] + [axis_xor(parts[k], "y", k) for k in (1, 2, 3)]
     token_loss, parts[0] = sync((token_loss, parts[0]))
-    parts = rows_call(at, parts)
-    parts = [
-        parts[0],
-        axis_xor(parts[2], "z", 1),
-        line_xor(parts[1], 2),
-        lax.ppermute(parts[3], ("tok", "z"), [(i, i ^ 9) for i in range(16)]),
-    ]
-    parts = half_call(at, parts)
-    total = parts[0]
-    for m in (1, 2, 3):
-        total = total + axis_xor(parts[m], "z", 2 * m).astype(F32)
-    return total[:6].astype(BF16)[None], token_loss
+    low = lax.all_to_all(rows_call(at, parts), ("tok", "z"), 0, 0, tiled=True)
+    total = jnp.sum(low.reshape(2, 8, 8, HALF_D).astype(F32), axis=1)[:, :6]
+    out = jnp.concatenate([total[0], total[1]], axis=1)
+    return out.astype(BF16)[None], token_loss
 
 
 def solution(mesh):

time: 279 us -> 245 us (0.88); the launches traced: 274 us -> 244 us
  starting transfers between devices: 84.2 us -> 25.4 us
  blocking collectives: 0 us -> 52 us
  waiting for transfers between devices: 107 us -> 74.3 us
  between operations: 1.17 us -> 14.3 us
  local copies, waits for them, and re-layouts: 33.1 us -> 29.6 us
  other arithmetic: 4.66 us -> 1.71 us
    all_to_all x0 -> x4, blocking collectives: none -> 52 us  [the longest x3 35.6 us: add_over_slice(): stats = jnp.sum(lax.all_to_all(spread, axis, 0, 0, tiled=True), axis=0)]
    ppermute x31 -> x11, starting transfers between devices: 59.5 us -> 9.74 us  [axis_xor(): lax.ppermute(block, axis, [(i, i ^ k) for i in range(lax.axis_size(axis))])]
    ppermute x31 -> x11, waiting for transfers between devices: 47.8 us -> 14.4 us  [axis_xor(): lax.ppermute(block, axis, [(i, i ^ k) for i in range(lax.axis_size(axis))])]
    ppermute x16 -> x10, starting transfers between devices: 24.7 us -> 15.6 us  [line_xor(): return lax.ppermute(block, LINE, [(x, x ^ k) for x in range(N_X)])]
    ppermute x16 -> x10, waiting for transfers between devices: 54 us -> 59.8 us  [line_xor(): return lax.ppermute(block, LINE, [(x, x ^ k) for x in range(N_X)])]
    ppermute x1 -> x0, waiting for transfers between devices: 4.8 us -> none  [shards(): lax.ppermute(parts[3], ('tok', 'z'), [(i, i ^ 9) for i in range(16)])]
    dynamic_slice x4 -> x1, local copies, waits for them, and re-layouts: 5.86 us -> 2.83 us  [shards(): sent = lax.dynamic_slice(head, (n * 896, (3 - x) * QUARTER), (896, QUARTER))]
    unnamed x36 -> x20, local copies, waits for them, and re-layouts: 8.44 us -> 7.82 us
  transfers between devices with their start and end apart: 48 -> 22, of which waited for: 27 -> 15; matrix products, arithmetic and copies ran while one was open for 9% -> 9% of each run, Pallas kernels for 4% -> 8%
where the time goes in v4:
time: 245 us; the launch traced here: 244 us
  waiting for transfers between devices  74.3 us (30%)
  blocking collectives  52 us (21%)
  Pallas kernels  45.3 us (18%)
  local copies, waits for them, and re-layouts  29.6 us (12%)
  starting transfers between devices  25.4 us (10%)
  between operations  14.3 us (6%)
    ppermute x10, waiting for transfers between devices, line_xor(): return lax.ppermute(block, LINE, [(x, x ^ k) for x in range(N_X)])  59.8 us
    all_to_all x3, blocking collectives, add_over_slice(): stats = jnp.sum(lax.all_to_all(spread, axis, 0, 0, tiled=True), axis=0)  35.6 us
    pallas_call x3, Pallas kernels, terms_call(): pl.pallas_call(functools.partial(terms_kernel, ks=ks, add=acc is not None...  23.4 us
    all_to_all x1, blocking collectives, shards(): low = lax.all_to_all(rows_call(at, parts), ('tok', 'z'), 0, 0, tiled=True)  16.4 us
    ppermute x10, starting transfers between devices, line_xor(): return lax.ppermute(block, LINE, [(x, x ^ k) for x in range(N_X)])  15.6 us
    ppermute x11, waiting for transfers between devices, axis_xor(): lax.ppermute(block, axis, [(i, i ^ k) for i in range(lax.axis_size(axis))])  14.4 us
    pallas_call x1, Pallas kernels, logits_call(): pl.pallas_call(logits_kernel, grid_spec=pltpu.PrefetchScalarGridSpec(num_...  14 us
    optimization_barrier x1, local copies, waits for them, and re-layouts, shards(): sync((head, tgt_wide, mask_wide, mate, got[0], nbr[0], own))  10.1 us
  transfers between devices with their start and end apart: 22, of which 15 were waited for; matrix products, arithmetic and copies ran while one was open for 9% of the time, Pallas kernels for 8%

profile of v4, /device:TPU:2, one launch (start us, length us, event | category | flops | bytes accessed | tf_op | source)
XLA Modules:
  0.0 243.8 jit_solution(4161659075068686710)
XLA Ops:
  7.3 1.7 copy-done
  9.2 2.2 collective-permute-start.1
  11.4 1.6 collective-permute-start.2
  13.0 1.8 collective-permute-done.1
  15.4 1.7 collective-permute-start.3
  17.1 2.9 %collective-permute-start.4 = (bf16[1,48,896]{2,1,0:T(8,128)(2,1)S(1)}, bf16[1,48,896]{2,1,0:T(8,128)(2,1)S(1)}, u32[]{:S(2)}, u32[]{:S(2)}) collective-permute-start(bf16[1,48,896]{2,1,0:T(8,128)(2,1)S(1)} %maximum_bitcast_fusion), channel_id=1, source_target_pairs={{0,32},{16,48},{32,0},{48,16},{1,33},{17,49},{33,1},{49,17},{2,34}... | collective-permute-start | bytes 258056 | tf_op jit(solution)/shard_map/ppermute | solution.py:31
  20.8 2.7 %collective-permute-done.4 = bf16[1,48,896]{2,1,0:T(8,128)(2,1)S(1)} collective-permute-done((bf16[1,48,896]{2,1,0:T(8,128)(2,1)S(1)}, bf16[1,48,896]{2,1,0:T(8,128)(2,1)S(1)}, u32[]{:S(2)}, u32[]{:S(2)}) %collective-permute-start.4) | collective-permute-done | bytes 86048 | tf_op jit(solution)/shard_map/ppermute | solution.py:31
  23.5 2.2 collective-permute-done.5
  26.5 2.9 %constant_dynamic-slice_fusion.1 = bf16[1792,512]{1,0:T(8,128)(2,1)} fusion(bf16[1792,2048]{1,0:T(8,128)(2,1)} %refs_1_, s32[]{:T(128)S(6)} %select_n.58), kind=kLoop, calls=%fused_computation.47 | loop fusion | bytes 3670020 | tf_op jit(solution)/shard_map/dynamic_slice | solution.py:326
  29.4 2.8 %constant_dynamic-slice_fusion.2 = (bf16[896,512]{1,0:T(8,128)(2,1)}, bf16[896,512]{1,0:T(8,128)(2,1)}) fusion(bf16[1792,2048]{1,0:T(8,128)(2,1)} %refs_1_, s32[]{:T(128)S(6)} %select_n.59), kind=kLoop, calls=%fused_computation.62 | loop fusion | bytes 3670020 | tf_op jit(solution)/shard_map/dynamic_slice | solution.py:322
  32.3 0.9 collective-permute-start.7
  33.1 1.0 convolution_convert_fusion.own
  34.2 1.2 copy-done.6
  35.3 0.9 slice.56
  36.2 2.9 %collective-permute-start.8 = (bf16[96,3584]{1,0:T(8,128)(2,1)}, bf16[96,3584]{1,0:T(8,128)(2,1)S(1)}, u32[]{:S(2)}, u32[]{:S(2)}) collective-permute-start(bf16[96,3584]{1,0:T(8,128)(2,1)} %slice.56), channel_id=1, source_target_pairs={{0,128},{64,192},{128,0},{192,64},{1,129},{65,193},{129,1},{193,65... | collective-permute-start | bytes 2064392 | tf_op jit(solution)/shard_map/ppermute | solution.py:27
  39.9 1.0 collective-permute-start
  41.0 15.1 %collective-permute-done = s32[2,192]{1,0:T(2,128)S(1)} collective-permute-done((s32[2,192]{1,0:T(2,128)S(1)}, s32[2,192]{1,0:T(2,128)S(1)}, u32[]{:S(2)}, u32[]{:S(2)}) %collective-permute-start) | collective-permute-done | bytes 1568 | tf_op jit(solution)/shard_map/ppermute | solution.py:27
  56.8 0.9 copy-done.4
  58.0 10.1 %copy.21 = bf16[1792,2048]{0,1:T(8,128)(2,1)} copy(bf16[1792,2048]{1,0:T(8,128)(2,1)} %refs_1_) | data formatting | bytes 14680064 | tf_op jit(solution)/shard_map/optimization_barrier | solution.py:338
  68.1 10.6 %collective-permute-done.9.refs_4_ = bf16[896,512]{1,0:T(8,128)(2,1)} collective-permute-done((bf16[896,512]{1,0:T(8,128)(2,1)}, bf16[896,512]{1,0:T(8,128)(2,1)}, u32[]{:S(2)}, u32[]{:S(2)}) %collective-permute-start.9) | collective-permute-done | bytes 917536 | tf_op jit(solution)/shard_map/ppermute | solution.py:27
  78.6 2.0 slice.46
  80.6 2.9 %collective-permute-start.11 = (bf16[96,3584]{1,0:T(8,128)(2,1)}, bf16[96,3584]{1,0:T(8,128)(2,1)}, u32[]{:S(2)}, u32[]{:S(2)}) collective-permute-start(bf16[96,3584]{1,0:T(8,128)(2,1)} %slice.46), channel_id=1, source_target_pairs={{0,128},{64,192},{128,0},{192,64},{1,129},{65,193},{129,1},{193,65... | collective-permute-start | bytes 2064392 | tf_op jit(solution)/shard_map/ppermute | solution.py:27
  83.6 16.3 %collective-permute-done.11.nbr_b = bf16[96,3584]{1,0:T(8,128)(2,1)} collective-permute-done((bf16[96,3584]{1,0:T(8,128)(2,1)}, bf16[96,3584]{1,0:T(8,128)(2,1)}, u32[]{:S(2)}, u32[]{:S(2)}) %collective-permute-start.11) | collective-permute-done | bytes 688160 | tf_op jit(solution)/shard_map/ppermute | solution.py:27
  99.9 1.1 copy-done.5
  101.0 14.0 %logits.1 = (f32[4,192,1024]{2,1,0:T(8,128)}, f32[4,8,256]{2,1,0:T(8,128)S(1)}) custom-call(s32[6]{0:T(128)S(1)} %stack.51.at, bf16[192,3584]{1,0:T(8,128)(2,1)} %copy-done.6, bf16[96,3584]{1,0:T(8,128)(2,1)S(1)} %copy-done.5, bf16[96,3584]{1,0:T(8,128)(2,1)} %collective-permute-done.11.nbr_b, bf16[8,4,48,896]{3,2,1,0:T(8,128)(2,1)} %bitcast.48, ...), custom_call_target="tpu_custom_call" | custom-call | flops 5637144576 | bytes 16777216 | tf_op jit(solution)/shard_map/logits/pallas_call | solution.py:111
  115.1 8.5 %all_to_all.20 = f32[4,4,8,256]{3,2,1,0:T(8,128)S(1)} all-to-all(f32[4,4,8,256]{3,2,1,0:T(8,128)S(1)} %broadcast_in_dim.21), channel_id=1, replica_groups=mesh['rep'=2,'tok'=2,'y'=4,'z'=8,'core'=2] {'rep','tok'}, dimensions={0} | all-to-all | bytes 262144 | tf_op jit(solution)/shard_map/all_to_all | solution.py:296
  123.7 8.4 %all_to_all.21 = f32[4,4,8,256]{3,2,1,0:T(8,128)S(1)} all-to-all(f32[4,4,8,256]{3,2,1,0:T(8,128)S(1)} %broadcast_in_dim.44), channel_id=1, replica_groups=mesh['rep'=2,'tok'=2,'y'=4,'z'=8,'core'=2] {'y'}, dimensions={0} | all-to-all | bytes 262144 | tf_op jit(solution)/shard_map/all_to_all | solution.py:296
  132.1 18.7 %all_to_all.22 = f32[8,4,8,256]{3,2,1,0:T(8,128)S(1)} all-to-all(f32[8,4,8,256]{3,2,1,0:T(8,128)S(1)} %broadcast_in_dim.45), channel_id=1, replica_groups=mesh['rep'=2,'tok'=2,'y'=4,'z'=8,'core'=2] {'z'}, dimensions={0} | all-to-all | bytes 524288 | tf_op jit(solution)/shard_map/all_to_all | solution.py:296
  150.9 5.6 %logit_grad.1 = (bf16[2,192,1024]{2,1,0:T(8,128)(2,1)}, bf16[2,192,1024]{2,1,0:T(8,128)(2,1)}) custom-call(s32[6]{0:T(128)S(1)} %stack.51.at, f32[4,192,1024]{2,1,0:T(8,128)} %get-tuple-element.43.logits, f32[4,8,256]{2,1,0:T(8,128)S(1)} %reduce_sum.38.stats, s32[2,192,128]{2,1,0:T(8,128)S(1)} %broadcast_in_dim.18.refs_7_.tgt, ...), custom_call_target="tpu_custom_call" | custom-call | tf_op jit(solution)/shard_map/logit_grad/pallas_call | solution.py:180
  156.5 1.5 collective-permute-start.16
  158.0 0.9 collective-permute-start.13
  158.9 1.1 collective-permute-start.15
  160.0 6.6 %gradient_terms.3.refs_3_ = f32[384,1792]{1,0:T(8,128)S(1)} custom-call(s32[6]{0:T(128)S(1)} %stack.51.at, bf16[2,192,1024]{2,1,0:T(8,128)(2,1)} %get-tuple-element.45.refs_0_, bf16[2048,1792]{1,0:T(8,128)(2,1)} %bitcast.11.refs_1_.refs_4_, bf16[2048,1792]{1,0:T(8,128)(2,1)} %collective-permute-done.14.refs_2_.refs_5_), custom_call_target="tpu_custom_call" | custom-call | flops 1409286144 | bytes 6291456 | tf_op jit(solution)/shard_map/gradient_terms/pallas_call | solution.py:244
  166.6 1.5 copy-done.2
  168.1 9.1 %collective-permute-done.16.refs_0_ = bf16[2,192,1024]{2,1,0:T(8,128)(2,1)S(1)} collective-permute-done((bf16[2,192,1024]{2,1,0:T(8,128)(2,1)}, bf16[2,192,1024]{2,1,0:T(8,128)(2,1)S(1)}, u32[]{:S(2)}, u32[]{:S(2)}) %collective-permute-start.16) | collective-permute-done | bytes 786464 | tf_op jit(solution)/shard_map/ppermute | solution.py:27
  177.2 6.9 %gradient_terms.4.refs_6_ = f32[384,1792]{1,0:T(8,128)S(1)} custom-call(s32[6]{0:T(128)S(1)} %stack.51.at, bf16[2,192,1024]{2,1,0:T(8,128)(2,1)S(1)} %collective-permute-done.16.refs_0_, bf16[2048,1792]{1,0:T(8,128)(2,1)} %bitcast.11.refs_1_.refs_4_, bf16[2048,1792]{1,0:T(8,128)(2,1)} %collective-permute-done.14.refs_2_.refs_5_, f32[384,1792]{1,0:T(8,128)} %copy-done.2), custom_call_target="tpu_custom_call" | custom-call | flops 1409286144 | bytes 6291456 | tf_op jit(solution)/shard_map/gradient_terms/pallas_call | solution.py:244
  184.1 1.5 copy-done.1
  185.6 4.9 %collective-permute-done.13.refs_0_ = bf16[2,192,1024]{2,1,0:T(8,128)(2,1)} collective-permute-done((bf16[2,192,1024]{2,1,0:T(8,128)(2,1)}, bf16[2,192,1024]{2,1,0:T(8,128)(2,1)}, u32[]{:S(2)}, u32[]{:S(2)}) %collective-permute-start.13) | collective-permute-done | bytes 786464 | tf_op jit(solution)/shard_map/ppermute | solution.py:27
  190.5 1.4 collective-permute-done.15.refs_3_
  191.9 9.9 %gradient_terms.5 = (f32[2,48,1792]{2,1,0:T(8,128)S(1)}, bf16[2,48,1792]{2,1,0:T(8,128)(2,1)}, bf16[2,48,1792]{2,1,0:T(8,128)(2,1)}, bf16[2,48,1792]{2,1,0:T(8,128)(2,1)}) custom-call(s32[6]{0:T(128)S(1)} %stack.51.at, bf16[2,192,1024]{2,1,0:T(8,128)(2,1)} %collective-permute-done.13.refs_0_, bf16[2048,1792]{1,0:T(8,128)(2,1)} %bitcast.11.refs_1_.refs_4_, ...), custom_call_target="tpu_custom_call" | custom-call | flops 2818572288 | bytes 12582912 | tf_op jit(solution)/shard_map/gradient_terms/pallas_call | solution.py:244
  202.4 2.2 collective-permute-start.19
  204.6 2.0 collective-permute-start.20
  207.6 0.9 collective-permute-done.17
  209.6 0.9 collective-permute-done.18.refs_1_
  210.5 4.6 %collective-permute-done.19.refs_2_ = bf16[2,48,1792]{2,1,0:T(8,128)(2,1)} collective-permute-done((bf16[2,48,1792]{2,1,0:T(8,128)(2,1)}, bf16[2,48,1792]{2,1,0:T(8,128)(2,1)}, u32[]{:S(2)}, u32[]{:S(2)}) %collective-permute-start.19) | collective-permute-done | bytes 344096 | tf_op jit(solution)/shard_map/ppermute | solution.py:31
  215.1 2.5 %collective-permute-done.20.refs_3_ = bf16[2,48,1792]{2,1,0:T(8,128)(2,1)} collective-permute-done((bf16[2,48,1792]{2,1,0:T(8,128)(2,1)}, bf16[2,48,1792]{2,1,0:T(8,128)(2,1)}, u32[]{:S(2)}, u32[]{:S(2)}) %collective-permute-start.20) | collective-permute-done | bytes 344096 | tf_op jit(solution)/shard_map/ppermute | solution.py:31
  217.6 2.2 rows.1
  219.9 16.4 %all_to_all.23 = bf16[16,8,1792]{2,1,0:T(8,128)(2,1)S(1)} all-to-all(bf16[16,8,1792]{2,1,0:T(8,128)(2,1)S(1)} %rows.1), channel_id=1, replica_groups=mesh['rep'=2,'tok'=2,'y'=4,'z'=8,'core'=2] {'tok','z'}, dimensions={0} | all-to-all | bytes 917504 | tf_op jit(solution)/shard_map/all_to_all | solution.py:372
  (76 shorter events, 7.9 us)
Async XLA Ops:
  7.2 1.8 copy-start
  7.2 92.8 %all-gather.3.cloned.1.call-start = ((), (), s32[]{:S(2)}) async-start(), calls=%async_computation.4 | async-start | bytes 3096576 | tf_op jit(solution)/shard_map/all_gather | solution.py:318
  9.2 5.6 %collective-permute-start.1 = (bf16[24,896]{1,0:T(8,128)(2,1)S(1)}, bf16[24,896]{1,0:T(8,128)(2,1)S(1)}, u32[]{:S(2)}, u32[]{:S(2)}) collective-permute-start(bf16[24,896]{1,0:T(8,128)(2,1)S(1)} %convolution_convert_fusion.1), channel_id=1, source_target_pairs={{0,64},{64,0},{128,192},{192,128},{1,65},{65,1},{129,193},{193,129... | collective-permute-start | bytes 129032 | tf_op jit(solution)/shard_map/ppermute | solution.py:27
  11.4 4.0 %collective-permute-start.2 = (bf16[24,896]{1,0:T(8,128)(2,1)S(1)}, bf16[24,896]{1,0:T(8,128)(2,1)S(1)}, u32[]{:S(2)}, u32[]{:S(2)}) collective-permute-start(bf16[24,896]{1,0:T(8,128)(2,1)S(1)} %convolution_convert_fusion.1), channel_id=1, source_target_pairs={{0,192},{64,128},{128,64},{192,0},{1,193},{65,129},{129,65},{193,1... | collective-permute-start | bytes 129032 | tf_op jit(solution)/shard_map/ppermute | solution.py:27
  15.4 5.4 %collective-permute-start.3 = (bf16[1,48,896]{2,1,0:T(8,128)(2,1)S(1)}, bf16[1,48,896]{2,1,0:T(8,128)(2,1)S(1)}, u32[]{:S(2)}, u32[]{:S(2)}) collective-permute-start(bf16[1,48,896]{2,1,0:T(8,128)(2,1)S(1)} %maximum_bitcast_fusion), channel_id=1, source_target_pairs={{0,16},{16,0},{32,48},{48,32},{1,17},{17,1},{33,49},{49,33},{2,18}... | collective-permute-start | bytes 258056 | tf_op jit(solution)/shard_map/ppermute | solution.py:31
  17.1 6.4 %collective-permute-start.4 = (bf16[1,48,896]{2,1,0:T(8,128)(2,1)S(1)}, bf16[1,48,896]{2,1,0:T(8,128)(2,1)S(1)}, u32[]{:S(2)}, u32[]{:S(2)}) collective-permute-start(bf16[1,48,896]{2,1,0:T(8,128)(2,1)S(1)} %maximum_bitcast_fusion), channel_id=1, source_target_pairs={{0,32},{16,48},{32,0},{48,16},{1,33},{17,49},{33,1},{49,17},{2,34}... | collective-permute-start | bytes 258056 | tf_op jit(solution)/shard_map/ppermute | solution.py:31
  20.0 5.7 %collective-permute-start.5 = (bf16[1,48,896]{2,1,0:T(8,128)(2,1)S(1)}, bf16[1,48,896]{2,1,0:T(8,128)(2,1)S(1)}, u32[]{:S(2)}, u32[]{:S(2)}) collective-permute-start(bf16[1,48,896]{2,1,0:T(8,128)(2,1)S(1)} %maximum_bitcast_fusion), channel_id=1, source_target_pairs={{0,48},{16,32},{32,16},{48,0},{1,49},{17,33},{33,17},{49,1},{2,50}... | collective-permute-start | bytes 258056 | tf_op jit(solution)/shard_map/ppermute | solution.py:31
  29.4 28.3 %collective-permute-start.6 = (bf16[1792,512]{1,0:T(8,128)(2,1)}, bf16[1792,512]{1,0:T(8,128)(2,1)}, u32[]{:S(2)}, u32[]{:S(2)}) collective-permute-start(bf16[1792,512]{1,0:T(8,128)(2,1)} %constant_dynamic-slice_fusion.1), channel_id=1, source_target_pairs={{0,1},{1,0},{2,3},{3,2},{4,5},{5,4},{6,7},{7,6},{8,9},{9,8},{10,11... | collective-permute-start | bytes 5505032 | tf_op jit(solution)/shard_map/ppermute | solution.py:31
  32.3 25.4 %collective-permute-start.7 = (bf16[896,512]{1,0:T(8,128)(2,1)}, bf16[896,512]{1,0:T(8,128)(2,1)}, u32[]{:S(2)}, u32[]{:S(2)}) collective-permute-start(bf16[896,512]{1,0:T(8,128)(2,1)} %get-tuple-element.59), channel_id=1, source_target_pairs={{0,192},{64,128},{128,64},{192,0},{1,193},{65,129},{129,65},{193,1... | collective-permute-start | bytes 2752520 | tf_op jit(solution)/shard_map/ppermute | solution.py:27
  33.1 6.0 %copy-start.7 = (s32[384]{0:T(512)S(1)}, s32[384]{0:T(512)}, u32[]{:S(2)}) copy-start(s32[384]{0:T(512)} %param.6) | copy-start | bytes 4612
  33.1 6.3 %copy-start.8 = (s32[384]{0:T(512)S(1)}, s32[384]{0:T(512)}, u32[]{:S(2)}) copy-start(s32[384]{0:T(512)} %param.7) | copy-start | bytes 4612
  34.1 1.2 copy-start.6
  36.2 20.6 %collective-permute-start.8 = (bf16[96,3584]{1,0:T(8,128)(2,1)}, bf16[96,3584]{1,0:T(8,128)(2,1)S(1)}, u32[]{:S(2)}, u32[]{:S(2)}) collective-permute-start(bf16[96,3584]{1,0:T(8,128)(2,1)} %slice.56), channel_id=1, source_target_pairs={{0,128},{64,192},{128,0},{192,64},{1,129},{65,193},{129,1},{193,65... | collective-permute-start | bytes 2064392 | tf_op jit(solution)/shard_map/ppermute | solution.py:27
  39.9 16.2 %collective-permute-start = (s32[2,192]{1,0:T(2,128)S(1)}, s32[2,192]{1,0:T(2,128)S(1)}, u32[]{:S(2)}, u32[]{:S(2)}) collective-permute-start(s32[2,192]{1,0:T(2,128)S(1)} %reshape.70), channel_id=1, source_target_pairs={{0,64},{64,0},{128,192},{192,128},{1,65},{65,1},{129,193},{193,129... | collective-permute-start | bytes 4616 | tf_op jit(solution)/shard_map/ppermute | solution.py:27
  56.2 22.5 %collective-permute-start.9 = (bf16[896,512]{1,0:T(8,128)(2,1)}, bf16[896,512]{1,0:T(8,128)(2,1)}, u32[]{:S(2)}, u32[]{:S(2)}) collective-permute-start(bf16[896,512]{1,0:T(8,128)(2,1)} %get-tuple-element.58), channel_id=1, source_target_pairs={{0,192},{64,128},{128,64},{192,0},{1,193},{65,129},{129,65},{193,1... | collective-permute-start | bytes 2752520 | tf_op jit(solution)/shard_map/ppermute | solution.py:27
  56.8 0.9 copy-start.4
  57.9 20.8 %collective-permute-start.10 = (bf16[896,512]{1,0:T(8,128)(2,1)}, bf16[896,512]{1,0:T(8,128)(2,1)}, u32[]{:S(2)}, u32[]{:S(2)}) collective-permute-start(bf16[896,512]{1,0:T(8,128)(2,1)} %collective-permute-done.7.refs_3_), channel_id=1, source_target_pairs={{0,1},{1,0},{2,3},{3,2},{4,5},{5,4},{6,7},{7,6},{8,9},{9,8},{10,11... | collective-permute-start | bytes 2752520 | tf_op jit(solution)/shard_map/ppermute | solution.py:31
  78.6 21.3 %collective-permute-start.12 = (bf16[896,512]{1,0:T(8,128)(2,1)}, bf16[896,512]{1,0:T(8,128)(2,1)}, u32[]{:S(2)}, u32[]{:S(2)}) collective-permute-start(bf16[896,512]{1,0:T(8,128)(2,1)} %collective-permute-done.9.refs_4_), channel_id=1, source_target_pairs={{0,1},{1,0},{2,3},{3,2},{4,5},{5,4},{6,7},{7,6},{8,9},{9,8},{10,11... | collective-permute-start | bytes 2752520 | tf_op jit(solution)/shard_map/ppermute | solution.py:31
  80.6 19.3 %collective-permute-start.11 = (bf16[96,3584]{1,0:T(8,128)(2,1)}, bf16[96,3584]{1,0:T(8,128)(2,1)}, u32[]{:S(2)}, u32[]{:S(2)}) collective-permute-start(bf16[96,3584]{1,0:T(8,128)(2,1)} %slice.46), channel_id=1, source_target_pairs={{0,128},{64,192},{128,0},{192,64},{1,129},{65,193},{129,1},{193,65... | collective-permute-start | bytes 2064392 | tf_op jit(solution)/shard_map/ppermute | solution.py:27
  99.9 1.1 copy-start.5
  115.1 44.9 %collective-permute-start.14 = (bf16[2048,1792]{1,0:T(8,128)(2,1)}, bf16[2048,1792]{1,0:T(8,128)(2,1)}, u32[]{:S(2)}, u32[]{:S(2)}) collective-permute-start(bf16[2048,1792]{1,0:T(8,128)(2,1)} %bitcast.11.refs_1_.refs_4_), channel_id=1, source_target_pairs={{0,1},{1,0},{2,3},{3,2},{4,5},{5,4},{6,7},{7,6},{8,9},{9,8},{10,11... | collective-permute-start | bytes 22020104 | tf_op jit(solution)/shard_map/ppermute | solution.py:31
  150.8 5.7 %copy-start.3 = (f32[4,8,256]{2,1,0:T(8,128)}, f32[4,8,256]{2,1,0:T(8,128)S(1)}, u32[]{:S(2)}) copy-start(f32[4,8,256]{2,1,0:T(8,128)S(1)} %reduce_sum.38.stats) | copy-start | bytes 98308
  156.5 20.7 %collective-permute-start.16 = (bf16[2,192,1024]{2,1,0:T(8,128)(2,1)}, bf16[2,192,1024]{2,1,0:T(8,128)(2,1)S(1)}, u32[]{:S(2)}, u32[]{:S(2)}) collective-permute-start(bf16[2,192,1024]{2,1,0:T(8,128)(2,1)} %get-tuple-element.47), channel_id=1, source_target_pairs={{0,128},{64,192},{128,0},{192,64},{1,129},{65,193},{129,1},{193,65... | collective-permute-start | bytes 2359304 | tf_op jit(solution)/shard_map/ppermute | solution.py:27
  158.0 32.5 %collective-permute-start.13 = (bf16[2,192,1024]{2,1,0:T(8,128)(2,1)}, bf16[2,192,1024]{2,1,0:T(8,128)(2,1)}, u32[]{:S(2)}, u32[]{:S(2)}) collective-permute-start(bf16[2,192,1024]{2,1,0:T(8,128)(2,1)} %get-tuple-element.45.refs_0_), channel_id=1, source_target_pairs={{0,64},{64,0},{128,192},{192,128},{1,65},{65,1},{129,193},{193,129... | collective-permute-start | bytes 2359304 | tf_op jit(solution)/shard_map/ppermute | solution.py:27
  158.9 33.0 %collective-permute-start.15 = (bf16[2,192,1024]{2,1,0:T(8,128)(2,1)}, bf16[2,192,1024]{2,1,0:T(8,128)(2,1)}, u32[]{:S(2)}, u32[]{:S(2)}) collective-permute-start(bf16[2,192,1024]{2,1,0:T(8,128)(2,1)} %get-tuple-element.47), channel_id=1, source_target_pairs={{0,192},{64,128},{128,64},{192,0},{1,193},{65,129},{129,65},{193,1... | collective-permute-start | bytes 2359304 | tf_op jit(solution)/shard_map/ppermute | solution.py:27
  166.6 1.5 copy-start.2
  184.1 1.5 copy-start.1
  201.8 8.7 %collective-permute-start.18 = (bf16[2,48,1792]{2,1,0:T(8,128)(2,1)}, bf16[2,48,1792]{2,1,0:T(8,128)(2,1)}, u32[]{:S(2)}, u32[]{:S(2)}) collective-permute-start(bf16[2,48,1792]{2,1,0:T(8,128)(2,1)} %get-tuple-element.52), channel_id=1, source_target_pairs={{0,16},{16,0},{32,48},{48,32},{1,17},{17,1},{33,49},{49,33},{2,18}... | collective-permute-start | bytes 1032200 | tf_op jit(solution)/shard_map/ppermute | solution.py:31
  202.4 12.7 %collective-permute-start.19 = (bf16[2,48,1792]{2,1,0:T(8,128)(2,1)}, bf16[2,48,1792]{2,1,0:T(8,128)(2,1)}, u32[]{:S(2)}, u32[]{:S(2)}) collective-permute-start(bf16[2,48,1792]{2,1,0:T(8,128)(2,1)} %get-tuple-element.53), channel_id=1, source_target_pairs={{0,32},{16,48},{32,0},{48,16},{1,33},{17,49},{33,1},{49,17},{2,34}... | collective-permute-start | bytes 1032200 | tf_op jit(solution)/shard_map/ppermute | solution.py:31
  204.6 13.0 %collective-permute-start.20 = (bf16[2,48,1792]{2,1,0:T(8,128)(2,1)}, bf16[2,48,1792]{2,1,0:T(8,128)(2,1)}, u32[]{:S(2)}, u32[]{:S(2)}) collective-permute-start(bf16[2,48,1792]{2,1,0:T(8,128)(2,1)} %get-tuple-element.54), channel_id=1, source_target_pairs={{0,48},{16,32},{32,16},{48,0},{1,49},{17,33},{33,17},{49,1},{2,50}... | collective-permute-start | bytes 1032200 | tf_op jit(solution)/shard_map/ppermute | solution.py:31
  207.3 1.2 collective-permute-start.17
Sparse Core Ops, SparseCore 0:
  26.6 43.6 all-gather.2

commit v5 on v4

--- a/solution.py
+++ b/solution.py
@@ -16,8 +16,9 @@
 ROWS = 192
 QUARTER = 512
 HALF_D = 1792
-CHUNKS = (896, 896)
+CHUNKS = (1344, 448)
 TILE = 256
+WIDE = 896
 VMEM = 50 * 1024 * 1024
 F32, BF16 = jnp.float32, jnp.bfloat16
 
@@ -35,7 +36,7 @@
     return pl.BlockSpec(shape, lambda s, at: (0,) * len(shape))
 
 
-def logits_kernel(at, own, nbr_a, nbr_b, *refs):
+def logits_kernel(at, own, nbr, *refs):
     far, head, mate, got, tgt = refs[0], refs[1], refs[2], refs[3:7], refs[7]
     logits, stats, rows, raw, sums = refs[8:]
     step = pl.program_id(0)
@@ -48,8 +49,7 @@
             begin = pl.multiple_of(half * HALF_D, 128)
             to = pl.ds(side * HALF_D, HALF_D)
             rows[0:ROWS, to] = own[:, pl.ds(begin, HALF_D)]
-            rows[ROWS : ROWS + 96, to] = nbr_a[:, pl.ds(begin, HALF_D)]
-            rows[ROWS + 96 : 2 * ROWS, to] = nbr_b[:, pl.ds(begin, HALF_D)]
+            rows[ROWS : 2 * ROWS, to] = nbr[:, pl.ds(begin, HALF_D)]
         for k in range(4):
             d = y ^ k
             column = pl.multiple_of((d // 2 ^ tok) * HALF_D + d % 2 * 896, 128)
@@ -98,12 +98,14 @@
     @pl.when(step == 3)
     def _():
         lane = lax.broadcasted_iota(jnp.int32, (ROWS, 128), 1)
+        stats[...] = jnp.zeros_like(stats)
         for j in range(4):
             wide = jnp.zeros((ROWS, 128), F32)
             for s in range(4):
-                wide = jnp.where(lane == s, jnp.sum(sums[s, j], axis=1, keepdims=True), wide)
+                at_lane = (at[1] ^ j) % 2 * 4 + s
+                wide = jnp.where(lane == at_lane, jnp.sum(sums[s, j], axis=1, keepdims=True), wide)
             wide = jnp.concatenate([wide, jnp.zeros((256 - ROWS, 128), F32)], axis=0)
-            stats[at[1] ^ j] = wide.T[:8]
+            stats[(at[1] ^ j) // 2] += wide.T[:8]
 
 
 def logits_call(at, own, nbr, far, head, mate, got, tgt):
@@ -113,15 +115,14 @@
         grid_spec=pltpu.PrefetchScalarGridSpec(
             num_scalar_prefetch=1,
             grid=(4,),
-            in_specs=[whole(ROWS, 2 * HALF_D)]
-            + [whole(ROWS // 2, 2 * HALF_D)] * 2
+            in_specs=[whole(ROWS, 2 * HALF_D)] * 2
             + [whole(8, 4, 48, 896)]
             + [weights, pl.BlockSpec((HALF_D, TILE), lambda s, at: (0, s // 2))]
             + [pl.BlockSpec((c, TILE), lambda s, at: (0, s // 2)) for c in CHUNKS] * 2
             + [whole(2, ROWS, 128)],
             out_specs=[
                 pl.BlockSpec((4, ROWS, TILE), lambda s, at: (0, 0, s % 2 * 2 + s // 2)),
-                whole(4, 8, 256),
+                whole(2, 8, 256),
             ],
             scratch_shapes=[
                 pltpu.VMEM((4 * ROWS, 2 * HALF_D), BF16),
@@ -131,14 +132,14 @@
         ),
         out_shape=[
             jax.ShapeDtypeStruct((4, ROWS, 4 * TILE), F32),
-            jax.ShapeDtypeStruct((4, 8, 256), F32),
+            jax.ShapeDtypeStruct((2, 8, 256), F32),
         ],
         compiler_params=pltpu.CompilerParams(vmem_limit_bytes=VMEM),
         cost_estimate=pl.CostEstimate(
             flops=4 * ROWS * 4 * TILE * 2 * HALF_D * 2, bytes_accessed=16 << 20, transcendentals=1 << 21
         ),
         name="logits",
-    )(at, own, *nbr, far, head, mate, *got, tgt)
+    )(at, own, nbr, far, head, mate, *got, tgt)
 
 
 def grad_kernel(at, logits, stats, tgt, mask, mine, theirs, scales):
@@ -147,10 +148,12 @@
     @pl.when(step == 0)
     def _():
         for j in range(4):
-            total = stats[at[1] ^ j].T
+            block = at[1] ^ j
+            total = stats[block // 2].T[:ROWS]
+            total = jnp.where(block % 2 == 0, total[:, 0:2], total[:, 4:6])
             weight = loss_scale * mask[j // 2]
-            scales[0, j] = (1.0 + kl_weight) * weight / total[:ROWS, 0:1]
-            scales[1, j] = kl_weight * weight / total[:ROWS, 1:2]
+            scales[0, j] = (1.0 + kl_weight) * weight / total[:, 0:1]
+            scales[1, j] = kl_weight * weight / total[:, 1:2]
 
     core, part = step // 2, step % 2
     column = lax.broadcasted_iota(jnp.int32, (48, TILE), 1)
@@ -184,7 +187,7 @@
             grid=(4,),
             in_specs=[
                 pl.BlockSpec((4, ROWS, TILE), lambda s, at: (0, 0, s)),
-                whole(4, 8, 256),
+                whole(2, 8, 256),
                 whole(2, ROWS, 128),
                 whole(2, ROWS, 128),
             ],
@@ -192,7 +195,7 @@
             scratch_shapes=[pltpu.VMEM((2, 4, ROWS, 128), F32)],
         ),
         out_shape=[jax.ShapeDtypeStruct((2, ROWS, 4 * TILE), BF16)] * 2,
-        compiler_params=pltpu.CompilerParams(vmem_limit_bytes=VMEM),
+        compiler_params=pltpu.CompilerParams(vmem_limit_bytes=VMEM // 3),
         name="logit_grad",
     )(at, logits, stats, tgt, mask)
 
@@ -226,10 +229,10 @@
 
 
 def terms_call(at, grads, head, mate, ks, acc=None, last=False):
-    tile = pl.BlockSpec((2 * ROWS, TILE), lambda s, at: (0, s))
+    tile = pl.BlockSpec((2 * ROWS, WIDE), lambda s, at: (0, s))
     in_specs, args = [], []
     for k, grad in zip(ks, grads):
-        weights = pl.BlockSpec((QUARTER, TILE), lambda s, at, k=k: (at[1] ^ k, s))
+        weights = pl.BlockSpec((QUARTER, WIDE), lambda s, at, k=k: (at[1] ^ k, s))
         in_specs += [pl.BlockSpec((2, ROWS, 4 * TILE), lambda s, at: (0, 0, 0)), weights, weights]
         args += [grad, head, mate]
     out_specs, scratch = tile, []
@@ -238,20 +241,20 @@
         in_specs.append(tile)
         args.append(acc)
     if last:
-        out_specs = [pl.BlockSpec((2, 48, TILE), lambda s, at: (0, 0, s))] * 4
+        out_specs = [pl.BlockSpec((2, 48, WIDE), lambda s, at: (0, 0, s))] * 4
         out_shape = [jax.ShapeDtypeStruct((2, 48, HALF_D), t) for t in (F32, BF16, BF16, BF16)]
-        scratch = [pltpu.VMEM((4, 2, 48, TILE), F32)]
+        scratch = [pltpu.VMEM((4, 2, 48, WIDE), F32)]
     return pl.pallas_call(
         functools.partial(terms_kernel, ks=ks, add=acc is not None, last=last),
         grid_spec=pltpu.PrefetchScalarGridSpec(
             num_scalar_prefetch=1,
-            grid=(HALF_D // TILE,),
+            grid=(HALF_D // WIDE,),
             in_specs=in_specs,
             out_specs=out_specs,
             scratch_shapes=scratch,
         ),
         out_shape=out_shape,
-        compiler_params=pltpu.CompilerParams(vmem_limit_bytes=VMEM),
+        compiler_params=pltpu.CompilerParams(vmem_limit_bytes=VMEM * 3 // 5),
         cost_estimate=pl.CostEstimate(
             flops=2 * 2 * ROWS * HALF_D * 2 * QUARTER * len(ks),
             bytes_accessed=(6 << 20) * len(ks),
@@ -285,7 +288,7 @@
             out_specs=pl.BlockSpec((16, 8, 896), lambda s, at: (0, 0, s)),
         ),
         out_shape=jax.ShapeDtypeStruct((16, 8, HALF_D), BF16),
-        compiler_params=pltpu.CompilerParams(vmem_limit_bytes=VMEM),
+        compiler_params=pltpu.CompilerParams(vmem_limit_bytes=VMEM // 3),
         name="rows",
     )(at, *parts)
 
@@ -311,38 +314,38 @@
 
     sync = lax.optimization_barrier
 
+    scal = jnp.stack([targets, loss_mask]).reshape(2, 32, 2, 6)
+    scal = lax.dynamic_index_in_dim(scal, core, 2, keepdims=False).reshape(2, ROWS)
     slab = pick_rows(lax.dynamic_slice(states, (z * 48, y * 896), (48, 896)), 24, core)
     piece = jnp.concatenate([line_xor(slab, 2), line_xor(slab, 3)], axis=0)[None]
+    far_scal = line_xor(scal, 2)
+    sent = [
+        lax.dynamic_slice(head, (n * CHUNKS[0], (3 - x) * QUARTER), (CHUNKS[n], QUARTER))
+        for n in range(2)
+    ]
+    piece, far_scal, sent[0] = sync((piece, far_scal, sent[0]))
+    got = [line_xor(sent[0], 3)]
     piece = jnp.concatenate([piece] + [axis_xor(piece, "y", k) for k in (1, 2, 3)])
-    piece, head, states = sync((piece, head, states))
+    own = pick_rows(states, ROWS, core)
+    piece, own = sync((piece, own))
     far = lax.all_gather(piece[None], "z", axis=0, tiled=True)
-
-    got = []
-    for n in range(2):
-        sent = lax.dynamic_slice(head, (n * 896, (3 - x) * QUARTER), (896, QUARTER))
-        got.append(line_xor(sent, 3))
-    own = pick_rows(states, ROWS, core)
-    nbr = [line_xor(own[:96], 1)]
+    nbr = line_xor(own, 1)
     mate = axis_xor(lax.dynamic_slice(head, (0, x * QUARTER), (HALF_D, QUARTER)), "core", 1)
 
     voc = (y * 8 + z) * 2
     begin = [(voc + c) * 2048 + x * QUARTER for c in (core, 1 - core)]
     at = jnp.stack([tok, x, y, z, begin[0], begin[1]]).astype(jnp.int32)
-    scal = jnp.stack([targets, loss_mask]).reshape(2, 32, 2, 6)
-    scal = lax.dynamic_index_in_dim(scal, core, 2, keepdims=False).reshape(2, ROWS)
-    scal = jnp.stack([scal, line_xor(scal, 2)], axis=1)
+    scal = jnp.stack([scal, far_scal], axis=1)
     mask = scal[1].astype(F32)
     tgt_wide = jnp.broadcast_to(scal[0][..., None], (2, ROWS, 128))
     mask_wide = jnp.broadcast_to(mask[..., None], (2, ROWS, 128))
 
-    head, tgt_wide, mask_wide, mate, got[0], nbr[0], own = sync(
-        (head, tgt_wide, mask_wide, mate, got[0], nbr[0], own)
-    )
-    nbr.append(line_xor(own[96:], 1))
-    got_mate = [axis_xor(got[0], "core", 1)]
     head_t = head.T
-    head_t, got[1], got_mate[0] = sync((head_t, got[1], got_mate[0]))
-    got_mate.append(axis_xor(got[1], "core", 1))
+    head_t, tgt_wide, mask_wide, mate, got[0], nbr, sent[1] = sync(
+        (head_t, tgt_wide, mask_wide, mate, got[0], nbr, sent[1])
+    )
+    got.append(line_xor(sent[1], 3))
+    got_mate = [axis_xor(g, "core", 1) for g in got]
     got = got + got_mate
 
     logits, stats = logits_call(at, own, nbr, far, head, mate, got, tgt_wide)
@@ -357,7 +360,7 @@
     parts = list(terms_call(at, grads[2:], head_t, mate_t, (2, 3), terms, last=True))
 
     stats, parts[0] = sync((stats, parts[0]))
-    stats = lax.dynamic_index_in_dim(stats, x, 0, keepdims=False)
+    stats = lax.dynamic_index_in_dim(stats.reshape(4, 4, 256), x, 0, keepdims=False)
     own_total, partner_total, picked, cross = (stats[s, :ROWS] for s in range(4))
     own_lse, partner_lse = jnp.log(own_total), jnp.log(partner_total)
     loss = mask[0] * (

time: 245 us -> 224 us (0.914)
  waiting for transfers between devices: 74.3 us -> 64.9 us
  Pallas kernels: 45.3 us -> 36.2 us
    optimization_barrier x1 -> x0, local copies, waits for them, and re-layouts: 10.1 us -> none  [shards(): sync((head, tgt_wide, mask_wide, mate, got[0], nbr[0], own))]
    unnamed x20 -> x23, local copies, waits for them, and re-layouts: 7.82 us -> 17.5 us
    ppermute x10 -> x9, waiting for transfers between devices: 59.8 us -> 50.8 us  [line_xor(): return lax.ppermute(block, LINE, [(x, x ^ k) for x in range(N_X)])]
    pallas_call x3, Pallas kernels: 23.4 us -> 15.5 us  [terms_call(): pl.pallas_call(functools.partial(terms_kernel, ks=ks, add=acc is not None...]
    slice x2 -> x0, local copies, waits for them, and re-layouts: 2.9 us -> none  [the longest x1 1.99 us: shards(): nbr.append(line_xor(own[96:], 1))]
    ppermute x10 -> x9, starting transfers between devices: 15.6 us -> 13.5 us  [line_xor(): return lax.ppermute(block, LINE, [(x, x ^ k) for x in range(N_X)])]
  transfers between devices with their start and end apart: 22 -> 21, of which waited for: 15 -> 14; matrix products, arithmetic and copies ran while one was open for 9% -> 11% of each run, Pallas kernels for 8% -> 6%
where the time goes in v5:
time: 224 us; the launch traced here: 223 us
  waiting for transfers between devices  64.9 us (29%)
  blocking collectives  51.7 us (23%)
  Pallas kernels  36.2 us (16%)
  local copies, waits for them, and re-layouts  28.8 us (13%)
  starting transfers between devices  23.2 us (10%)
  between operations  14.4 us (6%)
  matrix products  2.39 us (1%)
    ppermute x9, waiting for transfers between devices, line_xor(): return lax.ppermute(block, LINE, [(x, x ^ k) for x in range(N_X)])  50.8 us
    all_to_all x3, blocking collectives, add_over_slice(): stats = jnp.sum(lax.all_to_all(spread, axis, 0, 0, tiled=True), axis=0)  34.8 us
    unnamed x23, local copies, waits for them, and re-layouts  17.5 us
    all_to_all x1, blocking collectives, shards(): low = lax.all_to_all(rows_call(at, parts), ('tok', 'z'), 0, 0, tiled=True)  16.9 us
    pallas_call x3, Pallas kernels, terms_call(): pl.pallas_call(functools.partial(terms_kernel, ks=ks, add=acc is not None...  15.5 us
    pallas_call x1, Pallas kernels, logits_call(): pl.pallas_call(logits_kernel, grid_spec=pltpu.PrefetchScalarGridSpec(num_...  14.1 us
    ppermute x11, waiting for transfers between devices, axis_xor(): lax.ppermute(block, axis, [(i, i ^ k) for i in range(lax.axis_size(axis))])  14.1 us
    ppermute x9, starting transfers between devices, line_xor(): return lax.ppermute(block, LINE, [(x, x ^ k) for x in range(N_X)])  13.5 us
  transfers between devices with their start and end apart: 21, of which 14 were waited for; matrix products, arithmetic and copies ran while one was open for 11% of the time, Pallas kernels for 6%

profile of v5, /device:TPU:2, one launch (start us, length us, event | category | flops | bytes accessed | tf_op | source)
XLA Modules:
  0.0 223.4 jit_solution(15589718634130910231)
XLA Ops:
  7.3 1.7 copy-done
  9.2 2.2 collective-permute-start
  11.4 1.6 collective-permute-start.1
  13.0 0.8 stack.52
  13.9 0.8 stack.53
  15.1 2.0 collective-permute-start.2
  17.1 2.5 %constant_dynamic-slice_fusion.1 = bf16[1344,512]{1,0:T(8,128)(2,1)} fusion(bf16[1792,2048]{1,0:T(8,128)(2,1)} %refs_1_.1, s32[]{:T(128)S(6)} %select_n.58), kind=kLoop, calls=%fused_computation.48 | loop fusion | bytes 2752516 | tf_op jit(solution)/shard_map/dynamic_slice | solution.py:323
  20.3 1.1 collective-permute-start.5
  21.3 2.9 %collective-permute-start.6 = (bf16[1,48,896]{2,1,0:T(8,128)(2,1)S(1)}, bf16[1,48,896]{2,1,0:T(8,128)(2,1)S(1)}, u32[]{:S(2)}, u32[]{:S(2)}) collective-permute-start(bf16[1,48,896]{2,1,0:T(8,128)(2,1)S(1)} %maximum_bitcast_fusion), channel_id=1, source_target_pairs={{0,32},{16,48},{32,0},{48,16},{1,33},{17,49},{33,1},{49,17},{2,34}... | collective-permute-start | bytes 258056 | tf_op jit(solution)/shard_map/ppermute | solution.py:32
  24.2 0.7 collective-permute-start.7
  25.0 2.2 convolution_convert_fusion.own
  27.7 2.2 collective-permute-done.7
  29.9 0.8 pad_maximum_fusion
  30.8 2.8 %constant_dynamic-slice_fusion = bf16[1792,512]{1,0:T(8,128)(2,1)} fusion(bf16[1792,2048]{1,0:T(8,128)(2,1)} %refs_1_.1, s32[]{:T(128)S(6)} %select_n.59), kind=kLoop, calls=%fused_computation.47 | loop fusion | bytes 3670020 | tf_op jit(solution)/shard_map/dynamic_slice | solution.py:333
  33.6 0.9 collective-permute-start.4
  34.5 2.6 %collective-permute-start.8 = (bf16[192,3584]{1,0:T(8,128)(2,1)}, bf16[192,3584]{1,0:T(8,128)(2,1)}, u32[]{:S(2)}, u32[]{:S(2)}) collective-permute-start(bf16[192,3584]{1,0:T(8,128)(2,1)} %convolution_convert_fusion.own), channel_id=1, source_target_pairs={{0,128},{64,192},{128,0},{192,64},{1,129},{65,193},{129,1},{193,65... | collective-permute-start | bytes 4128776 | tf_op jit(solution)/shard_map/ppermute | solution.py:28
  37.3 10.1 %copy.21 = bf16[1792,2048]{0,1:T(8,128)(2,1)} copy(bf16[1792,2048]{1,0:T(8,128)(2,1)} %refs_1_.1) | data formatting | bytes 14680064 | tf_op args[1]
  47.4 1.0 constant_dynamic-slice_fusion.2
  48.5 18.0 %collective-permute-done.4.refs_3_ = bf16[1344,512]{1,0:T(8,128)(2,1)} collective-permute-done((bf16[1344,512]{1,0:T(8,128)(2,1)}, bf16[1344,512]{1,0:T(8,128)(2,1)}, u32[]{:S(2)}, u32[]{:S(2)}) %collective-permute-start.4) | collective-permute-done | bytes 1376288 | tf_op jit(solution)/shard_map/ppermute | solution.py:28
  66.5 1.5 collective-permute-done.8.nbr
  69.0 12.4 %collective-permute-done.9.refs_4_ = bf16[448,512]{1,0:T(8,128)(2,1)} collective-permute-done((bf16[448,512]{1,0:T(8,128)(2,1)S(1)}, bf16[448,512]{1,0:T(8,128)(2,1)}, u32[]{:S(2)}, u32[]{:S(2)}) %collective-permute-start.9) | collective-permute-done | bytes 458784 | tf_op jit(solution)/shard_map/ppermute | solution.py:28
  81.5 2.1 collective-permute-done.11.refs_6_
  83.6 14.1 %logits.1 = (f32[4,192,1024]{2,1,0:T(8,128)}, f32[2,8,256]{2,1,0:T(8,128)S(1)}) custom-call(s32[6]{0:T(128)S(1)} %stack.51.at, bf16[192,3584]{1,0:T(8,128)(2,1)} %convolution_convert_fusion.own, bf16[192,3584]{1,0:T(8,128)(2,1)} %collective-permute-done.8.nbr, bf16[8,4,48,896]{3,2,1,0:T(8,128)(2,1)} %bitcast.53, bf16[1792,2048]{1,0:T(8,128)(2,1)} %refs_1_.1, ...), custom_call_target="tpu_custom_call" | custom-call | flops 5637144576 | bytes 16777216 | tf_op jit(solution)/shard_map/logits/pallas_call | solution.py:113
  97.9 9.5 %all_to_all.20 = f32[4,2,8,256]{3,2,1,0:T(8,128)S(1)} all-to-all(f32[4,2,8,256]{3,2,1,0:T(8,128)S(1)} %broadcast_in_dim.21), channel_id=1, replica_groups=mesh['rep'=2,'tok'=2,'y'=4,'z'=8,'core'=2] {'rep','tok'}, dimensions={0} | all-to-all | bytes 131072 | tf_op jit(solution)/shard_map/all_to_all | solution.py:299
  107.4 8.0 %all_to_all.21 = f32[4,2,8,256]{3,2,1,0:T(8,128)S(1)} all-to-all(f32[4,2,8,256]{3,2,1,0:T(8,128)S(1)} %broadcast_in_dim.44), channel_id=1, replica_groups=mesh['rep'=2,'tok'=2,'y'=4,'z'=8,'core'=2] {'y'}, dimensions={0} | all-to-all | bytes 131072 | tf_op jit(solution)/shard_map/all_to_all | solution.py:299
  115.4 17.3 %all_to_all.22 = f32[8,2,8,256]{3,2,1,0:T(8,128)S(1)} all-to-all(f32[8,2,8,256]{3,2,1,0:T(8,128)S(1)} %broadcast_in_dim.45), channel_id=1, replica_groups=mesh['rep'=2,'tok'=2,'y'=4,'z'=8,'core'=2] {'z'}, dimensions={0} | all-to-all | bytes 262144 | tf_op jit(solution)/shard_map/all_to_all | solution.py:299
  132.8 1.9 copy-done.2
  134.7 4.3 %logit_grad.1 = (bf16[2,192,1024]{2,1,0:T(8,128)(2,1)}, bf16[2,192,1024]{2,1,0:T(8,128)(2,1)}) custom-call(s32[6]{0:T(128)S(1)} %stack.51.at, f32[4,192,1024]{2,1,0:T(8,128)S(1)} %copy-done.2, f32[2,8,256]{2,1,0:T(8,128)S(1)} %reduce_sum.38.stats, s32[2,192,128]{2,1,0:T(8,128)S(1)} %broadcast_in_dim.18.refs_7_.tgt, f32[2,192,128]{2,1,0:T(8,128)S(1)} %broadcast_in_dim.19.mask), custom_call_target="tpu_custom_call" | custom-call | tf_op jit(solution)/shard_map/logit_grad/pallas_call | solution.py:183
  139.0 1.5 collective-permute-start.15
  140.5 0.7 collective-permute-start.12
  141.2 1.3 collective-permute-start.14
  142.5 1.2 slice.47
  143.7 3.1 %copy-done.1 = bf16[1792,2048]{0,1:T(8,128)(2,1)S(1)} copy-done((bf16[1792,2048]{0,1:T(8,128)(2,1)S(1)}, bf16[1792,2048]{0,1:T(8,128)(2,1)}, u32[]{:S(2)}) %copy-start.1) | copy-done | bytes 7340056
  147.5 4.2 %gradient_terms.3.refs_3_ = f32[384,1792]{1,0:T(8,128)S(1)} custom-call(s32[6]{0:T(128)S(1)} %copy-done.4, bf16[2,192,1024]{2,1,0:T(8,128)(2,1)} %get-tuple-element.43.refs_0_, bf16[2048,1792]{1,0:T(8,128)(2,1)S(1)} %bitcast.44, bf16[2048,1792]{1,0:T(8,128)(2,1)} %collective-permute-done.13.refs_2_.refs_5_), custom_call_target="tpu_custom_call" | custom-call | flops 1409286144 | bytes 6291456 | tf_op jit(solution)/shard_map/gradient_terms/pallas_call | solution.py:247
  151.7 8.0 %collective-permute-done.15.refs_0_ = bf16[2,192,1024]{2,1,0:T(8,128)(2,1)S(1)} collective-permute-done((bf16[2,192,1024]{2,1,0:T(8,128)(2,1)}, bf16[2,192,1024]{2,1,0:T(8,128)(2,1)S(1)}, u32[]{:S(2)}, u32[]{:S(2)}) %collective-permute-start.15) | collective-permute-done | bytes 786464 | tf_op jit(solution)/shard_map/ppermute | solution.py:28
  159.7 4.0 %gradient_terms.4.refs_6_ = f32[384,1792]{1,0:T(8,128)S(1)} custom-call(s32[6]{0:T(128)S(1)} %copy-done.4, bf16[2,192,1024]{2,1,0:T(8,128)(2,1)S(1)} %collective-permute-done.15.refs_0_, bf16[2048,1792]{1,0:T(8,128)(2,1)S(1)} %bitcast.45, bf16[2048,1792]{1,0:T(8,128)(2,1)} %collective-permute-done.13.refs_2_.refs_5_, f32[384,1792]{1,0:T(8,128)S(1)} %gradient_terms.3.refs_3_), custom_call_target="tpu_custom_call" | custom-call | flops 1409286144 | bytes 6291456 | tf_op jit(solution)/shard_map/gradient_terms/pallas_call | solution.py:247
  163.7 8.9 %collective-permute-done.12.refs_0_ = bf16[2,192,1024]{2,1,0:T(8,128)(2,1)} collective-permute-done((bf16[2,192,1024]{2,1,0:T(8,128)(2,1)}, bf16[2,192,1024]{2,1,0:T(8,128)(2,1)}, u32[]{:S(2)}, u32[]{:S(2)}) %collective-permute-start.12) | collective-permute-done | bytes 786464 | tf_op jit(solution)/shard_map/ppermute | solution.py:28
  172.6 1.4 collective-permute-done.14.refs_3_
  174.0 7.3 %gradient_terms.5 = (f32[2,48,1792]{2,1,0:T(8,128)S(1)}, bf16[2,48,1792]{2,1,0:T(8,128)(2,1)}, bf16[2,48,1792]{2,1,0:T(8,128)(2,1)}, bf16[2,48,1792]{2,1,0:T(8,128)(2,1)}) custom-call(s32[6]{0:T(128)S(1)} %copy-done.5, bf16[2,192,1024]{2,1,0:T(8,128)(2,1)} %collective-permute-done.12.refs_0_, bf16[2048,1792]{1,0:T(8,128)(2,1)S(1)} %bitcast.46, ...), custom_call_target="tpu_custom_call" | custom-call | flops 2818572288 | bytes 12582912 | tf_op jit(solution)/shard_map/gradient_terms/pallas_call | solution.py:247
  181.9 2.1 collective-permute-start.18
  184.0 2.1 collective-permute-start.19
  186.4 0.9 collective-permute-done.16
  187.7 0.7 reshape.75
  188.4 1.3 collective-permute-done.17.refs_1_
  189.7 4.4 %collective-permute-done.18.refs_2_ = bf16[2,48,1792]{2,1,0:T(8,128)(2,1)} collective-permute-done((bf16[2,48,1792]{2,1,0:T(8,128)(2,1)}, bf16[2,48,1792]{2,1,0:T(8,128)(2,1)}, u32[]{:S(2)}, u32[]{:S(2)}) %collective-permute-start.18) | collective-permute-done | bytes 344096 | tf_op jit(solution)/shard_map/ppermute | solution.py:32
  194.2 2.5 %collective-permute-done.19.refs_3_ = bf16[2,48,1792]{2,1,0:T(8,128)(2,1)} collective-permute-done((bf16[2,48,1792]{2,1,0:T(8,128)(2,1)}, bf16[2,48,1792]{2,1,0:T(8,128)(2,1)}, u32[]{:S(2)}, u32[]{:S(2)}) %collective-permute-start.19) | collective-permute-done | bytes 344096 | tf_op jit(solution)/shard_map/ppermute | solution.py:32
  196.7 2.2 %rows.1 = bf16[16,8,1792]{2,1,0:T(8,128)(2,1)S(1)} custom-call(s32[6]{0:T(128)S(1)} %copy-done.6, f32[2,48,1792]{2,1,0:T(8,128)S(1)} %get-tuple-element.49.refs_0_, bf16[2,48,1792]{2,1,0:T(8,128)(2,1)} %collective-permute-done.17.refs_1_, bf16[2,48,1792]{2,1,0:T(8,128)(2,1)} %collective-permute-done.18.refs_2_, ...), custom_call_target="tpu_custom_call" | custom-call | tf_op jit(solution)/shard_map/rows/pallas_call | solution.py:282
  199.0 16.9 %all_to_all.23 = bf16[16,8,1792]{2,1,0:T(8,128)(2,1)S(1)} all-to-all(bf16[16,8,1792]{2,1,0:T(8,128)(2,1)S(1)} %rows.1), channel_id=1, replica_groups=mesh['rep'=2,'tok'=2,'y'=4,'z'=8,'core'=2] {'tok','z'}, dimensions={0} | all-to-all | bytes 917504 | tf_op jit(solution)/shard_map/all_to_all | solution.py:375
  (76 shorter events, 5.9 us)
Async XLA Ops:
  7.2 1.8 copy-start
  7.2 76.4 %all-gather.3.cloned.1.call-start = ((), (), s32[]{:S(2)}) async-start(), calls=%async_computation.4 | async-start | bytes 3096576 | tf_op jit(solution)/shard_map/all_gather | solution.py:331
  9.2 10.5 %collective-permute-start = (bf16[24,896]{1,0:T(8,128)(2,1)S(1)}, bf16[24,896]{1,0:T(8,128)(2,1)S(1)}, u32[]{:S(2)}, u32[]{:S(2)}) collective-permute-start(bf16[24,896]{1,0:T(8,128)(2,1)S(1)} %convolution_convert_fusion.1), channel_id=1, source_target_pairs={{0,64},{64,0},{128,192},{192,128},{1,65},{65,1},{129,193},{193,129... | collective-permute-start | bytes 129032 | tf_op jit(solution)/shard_map/ppermute | solution.py:28
  11.4 8.3 %collective-permute-start.1 = (bf16[24,896]{1,0:T(8,128)(2,1)S(1)}, bf16[24,896]{1,0:T(8,128)(2,1)S(1)}, u32[]{:S(2)}, u32[]{:S(2)}) collective-permute-start(bf16[24,896]{1,0:T(8,128)(2,1)S(1)} %convolution_convert_fusion.1), channel_id=1, source_target_pairs={{0,192},{64,128},{128,64},{192,0},{1,193},{65,129},{129,65},{193,1... | collective-permute-start | bytes 129032 | tf_op jit(solution)/shard_map/ppermute | solution.py:28
  15.1 5.2 %collective-permute-start.2 = (s32[2,192]{1,0:T(2,128)S(1)}, s32[2,192]{1,0:T(2,128)S(1)}, u32[]{:S(2)}, u32[]{:S(2)}) collective-permute-start(s32[2,192]{1,0:T(2,128)S(1)} %reshape.73), channel_id=1, source_target_pairs={{0,64},{64,0},{128,192},{192,128},{1,65},{65,1},{129,193},{193,129... | collective-permute-start | bytes 4616 | tf_op jit(solution)/shard_map/ppermute | solution.py:28
  20.3 6.9 %collective-permute-start.5 = (bf16[1,48,896]{2,1,0:T(8,128)(2,1)S(1)}, bf16[1,48,896]{2,1,0:T(8,128)(2,1)S(1)}, u32[]{:S(2)}, u32[]{:S(2)}) collective-permute-start(bf16[1,48,896]{2,1,0:T(8,128)(2,1)S(1)} %maximum_bitcast_fusion), channel_id=1, source_target_pairs={{0,16},{16,0},{32,48},{48,32},{1,17},{17,1},{33,49},{49,33},{2,18}... | collective-permute-start | bytes 258056 | tf_op jit(solution)/shard_map/ppermute | solution.py:32
  21.3 6.4 %collective-permute-start.6 = (bf16[1,48,896]{2,1,0:T(8,128)(2,1)S(1)}, bf16[1,48,896]{2,1,0:T(8,128)(2,1)S(1)}, u32[]{:S(2)}, u32[]{:S(2)}) collective-permute-start(bf16[1,48,896]{2,1,0:T(8,128)(2,1)S(1)} %maximum_bitcast_fusion), channel_id=1, source_target_pairs={{0,32},{16,48},{32,0},{48,16},{1,33},{17,49},{33,1},{49,17},{2,34}... | collective-permute-start | bytes 258056 | tf_op jit(solution)/shard_map/ppermute | solution.py:32
  24.2 5.7 %collective-permute-start.7 = (bf16[1,48,896]{2,1,0:T(8,128)(2,1)S(1)}, bf16[1,48,896]{2,1,0:T(8,128)(2,1)S(1)}, u32[]{:S(2)}, u32[]{:S(2)}) collective-permute-start(bf16[1,48,896]{2,1,0:T(8,128)(2,1)S(1)} %maximum_bitcast_fusion), channel_id=1, source_target_pairs={{0,48},{16,32},{32,16},{48,0},{1,49},{17,33},{33,17},{49,1},{2,50}... | collective-permute-start | bytes 258056 | tf_op jit(solution)/shard_map/ppermute | solution.py:32
  33.6 34.5 %collective-permute-start.3 = (bf16[1792,512]{1,0:T(8,128)(2,1)}, bf16[1792,512]{1,0:T(8,128)(2,1)}, u32[]{:S(2)}, u32[]{:S(2)}) collective-permute-start(bf16[1792,512]{1,0:T(8,128)(2,1)} %constant_dynamic-slice_fusion), channel_id=1, source_target_pairs={{0,1},{1,0},{2,3},{3,2},{4,5},{5,4},{6,7},{7,6},{8,9},{9,8},{10,11... | collective-permute-start | bytes 5505032 | tf_op jit(solution)/shard_map/ppermute | solution.py:32
  33.6 32.9 %collective-permute-start.4 = (bf16[1344,512]{1,0:T(8,128)(2,1)}, bf16[1344,512]{1,0:T(8,128)(2,1)}, u32[]{:S(2)}, u32[]{:S(2)}) collective-permute-start(bf16[1344,512]{1,0:T(8,128)(2,1)} %constant_dynamic-slice_fusion.1), channel_id=1, source_target_pairs={{0,192},{64,128},{128,64},{192,0},{1,193},{65,129},{129,65},{193,1... | collective-permute-start | bytes 4128776 | tf_op jit(solution)/shard_map/ppermute | solution.py:28
  34.5 33.5 %collective-permute-start.8 = (bf16[192,3584]{1,0:T(8,128)(2,1)}, bf16[192,3584]{1,0:T(8,128)(2,1)}, u32[]{:S(2)}, u32[]{:S(2)}) collective-permute-start(bf16[192,3584]{1,0:T(8,128)(2,1)} %convolution_convert_fusion.own), channel_id=1, source_target_pairs={{0,128},{64,192},{128,0},{192,64},{1,129},{65,193},{129,1},{193,65... | collective-permute-start | bytes 4128776 | tf_op jit(solution)/shard_map/ppermute | solution.py:28
  48.5 33.0 %copy-start.7 = (f32[1,2,192]{2,0,1:T(1,128)}, f32[1,2,192]{2,0,1:T(1,128)S(1)}, u32[]{:S(2)}) copy-start(f32[1,2,192]{2,0,1:T(1,128)S(1)} %get-tuple-element.59) | copy-start | bytes 4612
  68.3 15.3 %collective-permute-start.10 = (bf16[1344,512]{1,0:T(8,128)(2,1)}, bf16[1344,512]{1,0:T(8,128)(2,1)}, u32[]{:S(2)}, u32[]{:S(2)}) collective-permute-start(bf16[1344,512]{1,0:T(8,128)(2,1)} %collective-permute-done.4.refs_3_), channel_id=1, source_target_pairs={{0,1},{1,0},{2,3},{3,2},{4,5},{5,4},{6,7},{7,6},{8,9},{9,8},{10,11... | collective-permute-start | bytes 4128776 | tf_op jit(solution)/shard_map/ppermute | solution.py:32
  68.4 13.0 %collective-permute-start.9 = (bf16[448,512]{1,0:T(8,128)(2,1)S(1)}, bf16[448,512]{1,0:T(8,128)(2,1)}, u32[]{:S(2)}, u32[]{:S(2)}) collective-permute-start(bf16[448,512]{1,0:T(8,128)(2,1)S(1)} %constant_dynamic-slice_fusion.2), channel_id=1, source_target_pairs={{0,192},{64,128},{128,64},{192,0},{1,193},{65,129},{129,65},{193,1... | collective-permute-start | bytes 1376264 | tf_op jit(solution)/shard_map/ppermute | solution.py:28
  81.5 2.2 collective-permute-start.11
  81.5 51.3 %copy-start.3 = (s32[6]{0:T(128)}, s32[6]{0:T(128)S(1)}, u32[]{:S(2)}) copy-start(s32[6]{0:T(128)S(1)} %stack.51.at) | copy-start | bytes 76
  97.8 46.0 %collective-permute-start.13 = (bf16[2048,1792]{1,0:T(8,128)(2,1)}, bf16[2048,1792]{1,0:T(8,128)(2,1)}, u32[]{:S(2)}, u32[]{:S(2)}) collective-permute-start(bf16[2048,1792]{1,0:T(8,128)(2,1)} %bitcast.43), channel_id=1, source_target_pairs={{0,1},{1,0},{2,3},{3,2},{4,5},{5,4},{6,7},{7,6},{8,9},{9,8},{10,11... | collective-permute-start | bytes 22020104 | tf_op jit(solution)/shard_map/ppermute | solution.py:32
  132.8 1.9 copy-start.2
  139.0 20.7 %collective-permute-start.15 = (bf16[2,192,1024]{2,1,0:T(8,128)(2,1)}, bf16[2,192,1024]{2,1,0:T(8,128)(2,1)S(1)}, u32[]{:S(2)}, u32[]{:S(2)}) collective-permute-start(bf16[2,192,1024]{2,1,0:T(8,128)(2,1)} %get-tuple-element.45), channel_id=1, source_target_pairs={{0,128},{64,192},{128,0},{192,64},{1,129},{65,193},{129,1},{193,65... | collective-permute-start | bytes 2359304 | tf_op jit(solution)/shard_map/ppermute | solution.py:28
  140.5 32.2 %collective-permute-start.12 = (bf16[2,192,1024]{2,1,0:T(8,128)(2,1)}, bf16[2,192,1024]{2,1,0:T(8,128)(2,1)}, u32[]{:S(2)}, u32[]{:S(2)}) collective-permute-start(bf16[2,192,1024]{2,1,0:T(8,128)(2,1)} %get-tuple-element.43.refs_0_), channel_id=1, source_target_pairs={{0,64},{64,0},{128,192},{192,128},{1,65},{65,1},{129,193},{193,129... | collective-permute-start | bytes 2359304 | tf_op jit(solution)/shard_map/ppermute | solution.py:28
  141.2 32.8 %collective-permute-start.14 = (bf16[2,192,1024]{2,1,0:T(8,128)(2,1)}, bf16[2,192,1024]{2,1,0:T(8,128)(2,1)}, u32[]{:S(2)}, u32[]{:S(2)}) collective-permute-start(bf16[2,192,1024]{2,1,0:T(8,128)(2,1)} %get-tuple-element.45), channel_id=1, source_target_pairs={{0,192},{64,128},{128,64},{192,0},{1,193},{65,129},{129,65},{193,1... | collective-permute-start | bytes 2359304 | tf_op jit(solution)/shard_map/ppermute | solution.py:28
  143.7 3.1 %copy-start.1 = (bf16[1792,2048]{0,1:T(8,128)(2,1)S(1)}, bf16[1792,2048]{0,1:T(8,128)(2,1)}, u32[]{:S(2)}) copy-start(bf16[1792,2048]{0,1:T(8,128)(2,1)} %copy.21) | copy-start | bytes 22020100
  146.8 0.7 copy-start.4
  151.7 22.3 %copy-start.5 = (s32[6]{0:T(128)S(1)}, s32[6]{0:T(128)}, u32[]{:S(2)}) copy-start(s32[6]{0:T(128)} %copy-done.3) | copy-start | bytes 76
  163.7 22.4 %copy-start.8 = (f32[1,2,192]{2,0,1:T(1,128)S(1)}, f32[1,2,192]{2,0,1:T(1,128)}, u32[]{:S(2)}) copy-start(f32[1,2,192]{2,0,1:T(1,128)} %copy-done.7) | copy-start | bytes 4612
  163.7 22.4 %copy-start.9 = (f32[1,1,192]{2,0,1:T(1,128)S(1)}, f32[1,1,192]{2,0,1:T(1,128)}, u32[]{:S(2)}) copy-start(f32[1,1,192]{2,0,1:T(1,128)} %slice.47) | copy-start | bytes 2308
  163.7 33.0 %copy-start.6 = (s32[6]{0:T(128)S(1)}, s32[6]{0:T(128)}, u32[]{:S(2)}) copy-start(s32[6]{0:T(128)} %copy-done.3) | copy-start | bytes 76
  181.3 8.4 %collective-permute-start.17 = (bf16[2,48,1792]{2,1,0:T(8,128)(2,1)}, bf16[2,48,1792]{2,1,0:T(8,128)(2,1)}, u32[]{:S(2)}, u32[]{:S(2)}) collective-permute-start(bf16[2,48,1792]{2,1,0:T(8,128)(2,1)} %get-tuple-element.50), channel_id=1, source_target_pairs={{0,16},{16,0},{32,48},{48,32},{1,17},{17,1},{33,49},{49,33},{2,18}... | collective-permute-start | bytes 1032200 | tf_op jit(solution)/shard_map/ppermute | solution.py:32
  181.9 12.3 %collective-permute-start.18 = (bf16[2,48,1792]{2,1,0:T(8,128)(2,1)}, bf16[2,48,1792]{2,1,0:T(8,128)(2,1)}, u32[]{:S(2)}, u32[]{:S(2)}) collective-permute-start(bf16[2,48,1792]{2,1,0:T(8,128)(2,1)} %get-tuple-element.51), channel_id=1, source_target_pairs={{0,32},{16,48},{32,0},{48,16},{1,33},{17,49},{33,1},{49,17},{2,34}... | collective-permute-start | bytes 1032200 | tf_op jit(solution)/shard_map/ppermute | solution.py:32
  184.0 12.7 %collective-permute-start.19 = (bf16[2,48,1792]{2,1,0:T(8,128)(2,1)}, bf16[2,48,1792]{2,1,0:T(8,128)(2,1)}, u32[]{:S(2)}, u32[]{:S(2)}) collective-permute-start(bf16[2,48,1792]{2,1,0:T(8,128)(2,1)} %get-tuple-element.52), channel_id=1, source_target_pairs={{0,48},{16,32},{32,16},{48,0},{1,49},{17,33},{33,17},{49,1},{2,50}... | collective-permute-start | bytes 1032200 | tf_op jit(solution)/shard_map/ppermute | solution.py:32
  186.1 1.2 collective-permute-start.16
Sparse Core Ops, SparseCore 0:
  30.9 43.4 all-gather.2

commit v6 on v5

--- a/solution.py
+++ b/solution.py
@@ -38,7 +38,7 @@
 
 def logits_kernel(at, own, nbr, *refs):
     far, head, mate, got, tgt = refs[0], refs[1], refs[2], refs[3:7], refs[7]
-    logits, stats, rows, raw, sums = refs[8:]
+    logits, stats, rows, raws, sums = refs[8], refs[9], refs[10], refs[11:13], refs[13]
     step = pl.program_id(0)
     tok, y = at[0], at[2]
 
@@ -58,9 +58,11 @@
 
     lane = lax.broadcasted_iota(jnp.int32, (48, TILE), 1)
 
-    def one(head, got, part, core):
+    def product(raw, head, got):
         weights = jnp.concatenate([head[...]] + [chunk[...] for chunk in got], axis=0)
         raw[...] = jnp.dot(rows[...], weights, preferred_element_type=F32)
+
+    def work(raw, part, core):
         column = lane + (at[4 + core] + part * TILE)
         for chunk in range(8):
             pair, g = chunk // 4, chunk % 4
@@ -89,13 +91,16 @@
                 for s, term in enumerate(terms):
                     sums[s, j, here] += term[:, :128] + term[:, 128:]
 
-    for part in range(2):
-        for core in range(2):
-            @pl.when(step == part * 2 + core)
-            def _(part=part, core=core):
-                one((head, mate)[core], got[core * 2 : core * 2 + 2], part, core)
-
-    @pl.when(step == 3)
+    for n in range(5):
+        @pl.when(step == n)
+        def _(n=n):
+            if n < 4:
+                core = n % 2
+                product(raws[n % 2], (head, mate)[core], got[core * 2 : core * 2 + 2])
+            if n > 0:
+                work(raws[(n - 1) % 2], (n - 1) // 2, (n - 1) % 2)
+
+    @pl.when(step == 4)
     def _():
         lane = lax.broadcasted_iota(jnp.int32, (ROWS, 128), 1)
         stats[...] = jnp.zeros_like(stats)
@@ -109,23 +114,35 @@
 
 
 def logits_call(at, own, nbr, far, head, mate, got, tgt):
-    weights = pl.BlockSpec((HALF_D, TILE), lambda s, at: (0, at[1] * 2 + s // 2))
+    def once(*shape):
+        return pl.BlockSpec(
+            shape, lambda s, at: (0,) * len(shape), pipeline_mode=pl.Buffered(1)
+        )
+
+    def part(s):
+        return jnp.minimum(s // 2, 1)
+
+    def tile(s, at):
+        done = jnp.maximum(s - 1, 0)
+        return (0, 0, done % 2 * 2 + done // 2)
+
     return pl.pallas_call(
         logits_kernel,
         grid_spec=pltpu.PrefetchScalarGridSpec(
             num_scalar_prefetch=1,
-            grid=(4,),
-            in_specs=[whole(ROWS, 2 * HALF_D)] * 2
-            + [whole(8, 4, 48, 896)]
-            + [weights, pl.BlockSpec((HALF_D, TILE), lambda s, at: (0, s // 2))]
-            + [pl.BlockSpec((c, TILE), lambda s, at: (0, s // 2)) for c in CHUNKS] * 2
+            grid=(5,),
+            in_specs=[once(ROWS, 2 * HALF_D)] * 2
+            + [once(8, 4, 48, 896)]
+            + [
+                pl.BlockSpec((HALF_D, TILE), lambda s, at: (0, at[1] * 2 + part(s))),
+                pl.BlockSpec((HALF_D, TILE), lambda s, at: (0, part(s))),
+            ]
+            + [pl.BlockSpec((c, TILE), lambda s, at: (0, part(s))) for c in CHUNKS] * 2
             + [whole(2, ROWS, 128)],
-            out_specs=[
-                pl.BlockSpec((4, ROWS, TILE), lambda s, at: (0, 0, s % 2 * 2 + s // 2)),
-                whole(2, 8, 256),
-            ],
+            out_specs=[pl.BlockSpec((4, ROWS, TILE), tile), whole(2, 8, 256)],
             scratch_shapes=[
                 pltpu.VMEM((4 * ROWS, 2 * HALF_D), BF16),
+                pltpu.VMEM((4 * ROWS, TILE), F32),
                 pltpu.VMEM((4 * ROWS, TILE), F32),
                 pltpu.VMEM((4, 4, ROWS, 128), F32),
             ],
@@ -195,7 +212,7 @@
             scratch_shapes=[pltpu.VMEM((2, 4, ROWS, 128), F32)],
         ),
         out_shape=[jax.ShapeDtypeStruct((2, ROWS, 4 * TILE), BF16)] * 2,
-        compiler_params=pltpu.CompilerParams(vmem_limit_bytes=VMEM // 3),
+        compiler_params=pltpu.CompilerParams(vmem_limit_bytes=VMEM),
         name="logit_grad",
     )(at, logits, stats, tgt, mask)
 
@@ -294,7 +311,7 @@
 
 
 def add_over_slice(stats):
-    for axis in (LINE, "y", "z"):
+    for axis in ((*LINE, "y"), "z"):
         spread = jnp.broadcast_to(stats[None], (lax.axis_size(axis), *stats.shape))
         stats = jnp.sum(lax.all_to_all(spread, axis, 0, 0, tiled=True), axis=0)
     return stats
@@ -323,14 +340,13 @@
         lax.dynamic_slice(head, (n * CHUNKS[0], (3 - x) * QUARTER), (CHUNKS[n], QUARTER))
         for n in range(2)
     ]
-    piece, far_scal, sent[0] = sync((piece, far_scal, sent[0]))
+    piece, far_scal, *sent = sync((piece, far_scal, *sent))
     got = [line_xor(sent[0], 3)]
     piece = jnp.concatenate([piece] + [axis_xor(piece, "y", k) for k in (1, 2, 3)])
     own = pick_rows(states, ROWS, core)
     piece, own = sync((piece, own))
     far = lax.all_gather(piece[None], "z", axis=0, tiled=True)
     nbr = line_xor(own, 1)
-    mate = axis_xor(lax.dynamic_slice(head, (0, x * QUARTER), (HALF_D, QUARTER)), "core", 1)
 
     voc = (y * 8 + z) * 2
     begin = [(voc + c) * 2048 + x * QUARTER for c in (core, 1 - core)]
@@ -341,10 +357,13 @@
     mask_wide = jnp.broadcast_to(mask[..., None], (2, ROWS, 128))
 
     head_t = head.T
-    head_t, tgt_wide, mask_wide, mate, got[0], nbr, sent[1] = sync(
-        (head_t, tgt_wide, mask_wide, mate, got[0], nbr, sent[1])
+    head_t, cut = sync((head_t, head))
+    cut = lax.dynamic_slice(cut, (0, x * QUARTER), (HALF_D, QUARTER))
+    head_t, tgt_wide, mask_wide, got[0], nbr, sent[1], cut = sync(
+        (head_t, tgt_wide, mask_wide, got[0], nbr, sent[1], cut)
     )
     got.append(line_xor(sent[1], 3))
+    mate = axis_xor(cut, "core", 1)
     got_mate = [axis_xor(g, "core", 1) for g in got]
     got = got + got_mate
 

time: 224 us -> 219 us (0.978)
  blocking collectives: 51.7 us -> 48 us
  waiting for transfers between devices: 64.9 us -> 62 us
    ppermute x9, waiting for transfers between devices: 50.8 us -> 46.6 us  [line_xor(): return lax.ppermute(block, LINE, [(x, x ^ k) for x in range(N_X)])]
    all_to_all x3 -> x2, blocking collectives: 34.8 us -> 30.6 us  [add_over_slice(): stats = jnp.sum(lax.all_to_all(spread, axis, 0, 0, tiled=True), axis=0)]
  transfers between devices with their start and end apart: 21 -> 21, of which waited for: 14 -> 13; matrix products, arithmetic and copies ran while one was open for 11% -> 11% of each run, Pallas kernels for 6% -> 6%
where the time goes in v6:
time: 219 us; the launch traced here: 218 us
  waiting for transfers between devices  62 us (28%)
  blocking collectives  48 us (22%)
  Pallas kernels  37.9 us (17%)
  local copies, waits for them, and re-layouts  28.9 us (13%)
  starting transfers between devices  22.9 us (10%)
  between operations  14.4 us (7%)
  matrix products  2.3 us (1%)
    ppermute x9, waiting for transfers between devices, line_xor(): return lax.ppermute(block, LINE, [(x, x ^ k) for x in range(N_X)])  46.6 us
    all_to_all x2, blocking collectives, add_over_slice(): stats = jnp.sum(lax.all_to_all(spread, axis, 0, 0, tiled=True), axis=0)  30.6 us
    all_to_all x1, blocking collectives, shards(): low = lax.all_to_all(rows_call(at, parts), ('tok', 'z'), 0, 0, tiled=True)  17.3 us
    unnamed x23, local copies, waits for them, and re-layouts  16.8 us
    pallas_call x3, Pallas kernels, terms_call(): pl.pallas_call(functools.partial(terms_kernel, ks=ks, add=acc is not None...  15.5 us
    ppermute x11, waiting for transfers between devices, axis_xor(): lax.ppermute(block, axis, [(i, i ^ k) for i in range(lax.axis_size(axis))])  15.3 us
    pallas_call x1, Pallas kernels, logits_call(): pl.pallas_call(logits_kernel, grid_spec=pltpu.PrefetchScalarGridSpec(num_...  14.2 us
    ppermute x9, starting transfers between devices, line_xor(): return lax.ppermute(block, LINE, [(x, x ^ k) for x in range(N_X)])  12.6 us
  transfers between devices with their start and end apart: 21, of which 13 were waited for; matrix products, arithmetic and copies ran while one was open for 11% of the time, Pallas kernels for 6%

profile of v6, /device:TPU:2, one launch (start us, length us, event | category | flops | bytes accessed | tf_op | source)
XLA Modules:
  0.0 218.0 jit_solution(5286093188323855400)
XLA Ops:
  7.3 1.7 copy-done
  9.2 2.2 %collective-permute-start = (bf16[24,896]{1,0:T(8,128)(2,1)S(1)}, bf16[24,896]{1,0:T(8,128)(2,1)S(1)}, u32[]{:S(2)}, u32[]{:S(2)}) collective-permute-start(bf16[24,896]{1,0:T(8,128)(2,1)S(1)} %convolution_convert_fusion.1), channel_id=1, source_target_pairs={{0,64},{64,0},{128,192},{192,128},{1,65},{65,1},{129,193},{193,129... | collective-permute-start | bytes 129032 | tf_op jit(solution)/shard_map/ppermute | solution.py:28
  11.4 1.6 collective-permute-start.1
  13.0 0.8 stack.52
  13.9 0.8 stack.53
  15.1 2.0 collective-permute-start.2
  17.1 2.5 %constant_dynamic-slice_fusion.1 = bf16[1344,512]{1,0:T(8,128)(2,1)} fusion(bf16[1792,2048]{1,0:T(8,128)(2,1)} %refs_1_.1, s32[]{:T(128)S(6)} %select_n.58), kind=kLoop, calls=%fused_computation.48 | loop fusion | bytes 2752516 | tf_op jit(solution)/shard_map/dynamic_slice | solution.py:340
  19.6 1.8 constant_dynamic-slice_fusion.2
  21.5 1.7 collective-permute-start.4
  23.2 2.9 %collective-permute-start.5 = (bf16[1,48,896]{2,1,0:T(8,128)(2,1)S(1)}, bf16[1,48,896]{2,1,0:T(8,128)(2,1)S(1)}, u32[]{:S(2)}, u32[]{:S(2)}) collective-permute-start(bf16[1,48,896]{2,1,0:T(8,128)(2,1)S(1)} %maximum_bitcast_fusion), channel_id=1, source_target_pairs={{0,32},{16,48},{32,0},{48,16},{1,33},{17,49},{33,1},{49,17},{2,34}... | collective-permute-start | bytes 258056 | tf_op jit(solution)/shard_map/ppermute | solution.py:32
  26.3 2.1 convolution_convert_fusion.own
  28.4 1.2 collective-permute-done.5
  29.6 2.2 %collective-permute-done.6 = bf16[1,48,896]{2,1,0:T(8,128)(2,1)S(1)} collective-permute-done((bf16[1,48,896]{2,1,0:T(8,128)(2,1)S(1)}, bf16[1,48,896]{2,1,0:T(8,128)(2,1)S(1)}, u32[]{:S(2)}, u32[]{:S(2)}) %collective-permute-start.6) | collective-permute-done | bytes 86048 | tf_op jit(solution)/shard_map/ppermute | solution.py:32
  31.8 0.8 pad_maximum_fusion
  32.6 0.6 collective-permute-start.3
  33.2 1.2 collective-permute-start.7
  34.5 10.0 %copy.21 = bf16[1792,2048]{0,1:T(8,128)(2,1)} copy(bf16[1792,2048]{1,0:T(8,128)(2,1)} %refs_1_.1) | data formatting | bytes 14680064 | tf_op args[1]
  44.5 2.8 %constant_dynamic-slice_fusion = bf16[1792,512]{1,0:T(8,128)(2,1)} fusion(bf16[1792,2048]{1,0:T(8,128)(2,1)} %refs_1_.1, s32[]{:T(128)S(6)} %select_n.61), kind=kLoop, calls=%fused_computation.47 | loop fusion | bytes 3670020 | tf_op jit(solution)/shard_map/dynamic_slice | solution.py:361
  47.4 15.8 %collective-permute-done.3.refs_3_ = bf16[1344,512]{1,0:T(8,128)(2,1)} collective-permute-done((bf16[1344,512]{1,0:T(8,128)(2,1)}, bf16[1344,512]{1,0:T(8,128)(2,1)}, u32[]{:S(2)}, u32[]{:S(2)}) %collective-permute-start.3) | collective-permute-done | bytes 1376288 | tf_op jit(solution)/shard_map/ppermute | solution.py:28
  64.4 1.5 collective-permute-start.9
  65.9 11.3 %collective-permute-done.9.refs_4_ = bf16[448,512]{1,0:T(8,128)(2,1)} collective-permute-done((bf16[448,512]{1,0:T(8,128)(2,1)}, bf16[448,512]{1,0:T(8,128)(2,1)}, u32[]{:S(2)}, u32[]{:S(2)}) %collective-permute-start.9) | collective-permute-done | bytes 458784 | tf_op jit(solution)/shard_map/ppermute | solution.py:28
  77.3 2.1 collective-permute-done.11.refs_6_
  79.4 1.3 copy-done.2
  80.7 14.2 %logits.1 = (f32[4,192,1024]{2,1,0:T(8,128)}, f32[2,8,256]{2,1,0:T(8,128)S(1)}) custom-call(s32[6]{0:T(128)S(1)} %stack.51.at, bf16[192,3584]{1,0:T(8,128)(2,1)S(1)} %copy-done.2, bf16[192,3584]{1,0:T(8,128)(2,1)} %collective-permute-done.7.nbr, bf16[8,4,48,896]{3,2,1,0:T(8,128)(2,1)} %bitcast.53, bf16[1792,2048]{1,0:T(8,128)(2,1)} %refs_1_.1, ...), custom_call_target="tpu_custom_call" | custom-call | flops 5637144576 | bytes 16777216 | tf_op jit(solution)/shard_map/logits/pallas_call | solution.py:129
  95.1 13.3 %all_to_all.15 = f32[16,2,8,256]{3,2,1,0:T(8,128)S(1)} all-to-all(f32[16,2,8,256]{3,2,1,0:T(8,128)S(1)} %broadcast_in_dim.37), channel_id=1, replica_groups=mesh['rep'=2,'tok'=2,'y'=4,'z'=8,'core'=2] {'rep','tok','y'}, dimensions={0} | all-to-all | bytes 524288 | tf_op jit(solution)/shard_map/all_to_all | solution.py:316
  108.4 17.3 %all_to_all.16 = f32[8,2,8,256]{3,2,1,0:T(8,128)S(1)} all-to-all(f32[8,2,8,256]{3,2,1,0:T(8,128)S(1)} %broadcast_in_dim.38), channel_id=1, replica_groups=mesh['rep'=2,'tok'=2,'y'=4,'z'=8,'core'=2] {'z'}, dimensions={0} | all-to-all | bytes 262144 | tf_op jit(solution)/shard_map/all_to_all | solution.py:316
  125.8 6.0 %logit_grad.1 = (bf16[2,192,1024]{2,1,0:T(8,128)(2,1)}, bf16[2,192,1024]{2,1,0:T(8,128)(2,1)}) custom-call(s32[6]{0:T(128)S(1)} %stack.51.at, f32[4,192,1024]{2,1,0:T(8,128)} %get-tuple-element.47.logits, f32[2,8,256]{2,1,0:T(8,128)S(1)} %reduce_sum.28.stats, s32[2,192,128]{2,1,0:T(8,128)S(1)} %broadcast_in_dim.16.refs_7_.tgt, ...), custom_call_target="tpu_custom_call" | custom-call | tf_op jit(solution)/shard_map/logit_grad/pallas_call | solution.py:200
  131.7 1.5 collective-permute-start.15
  133.7 1.6 collective-permute-start.14
  135.2 1.2 slice.47
  136.5 3.1 %copy-done.1 = bf16[1792,2048]{0,1:T(8,128)(2,1)S(1)} copy-done((bf16[1792,2048]{0,1:T(8,128)(2,1)S(1)}, bf16[1792,2048]{0,1:T(8,128)(2,1)}, u32[]{:S(2)}) %copy-start.1) | copy-done | bytes 7340056
  139.6 0.6 copy-done.4
  140.2 4.2 %gradient_terms.3.refs_3_ = f32[384,1792]{1,0:T(8,128)S(1)} custom-call(s32[6]{0:T(128)S(1)} %copy-done.4, bf16[2,192,1024]{2,1,0:T(8,128)(2,1)} %get-tuple-element.49.refs_0_, bf16[2048,1792]{1,0:T(8,128)(2,1)S(1)} %bitcast.44, bf16[2048,1792]{1,0:T(8,128)(2,1)} %collective-permute-done.13.refs_2_.refs_5_), custom_call_target="tpu_custom_call" | custom-call | flops 1409286144 | bytes 6291456 | tf_op jit(solution)/shard_map/gradient_terms/pallas_call | solution.py:264
  144.4 8.0 %collective-permute-done.15.refs_0_ = bf16[2,192,1024]{2,1,0:T(8,128)(2,1)S(1)} collective-permute-done((bf16[2,192,1024]{2,1,0:T(8,128)(2,1)}, bf16[2,192,1024]{2,1,0:T(8,128)(2,1)S(1)}, u32[]{:S(2)}, u32[]{:S(2)}) %collective-permute-start.15) | collective-permute-done | bytes 786464 | tf_op jit(solution)/shard_map/ppermute | solution.py:28
  152.4 4.0 %gradient_terms.4.refs_6_ = f32[384,1792]{1,0:T(8,128)S(1)} custom-call(s32[6]{0:T(128)S(1)} %copy-done.5, bf16[2,192,1024]{2,1,0:T(8,128)(2,1)S(1)} %collective-permute-done.15.refs_0_, bf16[2048,1792]{1,0:T(8,128)(2,1)S(1)} %bitcast.45, bf16[2048,1792]{1,0:T(8,128)(2,1)} %collective-permute-done.13.refs_2_.refs_5_, f32[384,1792]{1,0:T(8,128)S(1)} %gradient_terms.3.refs_3_), custom_call_target="tpu_custom_call" | custom-call | flops 1409286144 | bytes 6291456 | tf_op jit(solution)/shard_map/gradient_terms/pallas_call | solution.py:264
  156.5 9.8 %collective-permute-done.12.refs_0_ = bf16[2,192,1024]{2,1,0:T(8,128)(2,1)} collective-permute-done((bf16[2,192,1024]{2,1,0:T(8,128)(2,1)}, bf16[2,192,1024]{2,1,0:T(8,128)(2,1)}, u32[]{:S(2)}, u32[]{:S(2)}) %collective-permute-start.12) | collective-permute-done | bytes 786464 | tf_op jit(solution)/shard_map/ppermute | solution.py:28
  166.2 1.4 collective-permute-done.14.refs_3_
  167.6 7.3 %gradient_terms.5 = (f32[2,48,1792]{2,1,0:T(8,128)S(1)}, bf16[2,48,1792]{2,1,0:T(8,128)(2,1)}, bf16[2,48,1792]{2,1,0:T(8,128)(2,1)}, bf16[2,48,1792]{2,1,0:T(8,128)(2,1)}) custom-call(s32[6]{0:T(128)S(1)} %copy-done.5, bf16[2,192,1024]{2,1,0:T(8,128)(2,1)} %collective-permute-done.12.refs_0_, bf16[2048,1792]{1,0:T(8,128)(2,1)S(1)} %bitcast.46, ...), custom_call_target="tpu_custom_call" | custom-call | flops 2818572288 | bytes 12582912 | tf_op jit(solution)/shard_map/gradient_terms/pallas_call | solution.py:264
  175.4 1.7 collective-permute-start.18
  177.2 2.4 %collective-permute-start.19 = (bf16[2,48,1792]{2,1,0:T(8,128)(2,1)}, bf16[2,48,1792]{2,1,0:T(8,128)(2,1)}, u32[]{:S(2)}, u32[]{:S(2)}) collective-permute-start(bf16[2,48,1792]{2,1,0:T(8,128)(2,1)} %get-tuple-element.58), channel_id=1, source_target_pairs={{0,48},{16,32},{32,16},{48,0},{1,49},{17,33},{33,17},{49,1},{2,50}... | collective-permute-start | bytes 1032200 | tf_op jit(solution)/shard_map/ppermute | solution.py:32
  179.9 0.9 collective-permute-done.16
  181.2 0.7 reshape.74
  181.9 2.4 %collective-permute-done.17.refs_1_ = bf16[2,48,1792]{2,1,0:T(8,128)(2,1)} collective-permute-done((bf16[2,48,1792]{2,1,0:T(8,128)(2,1)}, bf16[2,48,1792]{2,1,0:T(8,128)(2,1)}, u32[]{:S(2)}, u32[]{:S(2)}) %collective-permute-start.17) | collective-permute-done | bytes 344096 | tf_op jit(solution)/shard_map/ppermute | solution.py:32
  184.4 4.0 %collective-permute-done.18.refs_2_ = bf16[2,48,1792]{2,1,0:T(8,128)(2,1)} collective-permute-done((bf16[2,48,1792]{2,1,0:T(8,128)(2,1)}, bf16[2,48,1792]{2,1,0:T(8,128)(2,1)}, u32[]{:S(2)}, u32[]{:S(2)}) %collective-permute-start.18) | collective-permute-done | bytes 344096 | tf_op jit(solution)/shard_map/ppermute | solution.py:32
  188.3 2.5 %collective-permute-done.19.refs_3_ = bf16[2,48,1792]{2,1,0:T(8,128)(2,1)} collective-permute-done((bf16[2,48,1792]{2,1,0:T(8,128)(2,1)}, bf16[2,48,1792]{2,1,0:T(8,128)(2,1)}, u32[]{:S(2)}, u32[]{:S(2)}) %collective-permute-start.19) | collective-permute-done | bytes 344096 | tf_op jit(solution)/shard_map/ppermute | solution.py:32
  190.9 2.2 %rows.1 = bf16[16,8,1792]{2,1,0:T(8,128)(2,1)S(1)} custom-call(s32[6]{0:T(128)S(1)} %copy-done.6, f32[2,48,1792]{2,1,0:T(8,128)S(1)} %get-tuple-element.55.refs_0_, bf16[2,48,1792]{2,1,0:T(8,128)(2,1)} %collective-permute-done.17.refs_1_, bf16[2,48,1792]{2,1,0:T(8,128)(2,1)} %collective-permute-done.18.refs_2_, ...), custom_call_target="tpu_custom_call" | custom-call | tf_op jit(solution)/shard_map/rows/pallas_call | solution.py:299
  193.1 17.3 %all_to_all.17 = bf16[16,8,1792]{2,1,0:T(8,128)(2,1)S(1)} all-to-all(bf16[16,8,1792]{2,1,0:T(8,128)(2,1)S(1)} %rows.1), channel_id=1, replica_groups=mesh['rep'=2,'tok'=2,'y'=4,'z'=8,'core'=2] {'tok','z'}, dimensions={0} | all-to-all | bytes 917504 | tf_op jit(solution)/shard_map/all_to_all | solution.py:394
  210.5 0.6 pad_maximum_fusion.1
  (73 shorter events, 4.2 us)
Async XLA Ops:
  7.2 1.8 copy-start
  7.2 72.2 %all-gather.3.cloned.1.call-start = ((), (), s32[]{:S(2)}) async-start(), calls=%async_computation.3 | async-start | bytes 3096576 | tf_op jit(solution)/shard_map/all_gather | solution.py:348
  9.2 12.3 %collective-permute-start = (bf16[24,896]{1,0:T(8,128)(2,1)S(1)}, bf16[24,896]{1,0:T(8,128)(2,1)S(1)}, u32[]{:S(2)}, u32[]{:S(2)}) collective-permute-start(bf16[24,896]{1,0:T(8,128)(2,1)S(1)} %convolution_convert_fusion.1), channel_id=1, source_target_pairs={{0,64},{64,0},{128,192},{192,128},{1,65},{65,1},{129,193},{193,129... | collective-permute-start | bytes 129032 | tf_op jit(solution)/shard_map/ppermute | solution.py:28
  11.4 10.1 %collective-permute-start.1 = (bf16[24,896]{1,0:T(8,128)(2,1)S(1)}, bf16[24,896]{1,0:T(8,128)(2,1)S(1)}, u32[]{:S(2)}, u32[]{:S(2)}) collective-permute-start(bf16[24,896]{1,0:T(8,128)(2,1)S(1)} %convolution_convert_fusion.1), channel_id=1, source_target_pairs={{0,192},{64,128},{128,64},{192,0},{1,193},{65,129},{129,65},{193,1... | collective-permute-start | bytes 129032 | tf_op jit(solution)/shard_map/ppermute | solution.py:28
  15.1 6.4 %collective-permute-start.2 = (s32[2,192]{1,0:T(2,128)S(1)}, s32[2,192]{1,0:T(2,128)S(1)}, u32[]{:S(2)}, u32[]{:S(2)}) collective-permute-start(s32[2,192]{1,0:T(2,128)S(1)} %reshape.72), channel_id=1, source_target_pairs={{0,64},{64,0},{128,192},{192,128},{1,65},{65,1},{129,193},{193,129... | collective-permute-start | bytes 4616 | tf_op jit(solution)/shard_map/ppermute | solution.py:28
  21.5 6.9 %collective-permute-start.4 = (bf16[1,48,896]{2,1,0:T(8,128)(2,1)S(1)}, bf16[1,48,896]{2,1,0:T(8,128)(2,1)S(1)}, u32[]{:S(2)}, u32[]{:S(2)}) collective-permute-start(bf16[1,48,896]{2,1,0:T(8,128)(2,1)S(1)} %maximum_bitcast_fusion), channel_id=1, source_target_pairs={{0,16},{16,0},{32,48},{48,32},{1,17},{17,1},{33,49},{49,33},{2,18}... | collective-permute-start | bytes 258056 | tf_op jit(solution)/shard_map/ppermute | solution.py:32
  23.2 6.4 %collective-permute-start.5 = (bf16[1,48,896]{2,1,0:T(8,128)(2,1)S(1)}, bf16[1,48,896]{2,1,0:T(8,128)(2,1)S(1)}, u32[]{:S(2)}, u32[]{:S(2)}) collective-permute-start(bf16[1,48,896]{2,1,0:T(8,128)(2,1)S(1)} %maximum_bitcast_fusion), channel_id=1, source_target_pairs={{0,32},{16,48},{32,0},{48,16},{1,33},{17,49},{33,1},{49,17},{2,34}... | collective-permute-start | bytes 258056 | tf_op jit(solution)/shard_map/ppermute | solution.py:32
  26.1 5.7 %collective-permute-start.6 = (bf16[1,48,896]{2,1,0:T(8,128)(2,1)S(1)}, bf16[1,48,896]{2,1,0:T(8,128)(2,1)S(1)}, u32[]{:S(2)}, u32[]{:S(2)}) collective-permute-start(bf16[1,48,896]{2,1,0:T(8,128)(2,1)S(1)} %maximum_bitcast_fusion), channel_id=1, source_target_pairs={{0,48},{16,32},{32,16},{48,0},{1,49},{17,33},{33,17},{49,1},{2,50}... | collective-permute-start | bytes 258056 | tf_op jit(solution)/shard_map/ppermute | solution.py:32
  32.6 30.7 %collective-permute-start.3 = (bf16[1344,512]{1,0:T(8,128)(2,1)}, bf16[1344,512]{1,0:T(8,128)(2,1)}, u32[]{:S(2)}, u32[]{:S(2)}) collective-permute-start(bf16[1344,512]{1,0:T(8,128)(2,1)} %constant_dynamic-slice_fusion.1), channel_id=1, source_target_pairs={{0,192},{64,128},{128,64},{192,0},{1,193},{65,129},{129,65},{193,1... | collective-permute-start | bytes 4128776 | tf_op jit(solution)/shard_map/ppermute | solution.py:28
  33.2 30.3 %collective-permute-start.7 = (bf16[192,3584]{1,0:T(8,128)(2,1)}, bf16[192,3584]{1,0:T(8,128)(2,1)}, u32[]{:S(2)}, u32[]{:S(2)}) collective-permute-start(bf16[192,3584]{1,0:T(8,128)(2,1)} %convolution_convert_fusion.own), channel_id=1, source_target_pairs={{0,128},{64,192},{128,0},{192,64},{1,129},{65,193},{129,1},{193,65... | collective-permute-start | bytes 4128776 | tf_op jit(solution)/shard_map/ppermute | solution.py:28
  47.4 16.2 %copy-start.7 = (f32[1,2,192]{2,0,1:T(1,128)}, f32[1,2,192]{2,0,1:T(1,128)S(1)}, u32[]{:S(2)}) copy-start(f32[1,2,192]{2,0,1:T(1,128)S(1)} %get-tuple-element.65) | copy-start | bytes 4612
  63.8 15.6 %collective-permute-start.8 = (bf16[1792,512]{1,0:T(8,128)(2,1)}, bf16[1792,512]{1,0:T(8,128)(2,1)}, u32[]{:S(2)}, u32[]{:S(2)}) collective-permute-start(bf16[1792,512]{1,0:T(8,128)(2,1)} %constant_dynamic-slice_fusion), channel_id=1, source_target_pairs={{0,1},{1,0},{2,3},{3,2},{4,5},{5,4},{6,7},{7,6},{8,9},{9,8},{10,11... | collective-permute-start | bytes 5505032 | tf_op jit(solution)/shard_map/ppermute | solution.py:32
  63.9 15.5 %collective-permute-start.10 = (bf16[1344,512]{1,0:T(8,128)(2,1)}, bf16[1344,512]{1,0:T(8,128)(2,1)}, u32[]{:S(2)}, u32[]{:S(2)}) collective-permute-start(bf16[1344,512]{1,0:T(8,128)(2,1)} %collective-permute-done.3.refs_3_), channel_id=1, source_target_pairs={{0,1},{1,0},{2,3},{3,2},{4,5},{5,4},{6,7},{7,6},{8,9},{9,8},{10,11... | collective-permute-start | bytes 4128776 | tf_op jit(solution)/shard_map/ppermute | solution.py:32
  64.4 12.8 %collective-permute-start.9 = (bf16[448,512]{1,0:T(8,128)(2,1)}, bf16[448,512]{1,0:T(8,128)(2,1)}, u32[]{:S(2)}, u32[]{:S(2)}) collective-permute-start(bf16[448,512]{1,0:T(8,128)(2,1)} %constant_dynamic-slice_fusion.2), channel_id=1, source_target_pairs={{0,192},{64,128},{128,64},{192,0},{1,193},{65,129},{129,65},{193,1... | collective-permute-start | bytes 1376264 | tf_op jit(solution)/shard_map/ppermute | solution.py:28
  77.2 2.2 collective-permute-start.11
  77.3 48.5 %copy-start.3 = (s32[6]{0:T(128)}, s32[6]{0:T(128)S(1)}, u32[]{:S(2)}) copy-start(s32[6]{0:T(128)S(1)} %stack.51.at) | copy-start | bytes 76
  79.4 1.3 copy-start.2
  94.9 41.5 %collective-permute-start.13 = (bf16[2048,1792]{1,0:T(8,128)(2,1)}, bf16[2048,1792]{1,0:T(8,128)(2,1)}, u32[]{:S(2)}, u32[]{:S(2)}) collective-permute-start(bf16[2048,1792]{1,0:T(8,128)(2,1)} %bitcast.43), channel_id=1, source_target_pairs={{0,1},{1,0},{2,3},{3,2},{4,5},{5,4},{6,7},{7,6},{8,9},{9,8},{10,11... | collective-permute-start | bytes 22020104 | tf_op jit(solution)/shard_map/ppermute | solution.py:32
  131.7 20.7 %collective-permute-start.15 = (bf16[2,192,1024]{2,1,0:T(8,128)(2,1)}, bf16[2,192,1024]{2,1,0:T(8,128)(2,1)S(1)}, u32[]{:S(2)}, u32[]{:S(2)}) collective-permute-start(bf16[2,192,1024]{2,1,0:T(8,128)(2,1)} %get-tuple-element.51), channel_id=1, source_target_pairs={{0,128},{64,192},{128,0},{192,64},{1,129},{65,193},{129,1},{193,65... | collective-permute-start | bytes 2359304 | tf_op jit(solution)/shard_map/ppermute | solution.py:28
  133.2 33.0 %collective-permute-start.12 = (bf16[2,192,1024]{2,1,0:T(8,128)(2,1)}, bf16[2,192,1024]{2,1,0:T(8,128)(2,1)}, u32[]{:S(2)}, u32[]{:S(2)}) collective-permute-start(bf16[2,192,1024]{2,1,0:T(8,128)(2,1)} %get-tuple-element.49.refs_0_), channel_id=1, source_target_pairs={{0,64},{64,0},{128,192},{192,128},{1,65},{65,1},{129,193},{193,129... | collective-permute-start | bytes 2359304 | tf_op jit(solution)/shard_map/ppermute | solution.py:28
  133.7 33.9 %collective-permute-start.14 = (bf16[2,192,1024]{2,1,0:T(8,128)(2,1)}, bf16[2,192,1024]{2,1,0:T(8,128)(2,1)}, u32[]{:S(2)}, u32[]{:S(2)}) collective-permute-start(bf16[2,192,1024]{2,1,0:T(8,128)(2,1)} %get-tuple-element.51), channel_id=1, source_target_pairs={{0,192},{64,128},{128,64},{192,0},{1,193},{65,129},{129,65},{193,1... | collective-permute-start | bytes 2359304 | tf_op jit(solution)/shard_map/ppermute | solution.py:28
  136.5 3.1 %copy-start.1 = (bf16[1792,2048]{0,1:T(8,128)(2,1)S(1)}, bf16[1792,2048]{0,1:T(8,128)(2,1)}, u32[]{:S(2)}) copy-start(bf16[1792,2048]{0,1:T(8,128)(2,1)} %copy.21) | copy-start | bytes 22020100
  139.6 0.6 copy-start.4
  140.2 12.2 %copy-start.5 = (s32[6]{0:T(128)S(1)}, s32[6]{0:T(128)}, u32[]{:S(2)}) copy-start(s32[6]{0:T(128)} %copy-done.3) | copy-start | bytes 76
  156.4 23.1 %copy-start.8 = (f32[1,2,192]{2,0,1:T(1,128)S(1)}, f32[1,2,192]{2,0,1:T(1,128)}, u32[]{:S(2)}) copy-start(f32[1,2,192]{2,0,1:T(1,128)} %copy-done.7) | copy-start | bytes 4612
  156.4 23.2 %copy-start.9 = (f32[1,1,192]{2,0,1:T(1,128)S(1)}, f32[1,1,192]{2,0,1:T(1,128)}, u32[]{:S(2)}) copy-start(f32[1,1,192]{2,0,1:T(1,128)} %slice.47) | copy-start | bytes 2308
  156.4 34.4 %copy-start.6 = (s32[6]{0:T(128)S(1)}, s32[6]{0:T(128)}, u32[]{:S(2)}) copy-start(s32[6]{0:T(128)} %copy-done.3) | copy-start | bytes 76
  174.8 9.5 %collective-permute-start.17 = (bf16[2,48,1792]{2,1,0:T(8,128)(2,1)}, bf16[2,48,1792]{2,1,0:T(8,128)(2,1)}, u32[]{:S(2)}, u32[]{:S(2)}) collective-permute-start(bf16[2,48,1792]{2,1,0:T(8,128)(2,1)} %get-tuple-element.56), channel_id=1, source_target_pairs={{0,16},{16,0},{32,48},{48,32},{1,17},{17,1},{33,49},{49,33},{2,18}... | collective-permute-start | bytes 1032200 | tf_op jit(solution)/shard_map/ppermute | solution.py:32
  175.4 12.9 %collective-permute-start.18 = (bf16[2,48,1792]{2,1,0:T(8,128)(2,1)}, bf16[2,48,1792]{2,1,0:T(8,128)(2,1)}, u32[]{:S(2)}, u32[]{:S(2)}) collective-permute-start(bf16[2,48,1792]{2,1,0:T(8,128)(2,1)} %get-tuple-element.57), channel_id=1, source_target_pairs={{0,32},{16,48},{32,0},{48,16},{1,33},{17,49},{33,1},{49,17},{2,34}... | collective-permute-start | bytes 1032200 | tf_op jit(solution)/shard_map/ppermute | solution.py:32
  177.2 13.7 %collective-permute-start.19 = (bf16[2,48,1792]{2,1,0:T(8,128)(2,1)}, bf16[2,48,1792]{2,1,0:T(8,128)(2,1)}, u32[]{:S(2)}, u32[]{:S(2)}) collective-permute-start(bf16[2,48,1792]{2,1,0:T(8,128)(2,1)} %get-tuple-element.58), channel_id=1, source_target_pairs={{0,48},{16,32},{32,16},{48,0},{1,49},{17,33},{33,17},{49,1},{2,50}... | collective-permute-start | bytes 1032200 | tf_op jit(solution)/shard_map/ppermute | solution.py:32
  179.6 1.2 collective-permute-start.16
Sparse Core Ops, SparseCore 0:
  32.7 42.4 all-gather.2

commit v7 on v6

--- a/solution.py
+++ b/solution.py
@@ -16,7 +16,7 @@
 ROWS = 192
 QUARTER = 512
 HALF_D = 1792
-CHUNKS = (1344, 448)
+CHUNKS = (256, 1088, 448)
 TILE = 256
 WIDE = 896
 VMEM = 50 * 1024 * 1024
@@ -37,8 +37,8 @@
 
 
 def logits_kernel(at, own, nbr, *refs):
-    far, head, mate, got, tgt = refs[0], refs[1], refs[2], refs[3:7], refs[7]
-    logits, stats, rows, raws, sums = refs[8], refs[9], refs[10], refs[11:13], refs[13]
+    far, head, mate, got, tgt = refs[0], refs[1], refs[2], refs[3:9], refs[9]
+    logits, stats, rows, raws, sums = refs[10], refs[11], refs[12], refs[13:15], refs[15]
     step = pl.program_id(0)
     tok, y = at[0], at[2]
 
@@ -96,7 +96,7 @@
         def _(n=n):
             if n < 4:
                 core = n % 2
-                product(raws[n % 2], (head, mate)[core], got[core * 2 : core * 2 + 2])
+                product(raws[n % 2], (head, mate)[core], got[core * 3 : core * 3 + 3])
             if n > 0:
                 work(raws[(n - 1) % 2], (n - 1) // 2, (n - 1) % 2)
 
@@ -159,12 +159,12 @@
     )(at, own, nbr, far, head, mate, *got, tgt)
 
 
-def grad_kernel(at, logits, stats, tgt, mask, mine, theirs, scales):
+def grad_kernel(at, logits, stats, tgt, mask, out, scales, *, i):
     step = pl.program_id(0)
 
     @pl.when(step == 0)
     def _():
-        for j in range(4):
+        for j in (i, 2 + i):
             block = at[1] ^ j
             total = stats[block // 2].T[:ROWS]
             total = jnp.where(block % 2 == 0, total[:, 0:2], total[:, 4:6])
@@ -184,21 +184,20 @@
             target = jnp.concatenate([target, target], axis=1)
             weight = jnp.concatenate([weight, weight], axis=1)
             hit = jnp.where(column == target, weight, 0.0)
-            for i in range(2):
-                own = both[i]
-                shared = both[1 - i].astype(BF16).astype(F32)
-                own_scale, partner_scale = (
-                    jnp.concatenate([scales[n, pair * 2 + i, here]] * 2, axis=1) for n in range(2)
-                )
-                slope = own * (1.0 / softcap_limit)
-                value = jnp.exp(own) * own_scale - hit - jnp.exp(shared) * partner_scale
-                (mine, theirs)[i][pair, here] = (value * (1.0 - slope * slope)).astype(BF16)
-
-
-def grad_call(at, logits, stats, tgt, mask):
+            own = both[i]
+            shared = both[1 - i].astype(BF16).astype(F32)
+            own_scale, partner_scale = (
+                jnp.concatenate([scales[n, pair * 2 + i, here]] * 2, axis=1) for n in range(2)
+            )
+            slope = own * (1.0 / softcap_limit)
+            value = jnp.exp(own) * own_scale - hit - jnp.exp(shared) * partner_scale
+            out[pair, here] = (value * (1.0 - slope * slope)).astype(BF16)
+
+
+def grad_call(at, logits, stats, tgt, mask, i):
     out = pl.BlockSpec((2, ROWS, TILE), lambda s, at: (0, 0, s))
     return pl.pallas_call(
-        grad_kernel,
+        functools.partial(grad_kernel, i=i),
         grid_spec=pltpu.PrefetchScalarGridSpec(
             num_scalar_prefetch=1,
             grid=(4,),
@@ -208,10 +207,10 @@
                 whole(2, ROWS, 128),
                 whole(2, ROWS, 128),
             ],
-            out_specs=[out, out],
+            out_specs=out,
             scratch_shapes=[pltpu.VMEM((2, 4, ROWS, 128), F32)],
         ),
-        out_shape=[jax.ShapeDtypeStruct((2, ROWS, 4 * TILE), BF16)] * 2,
+        out_shape=jax.ShapeDtypeStruct((2, ROWS, 4 * TILE), BF16),
         compiler_params=pltpu.CompilerParams(vmem_limit_bytes=VMEM),
         name="logit_grad",
     )(at, logits, stats, tgt, mask)
@@ -337,14 +336,15 @@
     piece = jnp.concatenate([line_xor(slab, 2), line_xor(slab, 3)], axis=0)[None]
     far_scal = line_xor(scal, 2)
     sent = [
-        lax.dynamic_slice(head, (n * CHUNKS[0], (3 - x) * QUARTER), (CHUNKS[n], QUARTER))
-        for n in range(2)
+        lax.dynamic_slice(head, (sum(CHUNKS[:n]), (3 - x) * QUARTER), (CHUNKS[n], QUARTER))
+        for n in range(3)
     ]
     piece, far_scal, *sent = sync((piece, far_scal, *sent))
     got = [line_xor(sent[0], 3)]
     piece = jnp.concatenate([piece] + [axis_xor(piece, "y", k) for k in (1, 2, 3)])
     own = pick_rows(states, ROWS, core)
-    piece, own = sync((piece, own))
+    piece, own, got[0], sent[1] = sync((piece, own, got[0], sent[1]))
+    got.append(line_xor(sent[1], 3))
     far = lax.all_gather(piece[None], "z", axis=0, tiled=True)
     nbr = line_xor(own, 1)
 
@@ -359,10 +359,10 @@
     head_t = head.T
     head_t, cut = sync((head_t, head))
     cut = lax.dynamic_slice(cut, (0, x * QUARTER), (HALF_D, QUARTER))
-    head_t, tgt_wide, mask_wide, got[0], nbr, sent[1], cut = sync(
-        (head_t, tgt_wide, mask_wide, got[0], nbr, sent[1], cut)
+    head_t, tgt_wide, mask_wide, got[1], nbr, sent[2], cut = sync(
+        (head_t, tgt_wide, mask_wide, got[1], nbr, sent[2], cut)
     )
-    got.append(line_xor(sent[1], 3))
+    got.append(line_xor(sent[2], 3))
     mate = axis_xor(cut, "core", 1)
     got_mate = [axis_xor(g, "core", 1) for g in got]
     got = got + got_mate
@@ -372,11 +372,13 @@
     mate_t = axis_xor(head_t, "core", 1)
     stats = add_over_slice(stats)
 
-    mine, theirs = grad_call(at, logits, stats, tgt_wide, mask_wide)
-    grads = [mine, line_xor(theirs, 1), line_xor(mine, 2), line_xor(theirs, 3)]
+    theirs = grad_call(at, logits, stats, tgt_wide, mask_wide, 1)
+    near, cross_part = line_xor(theirs, 1), line_xor(theirs, 3)
+    mine = grad_call(at, logits, stats, tgt_wide, mask_wide, 0)
+    grads = [mine, near, line_xor(mine, 2), cross_part]
     terms = terms_call(at, grads[:1], head_t, mate_t, (0,))
-    terms = terms_call(at, grads[1:2], head_t, mate_t, (1,), terms)
-    parts = list(terms_call(at, grads[2:], head_t, mate_t, (2, 3), terms, last=True))
+    terms = terms_call(at, grads[3:], head_t, mate_t, (3,), terms)
+    parts = list(terms_call(at, grads[1:3], head_t, mate_t, (1, 2), terms, last=True))
 
     stats, parts[0] = sync((stats, parts[0]))
     stats = lax.dynamic_index_in_dim(stats.reshape(4, 4, 256), x, 0, keepdims=False)

time: 219 us -> 227 us (1.037)
  Pallas kernels: 37.9 us -> 41.6 us
  starting transfers between devices: 22.9 us -> 25.3 us
    pallas_call x1 -> x2, Pallas kernels: 5.95 us -> 9.27 us  [grad_call(): pl.pallas_call(functools.partial(grad_kernel, i=i), grid_spec=pltpu.Prefe...]
    ppermute x9 -> x10, starting transfers between devices: 12.6 us -> 14.5 us  [line_xor(): return lax.ppermute(block, LINE, [(x, x ^ k) for x in range(N_X)])]
    ppermute x9 -> x10, waiting for transfers between devices: 46.6 us -> 45.1 us  [line_xor(): return lax.ppermute(block, LINE, [(x, x ^ k) for x in range(N_X)])]
    ppermute x11 -> x12, waiting for transfers between devices: 15.3 us -> 16.6 us  [axis_xor(): lax.ppermute(block, axis, [(i, i ^ k) for i in range(lax.axis_size(axis))])]
    unnamed x23 -> x31, local copies, waits for them, and re-layouts: 16.8 us -> 17.9 us
    dynamic_slice x2 -> x3, local copies, waits for them, and re-layouts: 4.35 us -> 5.14 us  [shards(): lax.dynamic_slice(head, (sum(CHUNKS[:n]), (3 - x) * QUARTER), (CHUNKS[n],...]
    ppermute x11 -> x12, starting transfers between devices: 10.3 us -> 10.8 us  [axis_xor(): lax.ppermute(block, axis, [(i, i ^ k) for i in range(lax.axis_size(axis))])]
  transfers between devices with their start and end apart: 21 -> 23, of which waited for: 13 -> 14; matrix products, arithmetic and copies ran while one was open for 11% -> 12% of each run, Pallas kernels for 6% -> 8%
where the time goes in v7:
time: 227 us; the launch traced here: 226 us
  waiting for transfers between devices  61.7 us (27%)
  blocking collectives  48.2 us (21%)
  Pallas kernels  41.6 us (18%)
  local copies, waits for them, and re-layouts  30.8 us (14%)
  starting transfers between devices  25.3 us (11%)
  between operations  14.4 us (6%)
  matrix products  2.41 us (1%)
    ppermute x10, waiting for transfers between devices, line_xor(): return lax.ppermute(block, LINE, [(x, x ^ k) for x in range(N_X)])  45.1 us
    all_to_all x2, blocking collectives, add_over_slice(): stats = jnp.sum(lax.all_to_all(spread, axis, 0, 0, tiled=True), axis=0)  31.9 us
    unnamed x31, local copies, waits for them, and re-layouts  17.9 us
    ppermute x12, waiting for transfers between devices, axis_xor(): lax.ppermute(block, axis, [(i, i ^ k) for i in range(lax.axis_size(axis))])  16.6 us
    all_to_all x1, blocking collectives, shards(): low = lax.all_to_all(rows_call(at, parts), ('tok', 'z'), 0, 0, tiled=True)  16.2 us
    pallas_call x3, Pallas kernels, terms_call(): pl.pallas_call(functools.partial(terms_kernel, ks=ks, add=acc is not None...  15.5 us
    pallas_call x1, Pallas kernels, logits_call(): pl.pallas_call(logits_kernel, grid_spec=pltpu.PrefetchScalarGridSpec(num_...  14.6 us
    ppermute x10, starting transfers between devices, line_xor(): return lax.ppermute(block, LINE, [(x, x ^ k) for x in range(N_X)])  14.5 us
  transfers between devices with their start and end apart: 23, of which 14 were waited for; matrix products, arithmetic and copies ran while one was open for 12% of the time, Pallas kernels for 8%

profile of v7, /device:TPU:2, one launch (start us, length us, event | category | flops | bytes accessed | tf_op | source)
XLA Modules:
  0.0 226.1 jit_solution(17835320780263867439)
XLA Ops:
  7.3 1.7 copy-done
  9.2 2.2 collective-permute-start
  11.4 1.6 collective-permute-start.1
  13.0 0.8 stack.52
  13.9 0.8 stack.53
  15.1 2.0 collective-permute-start.2
  17.1 2.3 %constant_dynamic-slice_fusion.3 = bf16[1088,512]{1,0:T(8,128)(2,1)} fusion(bf16[1792,2048]{1,0:T(8,128)(2,1)} %refs_1_.1, s32[]{:T(128)S(6)} %select_n.59), kind=kLoop, calls=%fused_computation.64 | loop fusion | bytes 2228228 | tf_op jit(solution)/shard_map/dynamic_slice | solution.py:339
  19.4 1.8 constant_dynamic-slice_fusion.2
  21.2 1.0 constant_dynamic-slice_fusion.1
  22.3 1.7 collective-permute-start.3
  24.0 2.9 %collective-permute-start.4 = (bf16[1,48,896]{2,1,0:T(8,128)(2,1)S(1)}, bf16[1,48,896]{2,1,0:T(8,128)(2,1)S(1)}, u32[]{:S(2)}, u32[]{:S(2)}) collective-permute-start(bf16[1,48,896]{2,1,0:T(8,128)(2,1)S(1)} %maximum_bitcast_fusion), channel_id=1, source_target_pairs={{0,32},{16,48},{32,0},{48,16},{1,33},{17,49},{33,1},{49,17},{2,34}... | collective-permute-start | bytes 258056 | tf_op jit(solution)/shard_map/ppermute | solution.py:32
  27.6 2.2 convolution_convert_fusion.own
  30.4 2.2 collective-permute-done.5
  32.6 0.8 pad_maximum_fusion
  33.5 1.9 collective-permute-start.8
  35.4 1.6 collective-permute-start.7
  37.1 10.1 %copy.21 = bf16[1792,2048]{0,1:T(8,128)(2,1)} copy(bf16[1792,2048]{1,0:T(8,128)(2,1)} %refs_1_.1) | data formatting | bytes 14680064 | tf_op args[1]
  47.2 2.8 %constant_dynamic-slice_fusion = bf16[1792,512]{1,0:T(8,128)(2,1)} fusion(bf16[1792,2048]{1,0:T(8,128)(2,1)} %refs_1_.1, s32[]{:T(128)S(6)} %select_n.62), kind=kLoop, calls=%fused_computation.47 | loop fusion | bytes 3670020 | tf_op jit(solution)/shard_map/dynamic_slice | solution.py:361
  50.1 9.2 %collective-permute-done.7.refs_4_ = bf16[1088,512]{1,0:T(8,128)(2,1)} collective-permute-done((bf16[1088,512]{1,0:T(8,128)(2,1)}, bf16[1088,512]{1,0:T(8,128)(2,1)}, u32[]{:S(2)}, u32[]{:S(2)}) %collective-permute-start.7) | collective-permute-done | bytes 1114144 | tf_op jit(solution)/shard_map/ppermute | solution.py:28
  59.2 4.8 %collective-permute-done.8.nbr = bf16[192,3584]{1,0:T(8,128)(2,1)} collective-permute-done((bf16[192,3584]{1,0:T(8,128)(2,1)}, bf16[192,3584]{1,0:T(8,128)(2,1)}, u32[]{:S(2)}, u32[]{:S(2)}) %collective-permute-start.8) | collective-permute-done | bytes 1376288 | tf_op jit(solution)/shard_map/ppermute | solution.py:28
  65.5 12.3 %collective-permute-done.10.refs_5_ = bf16[448,512]{1,0:T(8,128)(2,1)} collective-permute-done((bf16[448,512]{1,0:T(8,128)(2,1)}, bf16[448,512]{1,0:T(8,128)(2,1)}, u32[]{:S(2)}, u32[]{:S(2)}) %collective-permute-start.10) | collective-permute-done | bytes 458784 | tf_op jit(solution)/shard_map/ppermute | solution.py:28
  78.4 1.5 collective-permute-done.11.refs_6_
  80.3 14.6 %logits.1 = (f32[4,192,1024]{2,1,0:T(8,128)}, f32[2,8,256]{2,1,0:T(8,128)S(1)}) custom-call(s32[6]{0:T(128)S(1)} %stack.51.at, bf16[192,3584]{1,0:T(8,128)(2,1)} %convolution_convert_fusion.own, bf16[192,3584]{1,0:T(8,128)(2,1)} %collective-permute-done.8.nbr, bf16[8,4,48,896]{3,2,1,0:T(8,128)(2,1)} %bitcast.53, bf16[1792,2048]{1,0:T(8,128)(2,1)} %refs_1_.1, ...), custom_call_target="tpu_custom_call" | custom-call | flops 5637144576 | bytes 16777216 | tf_op jit(solution)/shard_map/logits/pallas_call | solution.py:129
  95.1 14.6 %all_to_all.15 = f32[16,2,8,256]{3,2,1,0:T(8,128)S(1)} all-to-all(f32[16,2,8,256]{3,2,1,0:T(8,128)S(1)} %broadcast_in_dim.37), channel_id=1, replica_groups=mesh['rep'=2,'tok'=2,'y'=4,'z'=8,'core'=2] {'rep','tok','y'}, dimensions={0} | all-to-all | bytes 524288 | tf_op jit(solution)/shard_map/all_to_all | solution.py:315
  109.7 17.3 %all_to_all.16 = f32[8,2,8,256]{3,2,1,0:T(8,128)S(1)} all-to-all(f32[8,2,8,256]{3,2,1,0:T(8,128)S(1)} %broadcast_in_dim.38), channel_id=1, replica_groups=mesh['rep'=2,'tok'=2,'y'=4,'z'=8,'core'=2] {'z'}, dimensions={0} | all-to-all | bytes 262144 | tf_op jit(solution)/shard_map/all_to_all | solution.py:315
  127.1 5.2 %logit_grad.2 = bf16[2,192,1024]{2,1,0:T(8,128)(2,1)} custom-call(s32[6]{0:T(128)S(1)} %stack.51.at, f32[4,192,1024]{2,1,0:T(8,128)} %get-tuple-element.51.logits, f32[2,8,256]{2,1,0:T(8,128)S(1)} %reduce_sum.28.stats, s32[2,192,128]{2,1,0:T(8,128)S(1)} %broadcast_in_dim.16.refs_9_.tgt, f32[2,192,128]{2,1,0:T(8,128)S(1)} %broadcast_in_dim.17.mask), custom_call_target="tpu_custom_call" | custom-call | tf_op jit(solution)/shard_map/logit_grad/pallas_call | solution.py:199
  132.7 0.9 copy-done.3
  133.7 0.9 copy-done.5
  134.6 0.6 copy-done.7
  135.2 4.1 %logit_grad.3.refs_0_ = bf16[2,192,1024]{2,1,0:T(8,128)(2,1)S(1)} custom-call(s32[6]{0:T(128)S(1)} %copy-done.7, f32[4,192,1024]{2,1,0:T(8,128)} %get-tuple-element.51.logits, f32[2,8,256]{2,1,0:T(8,128)S(1)} %reduce_sum.28.stats, s32[2,192,128]{2,1,0:T(8,128)S(1)} %copy-done.3, f32[2,192,128]{2,1,0:T(8,128)S(1)} %copy-done.5), custom_call_target="tpu_custom_call" | custom-call | tf_op jit(solution)/shard_map/logit_grad/pallas_call | solution.py:199
  139.3 3.2 %collective-permute-start.16 = (bf16[2,192,1024]{2,1,0:T(8,128)(2,1)S(1)}, bf16[2,192,1024]{2,1,0:T(8,128)(2,1)}, u32[]{:S(2)}, u32[]{:S(2)}) collective-permute-start(bf16[2,192,1024]{2,1,0:T(8,128)(2,1)S(1)} %logit_grad.3.refs_0_), channel_id=1, source_target_pairs={{0,64},{64,0},{128,192},{192,128},{1,65},{65,1},{129,193},{193,129... | collective-permute-start | bytes 2359304 | tf_op jit(solution)/shard_map/ppermute | solution.py:28
  143.0 1.2 slice.47
  144.3 3.1 %copy-done.1 = bf16[1792,2048]{0,1:T(8,128)(2,1)S(1)} copy-done((bf16[1792,2048]{0,1:T(8,128)(2,1)S(1)}, bf16[1792,2048]{0,1:T(8,128)(2,1)}, u32[]{:S(2)}) %copy-start.1) | copy-done | bytes 7340056
  147.9 3.9 %gradient_terms.3.refs_3_ = f32[384,1792]{1,0:T(8,128)S(1)} custom-call(s32[6]{0:T(128)S(1)} %copy-done.8, bf16[2,192,1024]{2,1,0:T(8,128)(2,1)S(1)} %logit_grad.3.refs_0_, bf16[2048,1792]{1,0:T(8,128)(2,1)S(1)} %bitcast.44, bf16[2048,1792]{1,0:T(8,128)(2,1)} %collective-permute-done.15.refs_2_.refs_5_), custom_call_target="tpu_custom_call" | custom-call | flops 1409286144 | bytes 6291456 | tf_op jit(solution)/shard_map/gradient_terms/pallas_call | solution.py:263
  151.9 14.7 %collective-permute-done.17.refs_0_ = bf16[2,192,1024]{2,1,0:T(8,128)(2,1)} collective-permute-done((bf16[2,192,1024]{2,1,0:T(8,128)(2,1)}, bf16[2,192,1024]{2,1,0:T(8,128)(2,1)}, u32[]{:S(2)}, u32[]{:S(2)}) %collective-permute-start.17) | collective-permute-done | bytes 786464 | tf_op jit(solution)/shard_map/ppermute | solution.py:28
  166.6 4.2 %gradient_terms.4.refs_6_ = f32[384,1792]{1,0:T(8,128)S(1)} custom-call(s32[6]{0:T(128)S(1)} %copy-done.8, bf16[2,192,1024]{2,1,0:T(8,128)(2,1)} %collective-permute-done.17.refs_0_, bf16[2048,1792]{1,0:T(8,128)(2,1)S(1)} %bitcast.45, bf16[2048,1792]{1,0:T(8,128)(2,1)} %collective-permute-done.15.refs_2_.refs_5_, f32[384,1792]{1,0:T(8,128)S(1)} %gradient_terms.3.refs_3_), custom_call_target="tpu_custom_call" | custom-call | flops 1409286144 | bytes 6291456 | tf_op jit(solution)/shard_map/gradient_terms/pallas_call | solution.py:263
  170.9 3.9 %collective-permute-done.14.refs_0_ = bf16[2,192,1024]{2,1,0:T(8,128)(2,1)} collective-permute-done((bf16[2,192,1024]{2,1,0:T(8,128)(2,1)}, bf16[2,192,1024]{2,1,0:T(8,128)(2,1)}, u32[]{:S(2)}, u32[]{:S(2)}) %collective-permute-start.14) | collective-permute-done | bytes 786464 | tf_op jit(solution)/shard_map/ppermute | solution.py:28
  174.8 7.3 %gradient_terms.5 = (f32[2,48,1792]{2,1,0:T(8,128)S(1)}, bf16[2,48,1792]{2,1,0:T(8,128)(2,1)}, bf16[2,48,1792]{2,1,0:T(8,128)(2,1)}, bf16[2,48,1792]{2,1,0:T(8,128)(2,1)}) custom-call(s32[6]{0:T(128)S(1)} %copy-done.9, bf16[2,192,1024]{2,1,0:T(8,128)(2,1)} %collective-permute-done.14.refs_0_, bf16[2048,1792]{1,0:T(8,128)(2,1)S(1)} %bitcast.46, ...), custom_call_target="tpu_custom_call" | custom-call | flops 2818572288 | bytes 12582912 | tf_op jit(solution)/shard_map/gradient_terms/pallas_call | solution.py:263
  182.4 2.5 %collective-permute-start.20 = (bf16[2,48,1792]{2,1,0:T(8,128)(2,1)}, bf16[2,48,1792]{2,1,0:T(8,128)(2,1)}, u32[]{:S(2)}, u32[]{:S(2)}) collective-permute-start(bf16[2,48,1792]{2,1,0:T(8,128)(2,1)} %get-tuple-element.59), channel_id=1, source_target_pairs={{0,32},{16,48},{32,0},{48,16},{1,33},{17,49},{33,1},{49,17},{2,34}... | collective-permute-start | bytes 1032200 | tf_op jit(solution)/shard_map/ppermute | solution.py:32
  184.9 1.8 collective-permute-start.21
  187.1 0.9 collective-permute-done.18
  188.4 0.7 reshape.74
  189.1 3.4 %collective-permute-done.19.refs_1_ = bf16[2,48,1792]{2,1,0:T(8,128)(2,1)} collective-permute-done((bf16[2,48,1792]{2,1,0:T(8,128)(2,1)}, bf16[2,48,1792]{2,1,0:T(8,128)(2,1)}, u32[]{:S(2)}, u32[]{:S(2)}) %collective-permute-start.19) | collective-permute-done | bytes 344096 | tf_op jit(solution)/shard_map/ppermute | solution.py:32
  192.5 5.0 %collective-permute-done.20.refs_2_ = bf16[2,48,1792]{2,1,0:T(8,128)(2,1)} collective-permute-done((bf16[2,48,1792]{2,1,0:T(8,128)(2,1)}, bf16[2,48,1792]{2,1,0:T(8,128)(2,1)}, u32[]{:S(2)}, u32[]{:S(2)}) %collective-permute-start.20) | collective-permute-done | bytes 344096 | tf_op jit(solution)/shard_map/ppermute | solution.py:32
  197.4 2.6 %collective-permute-done.21.refs_3_ = bf16[2,48,1792]{2,1,0:T(8,128)(2,1)} collective-permute-done((bf16[2,48,1792]{2,1,0:T(8,128)(2,1)}, bf16[2,48,1792]{2,1,0:T(8,128)(2,1)}, u32[]{:S(2)}, u32[]{:S(2)}) %collective-permute-start.21) | collective-permute-done | bytes 344096 | tf_op jit(solution)/shard_map/ppermute | solution.py:32
  200.1 2.2 rows.1
  202.3 16.2 %all_to_all.17 = bf16[16,8,1792]{2,1,0:T(8,128)(2,1)S(1)} all-to-all(bf16[16,8,1792]{2,1,0:T(8,128)(2,1)S(1)} %rows.1), channel_id=1, replica_groups=mesh['rep'=2,'tok'=2,'y'=4,'z'=8,'core'=2] {'tok','z'}, dimensions={0} | all-to-all | bytes 917504 | tf_op jit(solution)/shard_map/all_to_all | solution.py:396
  218.6 0.6 pad_maximum_fusion.1
  (87 shorter events, 7.6 us)
Async XLA Ops:
  7.2 1.8 copy-start
  7.2 73.1 %all-gather.3.cloned.1.call-start = ((), (), s32[]{:S(2)}) async-start(), calls=%async_computation.3 | async-start | bytes 3096576 | tf_op jit(solution)/shard_map/all_gather | solution.py:348
  9.2 13.1 %collective-permute-start = (bf16[24,896]{1,0:T(8,128)(2,1)S(1)}, bf16[24,896]{1,0:T(8,128)(2,1)S(1)}, u32[]{:S(2)}, u32[]{:S(2)}) collective-permute-start(bf16[24,896]{1,0:T(8,128)(2,1)S(1)} %convolution_convert_fusion.1), channel_id=1, source_target_pairs={{0,64},{64,0},{128,192},{192,128},{1,65},{65,1},{129,193},{193,129... | collective-permute-start | bytes 129032 | tf_op jit(solution)/shard_map/ppermute | solution.py:28
  11.4 10.9 %collective-permute-start.1 = (bf16[24,896]{1,0:T(8,128)(2,1)S(1)}, bf16[24,896]{1,0:T(8,128)(2,1)S(1)}, u32[]{:S(2)}, u32[]{:S(2)}) collective-permute-start(bf16[24,896]{1,0:T(8,128)(2,1)S(1)} %convolution_convert_fusion.1), channel_id=1, source_target_pairs={{0,192},{64,128},{128,64},{192,0},{1,193},{65,129},{129,65},{193,1... | collective-permute-start | bytes 129032 | tf_op jit(solution)/shard_map/ppermute | solution.py:28
  15.1 7.2 %collective-permute-start.2 = (s32[2,192]{1,0:T(2,128)S(1)}, s32[2,192]{1,0:T(2,128)S(1)}, u32[]{:S(2)}, u32[]{:S(2)}) collective-permute-start(s32[2,192]{1,0:T(2,128)S(1)} %reshape.72), channel_id=1, source_target_pairs={{0,64},{64,0},{128,192},{192,128},{1,65},{65,1},{129,193},{193,129... | collective-permute-start | bytes 4616 | tf_op jit(solution)/shard_map/ppermute | solution.py:28
  22.3 7.5 %collective-permute-start.3 = (bf16[1,48,896]{2,1,0:T(8,128)(2,1)S(1)}, bf16[1,48,896]{2,1,0:T(8,128)(2,1)S(1)}, u32[]{:S(2)}, u32[]{:S(2)}) collective-permute-start(bf16[1,48,896]{2,1,0:T(8,128)(2,1)S(1)} %maximum_bitcast_fusion), channel_id=1, source_target_pairs={{0,16},{16,0},{32,48},{48,32},{1,17},{17,1},{33,49},{49,33},{2,18}... | collective-permute-start | bytes 258056 | tf_op jit(solution)/shard_map/ppermute | solution.py:32
  24.0 6.4 %collective-permute-start.4 = (bf16[1,48,896]{2,1,0:T(8,128)(2,1)S(1)}, bf16[1,48,896]{2,1,0:T(8,128)(2,1)S(1)}, u32[]{:S(2)}, u32[]{:S(2)}) collective-permute-start(bf16[1,48,896]{2,1,0:T(8,128)(2,1)S(1)} %maximum_bitcast_fusion), channel_id=1, source_target_pairs={{0,32},{16,48},{32,0},{48,16},{1,33},{17,49},{33,1},{49,17},{2,34}... | collective-permute-start | bytes 258056 | tf_op jit(solution)/shard_map/ppermute | solution.py:32
  26.9 5.7 %collective-permute-start.5 = (bf16[1,48,896]{2,1,0:T(8,128)(2,1)S(1)}, bf16[1,48,896]{2,1,0:T(8,128)(2,1)S(1)}, u32[]{:S(2)}, u32[]{:S(2)}) collective-permute-start(bf16[1,48,896]{2,1,0:T(8,128)(2,1)S(1)} %maximum_bitcast_fusion), channel_id=1, source_target_pairs={{0,48},{16,32},{32,16},{48,0},{1,49},{17,33},{33,17},{49,1},{2,50}... | collective-permute-start | bytes 258056 | tf_op jit(solution)/shard_map/ppermute | solution.py:32
  27.1 6.4 %collective-permute-start.6 = (bf16[256,512]{1,0:T(8,128)(2,1)S(1)}, bf16[256,512]{1,0:T(8,128)(2,1)S(1)}, u32[]{:S(2)}, u32[]{:S(2)}) collective-permute-start(bf16[256,512]{1,0:T(8,128)(2,1)S(1)} %constant_dynamic-slice_fusion.1), channel_id=1, source_target_pairs={{0,192},{64,128},{128,64},{192,0},{1,193},{65,129},{129,65},{193,1... | collective-permute-start | bytes 786440 | tf_op jit(solution)/shard_map/ppermute | solution.py:28
  33.5 30.5 %collective-permute-start.8 = (bf16[192,3584]{1,0:T(8,128)(2,1)}, bf16[192,3584]{1,0:T(8,128)(2,1)}, u32[]{:S(2)}, u32[]{:S(2)}) collective-permute-start(bf16[192,3584]{1,0:T(8,128)(2,1)} %convolution_convert_fusion.own), channel_id=1, source_target_pairs={{0,128},{64,192},{128,0},{192,64},{1,129},{65,193},{129,1},{193,65... | collective-permute-start | bytes 4128776 | tf_op jit(solution)/shard_map/ppermute | solution.py:28
  35.4 23.8 %collective-permute-start.7 = (bf16[1088,512]{1,0:T(8,128)(2,1)}, bf16[1088,512]{1,0:T(8,128)(2,1)}, u32[]{:S(2)}, u32[]{:S(2)}) collective-permute-start(bf16[1088,512]{1,0:T(8,128)(2,1)} %constant_dynamic-slice_fusion.3), channel_id=1, source_target_pairs={{0,192},{64,128},{128,64},{192,0},{1,193},{65,129},{129,65},{193,1... | collective-permute-start | bytes 3342344 | tf_op jit(solution)/shard_map/ppermute | solution.py:28
  50.0 27.7 %copy-start.11 = (f32[1,2,192]{2,0,1:T(1,128)}, f32[1,2,192]{2,0,1:T(1,128)S(1)}, u32[]{:S(2)}) copy-start(f32[1,2,192]{2,0,1:T(1,128)S(1)} %get-tuple-element.67) | copy-start | bytes 4612
  64.2 62.9 %copy-start.2 = (s32[2,192,128]{2,1,0:T(8,128)}, s32[2,192,128]{2,1,0:T(8,128)S(1)}, u32[]{:S(2)}) copy-start(s32[2,192,128]{2,1,0:T(8,128)S(1)} %broadcast_in_dim.16.refs_9_.tgt) | copy-start | bytes 589828
  64.3 62.8 %copy-start.4 = (f32[2,192,128]{2,1,0:T(8,128)}, f32[2,192,128]{2,1,0:T(8,128)S(1)}, u32[]{:S(2)}) copy-start(f32[2,192,128]{2,1,0:T(8,128)S(1)} %broadcast_in_dim.17.mask) | copy-start | bytes 589828
  64.3 16.0 %collective-permute-start.9 = (bf16[1792,512]{1,0:T(8,128)(2,1)}, bf16[1792,512]{1,0:T(8,128)(2,1)}, u32[]{:S(2)}, u32[]{:S(2)}) collective-permute-start(bf16[1792,512]{1,0:T(8,128)(2,1)} %constant_dynamic-slice_fusion), channel_id=1, source_target_pairs={{0,1},{1,0},{2,3},{3,2},{4,5},{5,4},{6,7},{7,6},{8,9},{9,8},{10,11... | collective-permute-start | bytes 5505032 | tf_op jit(solution)/shard_map/ppermute | solution.py:32
  64.4 15.9 %collective-permute-start.12 = (bf16[1088,512]{1,0:T(8,128)(2,1)}, bf16[1088,512]{1,0:T(8,128)(2,1)}, u32[]{:S(2)}, u32[]{:S(2)}) collective-permute-start(bf16[1088,512]{1,0:T(8,128)(2,1)} %collective-permute-done.7.refs_4_), channel_id=1, source_target_pairs={{0,1},{1,0},{2,3},{3,2},{4,5},{5,4},{6,7},{7,6},{8,9},{9,8},{10,11... | collective-permute-start | bytes 3342344 | tf_op jit(solution)/shard_map/ppermute | solution.py:32
  64.9 12.8 %collective-permute-start.10 = (bf16[448,512]{1,0:T(8,128)(2,1)}, bf16[448,512]{1,0:T(8,128)(2,1)}, u32[]{:S(2)}, u32[]{:S(2)}) collective-permute-start(bf16[448,512]{1,0:T(8,128)(2,1)} %constant_dynamic-slice_fusion.2), channel_id=1, source_target_pairs={{0,192},{64,128},{128,64},{192,0},{1,193},{65,129},{129,65},{193,1... | collective-permute-start | bytes 1376264 | tf_op jit(solution)/shard_map/ppermute | solution.py:28
  77.8 2.5 %collective-permute-start.13 = (bf16[448,512]{1,0:T(8,128)(2,1)}, bf16[448,512]{1,0:T(8,128)(2,1)}, u32[]{:S(2)}, u32[]{:S(2)}) collective-permute-start(bf16[448,512]{1,0:T(8,128)(2,1)} %collective-permute-done.10.refs_5_), channel_id=1, source_target_pairs={{0,1},{1,0},{2,3},{3,2},{4,5},{5,4},{6,7},{7,6},{8,9},{9,8},{10,11... | collective-permute-start | bytes 1376264 | tf_op jit(solution)/shard_map/ppermute | solution.py:32
  77.8 2.1 collective-permute-start.11
  78.4 48.8 %copy-start.6 = (s32[6]{0:T(128)}, s32[6]{0:T(128)S(1)}, u32[]{:S(2)}) copy-start(s32[6]{0:T(128)S(1)} %stack.51.at) | copy-start | bytes 76
  95.0 49.3 %collective-permute-start.15 = (bf16[2048,1792]{1,0:T(8,128)(2,1)}, bf16[2048,1792]{1,0:T(8,128)(2,1)}, u32[]{:S(2)}, u32[]{:S(2)}) collective-permute-start(bf16[2048,1792]{1,0:T(8,128)(2,1)} %bitcast.43), channel_id=1, source_target_pairs={{0,1},{1,0},{2,3},{3,2},{4,5},{5,4},{6,7},{7,6},{8,9},{9,8},{10,11... | collective-permute-start | bytes 22020104 | tf_op jit(solution)/shard_map/ppermute | solution.py:32
  132.3 34.2 %collective-permute-start.17 = (bf16[2,192,1024]{2,1,0:T(8,128)(2,1)}, bf16[2,192,1024]{2,1,0:T(8,128)(2,1)}, u32[]{:S(2)}, u32[]{:S(2)}) collective-permute-start(bf16[2,192,1024]{2,1,0:T(8,128)(2,1)} %logit_grad.2), channel_id=1, source_target_pairs={{0,192},{64,128},{128,64},{192,0},{1,193},{65,129},{129,65},{193,1... | collective-permute-start | bytes 2359304 | tf_op jit(solution)/shard_map/ppermute | solution.py:28
  132.7 0.9 copy-start.3
  133.7 0.9 copy-start.5
  134.6 0.6 copy-start.7
  139.3 31.6 %collective-permute-start.16 = (bf16[2,192,1024]{2,1,0:T(8,128)(2,1)S(1)}, bf16[2,192,1024]{2,1,0:T(8,128)(2,1)}, u32[]{:S(2)}, u32[]{:S(2)}) collective-permute-start(bf16[2,192,1024]{2,1,0:T(8,128)(2,1)S(1)} %logit_grad.3.refs_0_), channel_id=1, source_target_pairs={{0,64},{64,0},{128,192},{192,128},{1,65},{65,1},{129,193},{193,129... | collective-permute-start | bytes 2359304 | tf_op jit(solution)/shard_map/ppermute | solution.py:28
  142.5 32.3 %collective-permute-start.14 = (bf16[2,192,1024]{2,1,0:T(8,128)(2,1)}, bf16[2,192,1024]{2,1,0:T(8,128)(2,1)}, u32[]{:S(2)}, u32[]{:S(2)}) collective-permute-start(bf16[2,192,1024]{2,1,0:T(8,128)(2,1)} %logit_grad.2), channel_id=1, source_target_pairs={{0,128},{64,192},{128,0},{192,64},{1,129},{65,193},{129,1},{193,65... | collective-permute-start | bytes 2359304 | tf_op jit(solution)/shard_map/ppermute | solution.py:28
  144.3 3.1 %copy-start.1 = (bf16[1792,2048]{0,1:T(8,128)(2,1)S(1)}, bf16[1792,2048]{0,1:T(8,128)(2,1)}, u32[]{:S(2)}) copy-start(bf16[1792,2048]{0,1:T(8,128)(2,1)} %copy.21) | copy-start | bytes 22020100
  147.3 0.6 copy-start.8
  151.9 22.9 %copy-start.9 = (s32[6]{0:T(128)S(1)}, s32[6]{0:T(128)}, u32[]{:S(2)}) copy-start(s32[6]{0:T(128)} %copy-done.6) | copy-start | bytes 76
  170.8 15.9 %copy-start.12 = (f32[1,2,192]{2,0,1:T(1,128)S(1)}, f32[1,2,192]{2,0,1:T(1,128)}, u32[]{:S(2)}) copy-start(f32[1,2,192]{2,0,1:T(1,128)} %copy-done.11) | copy-start | bytes 4612
  170.8 16.0 %copy-start.13 = (f32[1,1,192]{2,0,1:T(1,128)S(1)}, f32[1,1,192]{2,0,1:T(1,128)}, u32[]{:S(2)}) copy-start(f32[1,1,192]{2,0,1:T(1,128)} %slice.47) | copy-start | bytes 2308
  170.8 29.2 %copy-start.10 = (s32[6]{0:T(128)S(1)}, s32[6]{0:T(128)}, u32[]{:S(2)}) copy-start(s32[6]{0:T(128)} %copy-done.6) | copy-start | bytes 76
  182.1 10.4 %collective-permute-start.19 = (bf16[2,48,1792]{2,1,0:T(8,128)(2,1)}, bf16[2,48,1792]{2,1,0:T(8,128)(2,1)}, u32[]{:S(2)}, u32[]{:S(2)}) collective-permute-start(bf16[2,48,1792]{2,1,0:T(8,128)(2,1)} %get-tuple-element.58), channel_id=1, source_target_pairs={{0,16},{16,0},{32,48},{48,32},{1,17},{17,1},{33,49},{49,33},{2,18}... | collective-permute-start | bytes 1032200 | tf_op jit(solution)/shard_map/ppermute | solution.py:32
  182.4 15.0 %collective-permute-start.20 = (bf16[2,48,1792]{2,1,0:T(8,128)(2,1)}, bf16[2,48,1792]{2,1,0:T(8,128)(2,1)}, u32[]{:S(2)}, u32[]{:S(2)}) collective-permute-start(bf16[2,48,1792]{2,1,0:T(8,128)(2,1)} %get-tuple-element.59), channel_id=1, source_target_pairs={{0,32},{16,48},{32,0},{48,16},{1,33},{17,49},{33,1},{49,17},{2,34}... | collective-permute-start | bytes 1032200 | tf_op jit(solution)/shard_map/ppermute | solution.py:32
  184.9 15.1 %collective-permute-start.21 = (bf16[2,48,1792]{2,1,0:T(8,128)(2,1)}, bf16[2,48,1792]{2,1,0:T(8,128)(2,1)}, u32[]{:S(2)}, u32[]{:S(2)}) collective-permute-start(bf16[2,48,1792]{2,1,0:T(8,128)(2,1)} %get-tuple-element.60), channel_id=1, source_target_pairs={{0,48},{16,32},{32,16},{48,0},{1,49},{17,33},{33,17},{49,1},{2,50}... | collective-permute-start | bytes 1032200 | tf_op jit(solution)/shard_map/ppermute | solution.py:32
  186.8 1.2 collective-permute-start.18
Sparse Core Ops, SparseCore 0:
  33.7 44.9 all-gather.2

commit v8 on v6

--- a/solution.py
+++ b/solution.py
@@ -16,7 +16,7 @@
 ROWS = 192
 QUARTER = 512
 HALF_D = 1792
-CHUNKS = (1344, 448)
+CHUNKS = (1536, 256)
 TILE = 256
 WIDE = 896
 VMEM = 50 * 1024 * 1024

time: 219 us -> 220 us (level)
  no operation moved by 1% of the time
where the time goes in v8:
time: 220 us; the launch traced here: 218 us
  waiting for transfers between devices  62.1 us (28%)
  blocking collectives  48.4 us (22%)
  Pallas kernels  37.9 us (17%)
  local copies, waits for them, and re-layouts  28.9 us (13%)
  starting transfers between devices  22 us (10%)
  between operations  14.4 us (7%)
  matrix products  2.37 us (1%)
    ppermute x9, waiting for transfers between devices, line_xor(): return lax.ppermute(block, LINE, [(x, x ^ k) for x in range(N_X)])  47.4 us
    all_to_all x2, blocking collectives, add_over_slice(): stats = jnp.sum(lax.all_to_all(spread, axis, 0, 0, tiled=True), axis=0)  30.8 us
    all_to_all x1, blocking collectives, shards(): low = lax.all_to_all(rows_call(at, parts), ('tok', 'z'), 0, 0, tiled=True)  17.6 us
    unnamed x23, local copies, waits for them, and re-layouts  16.8 us
    pallas_call x3, Pallas kernels, terms_call(): pl.pallas_call(functools.partial(terms_kernel, ks=ks, add=acc is not None...  15.5 us
    ppermute x11, waiting for transfers between devices, axis_xor(): lax.ppermute(block, axis, [(i, i ^ k) for i in range(lax.axis_size(axis))])  14.6 us
    pallas_call x1, Pallas kernels, logits_call(): pl.pallas_call(logits_kernel, grid_spec=pltpu.PrefetchScalarGridSpec(num_...  14.2 us
    ppermute x9, starting transfers between devices, line_xor(): return lax.ppermute(block, LINE, [(x, x ^ k) for x in range(N_X)])  11.7 us
  transfers between devices with their start and end apart: 21, of which 13 were waited for; matrix products, arithmetic and copies ran while one was open for 11% of the time, Pallas kernels for 6%

profile of v8, /device:TPU:2, one launch (start us, length us, event | category | flops | bytes accessed | tf_op | source)
XLA Modules:
  0.0 217.7 jit_solution(825134155307387043)
XLA Ops:
  7.3 1.7 copy-done
  9.2 2.2 %collective-permute-start = (bf16[24,896]{1,0:T(8,128)(2,1)S(1)}, bf16[24,896]{1,0:T(8,128)(2,1)S(1)}, u32[]{:S(2)}, u32[]{:S(2)}) collective-permute-start(bf16[24,896]{1,0:T(8,128)(2,1)S(1)} %convolution_convert_fusion.1), channel_id=1, source_target_pairs={{0,64},{64,0},{128,192},{192,128},{1,65},{65,1},{129,193},{193,129... | collective-permute-start | bytes 129032 | tf_op jit(solution)/shard_map/ppermute | solution.py:28
  11.4 1.6 collective-permute-start.1
  13.0 0.8 stack.52
  13.9 0.8 stack.53
  15.1 2.0 collective-permute-start.2
  17.1 2.7 %constant_dynamic-slice_fusion.1 = bf16[1536,512]{1,0:T(8,128)(2,1)} fusion(bf16[1792,2048]{1,0:T(8,128)(2,1)} %refs_1_.1, s32[]{:T(128)S(6)} %select_n.58), kind=kLoop, calls=%fused_computation.48 | loop fusion | bytes 3145732 | tf_op jit(solution)/shard_map/dynamic_slice | solution.py:340
  19.7 1.7 constant_dynamic-slice_fusion.2
  21.5 1.7 collective-permute-start.4
  23.1 2.9 %collective-permute-start.5 = (bf16[1,48,896]{2,1,0:T(8,128)(2,1)S(1)}, bf16[1,48,896]{2,1,0:T(8,128)(2,1)S(1)}, u32[]{:S(2)}, u32[]{:S(2)}) collective-permute-start(bf16[1,48,896]{2,1,0:T(8,128)(2,1)S(1)} %maximum_bitcast_fusion), channel_id=1, source_target_pairs={{0,32},{16,48},{32,0},{48,16},{1,33},{17,49},{33,1},{49,17},{2,34}... | collective-permute-start | bytes 258056 | tf_op jit(solution)/shard_map/ppermute | solution.py:32
  26.2 2.2 convolution_convert_fusion.own
  28.4 1.1 collective-permute-done.5
  29.5 2.2 %collective-permute-done.6 = bf16[1,48,896]{2,1,0:T(8,128)(2,1)S(1)} collective-permute-done((bf16[1,48,896]{2,1,0:T(8,128)(2,1)S(1)}, bf16[1,48,896]{2,1,0:T(8,128)(2,1)S(1)}, u32[]{:S(2)}, u32[]{:S(2)}) %collective-permute-start.6) | collective-permute-done | bytes 86048 | tf_op jit(solution)/shard_map/ppermute | solution.py:32
  31.7 0.8 pad_maximum_fusion
  32.5 0.6 collective-permute-start.3
  33.2 1.2 collective-permute-start.7
  34.5 10.0 %copy.21 = bf16[1792,2048]{0,1:T(8,128)(2,1)} copy(bf16[1792,2048]{1,0:T(8,128)(2,1)} %refs_1_.1) | data formatting | bytes 14680064 | tf_op args[1]
  44.5 2.8 %constant_dynamic-slice_fusion = bf16[1792,512]{1,0:T(8,128)(2,1)} fusion(bf16[1792,2048]{1,0:T(8,128)(2,1)} %refs_1_.1, s32[]{:T(128)S(6)} %select_n.61), kind=kLoop, calls=%fused_computation.47 | loop fusion | bytes 3670020 | tf_op jit(solution)/shard_map/dynamic_slice | solution.py:361
  47.4 16.1 %collective-permute-done.7.nbr = bf16[192,3584]{1,0:T(8,128)(2,1)} collective-permute-done((bf16[192,3584]{1,0:T(8,128)(2,1)}, bf16[192,3584]{1,0:T(8,128)(2,1)}, u32[]{:S(2)}, u32[]{:S(2)}) %collective-permute-start.7) | collective-permute-done | bytes 1376288 | tf_op jit(solution)/shard_map/ppermute | solution.py:28
  63.5 4.0 %collective-permute-done.3.refs_3_ = bf16[1536,512]{1,0:T(8,128)(2,1)} collective-permute-done((bf16[1536,512]{1,0:T(8,128)(2,1)}, bf16[1536,512]{1,0:T(8,128)(2,1)}, u32[]{:S(2)}, u32[]{:S(2)}) %collective-permute-start.3) | collective-permute-done | bytes 1572896 | tf_op jit(solution)/shard_map/ppermute | solution.py:28
  68.8 8.0 %collective-permute-done.9.refs_4_ = bf16[256,512]{1,0:T(8,128)(2,1)S(1)} collective-permute-done((bf16[256,512]{1,0:T(8,128)(2,1)}, bf16[256,512]{1,0:T(8,128)(2,1)S(1)}, u32[]{:S(2)}, u32[]{:S(2)}) %collective-permute-start.9) | collective-permute-done | bytes 262176 | tf_op jit(solution)/shard_map/ppermute | solution.py:28
  76.9 1.6 collective-permute-done.11.refs_6_
  78.5 1.3 copy-done.2
  79.8 14.2 %logits.1 = (f32[4,192,1024]{2,1,0:T(8,128)}, f32[2,8,256]{2,1,0:T(8,128)S(1)}) custom-call(s32[6]{0:T(128)S(1)} %stack.51.at, bf16[192,3584]{1,0:T(8,128)(2,1)S(1)} %copy-done.2, bf16[192,3584]{1,0:T(8,128)(2,1)} %collective-permute-done.7.nbr, bf16[8,4,48,896]{3,2,1,0:T(8,128)(2,1)} %bitcast.53, bf16[1792,2048]{1,0:T(8,128)(2,1)} %refs_1_.1, ...), custom_call_target="tpu_custom_call" | custom-call | flops 5637144576 | bytes 16777216 | tf_op jit(solution)/shard_map/logits/pallas_call | solution.py:129
  94.2 13.5 %all_to_all.15 = f32[16,2,8,256]{3,2,1,0:T(8,128)S(1)} all-to-all(f32[16,2,8,256]{3,2,1,0:T(8,128)S(1)} %broadcast_in_dim.37), channel_id=1, replica_groups=mesh['rep'=2,'tok'=2,'y'=4,'z'=8,'core'=2] {'rep','tok','y'}, dimensions={0} | all-to-all | bytes 524288 | tf_op jit(solution)/shard_map/all_to_all | solution.py:316
  107.7 17.3 %all_to_all.16 = f32[8,2,8,256]{3,2,1,0:T(8,128)S(1)} all-to-all(f32[8,2,8,256]{3,2,1,0:T(8,128)S(1)} %broadcast_in_dim.38), channel_id=1, replica_groups=mesh['rep'=2,'tok'=2,'y'=4,'z'=8,'core'=2] {'z'}, dimensions={0} | all-to-all | bytes 262144 | tf_op jit(solution)/shard_map/all_to_all | solution.py:316
  125.1 6.0 %logit_grad.1 = (bf16[2,192,1024]{2,1,0:T(8,128)(2,1)}, bf16[2,192,1024]{2,1,0:T(8,128)(2,1)}) custom-call(s32[6]{0:T(128)S(1)} %stack.51.at, f32[4,192,1024]{2,1,0:T(8,128)} %get-tuple-element.47.logits, f32[2,8,256]{2,1,0:T(8,128)S(1)} %reduce_sum.28.stats, s32[2,192,128]{2,1,0:T(8,128)S(1)} %broadcast_in_dim.16.refs_7_.tgt, ...), custom_call_target="tpu_custom_call" | custom-call | tf_op jit(solution)/shard_map/logit_grad/pallas_call | solution.py:200
  131.1 1.4 collective-permute-start.15
  133.0 1.6 collective-permute-start.14
  134.6 1.2 slice.47
  135.8 3.1 %copy-done.1 = bf16[1792,2048]{0,1:T(8,128)(2,1)S(1)} copy-done((bf16[1792,2048]{0,1:T(8,128)(2,1)S(1)}, bf16[1792,2048]{0,1:T(8,128)(2,1)}, u32[]{:S(2)}) %copy-start.1) | copy-done | bytes 7340056
  138.9 0.6 copy-done.4
  139.5 4.2 %gradient_terms.3.refs_3_ = f32[384,1792]{1,0:T(8,128)S(1)} custom-call(s32[6]{0:T(128)S(1)} %copy-done.4, bf16[2,192,1024]{2,1,0:T(8,128)(2,1)} %get-tuple-element.49.refs_0_, bf16[2048,1792]{1,0:T(8,128)(2,1)S(1)} %bitcast.44, bf16[2048,1792]{1,0:T(8,128)(2,1)} %collective-permute-done.13.refs_2_.refs_5_), custom_call_target="tpu_custom_call" | custom-call | flops 1409286144 | bytes 6291456 | tf_op jit(solution)/shard_map/gradient_terms/pallas_call | solution.py:264
  143.7 8.0 %collective-permute-done.15.refs_0_ = bf16[2,192,1024]{2,1,0:T(8,128)(2,1)S(1)} collective-permute-done((bf16[2,192,1024]{2,1,0:T(8,128)(2,1)}, bf16[2,192,1024]{2,1,0:T(8,128)(2,1)S(1)}, u32[]{:S(2)}, u32[]{:S(2)}) %collective-permute-start.15) | collective-permute-done | bytes 786464 | tf_op jit(solution)/shard_map/ppermute | solution.py:28
  151.8 4.0 %gradient_terms.4.refs_6_ = f32[384,1792]{1,0:T(8,128)S(1)} custom-call(s32[6]{0:T(128)S(1)} %copy-done.5, bf16[2,192,1024]{2,1,0:T(8,128)(2,1)S(1)} %collective-permute-done.15.refs_0_, bf16[2048,1792]{1,0:T(8,128)(2,1)S(1)} %bitcast.45, bf16[2048,1792]{1,0:T(8,128)(2,1)} %collective-permute-done.13.refs_2_.refs_5_, f32[384,1792]{1,0:T(8,128)S(1)} %gradient_terms.3.refs_3_), custom_call_target="tpu_custom_call" | custom-call | flops 1409286144 | bytes 6291456 | tf_op jit(solution)/shard_map/gradient_terms/pallas_call | solution.py:264
  155.8 10.0 %collective-permute-done.12.refs_0_ = bf16[2,192,1024]{2,1,0:T(8,128)(2,1)} collective-permute-done((bf16[2,192,1024]{2,1,0:T(8,128)(2,1)}, bf16[2,192,1024]{2,1,0:T(8,128)(2,1)}, u32[]{:S(2)}, u32[]{:S(2)}) %collective-permute-start.12) | collective-permute-done | bytes 786464 | tf_op jit(solution)/shard_map/ppermute | solution.py:28
  165.8 1.4 collective-permute-done.14.refs_3_
  167.2 7.3 %gradient_terms.5 = (f32[2,48,1792]{2,1,0:T(8,128)S(1)}, bf16[2,48,1792]{2,1,0:T(8,128)(2,1)}, bf16[2,48,1792]{2,1,0:T(8,128)(2,1)}, bf16[2,48,1792]{2,1,0:T(8,128)(2,1)}) custom-call(s32[6]{0:T(128)S(1)} %copy-done.5, bf16[2,192,1024]{2,1,0:T(8,128)(2,1)} %collective-permute-done.12.refs_0_, bf16[2048,1792]{1,0:T(8,128)(2,1)S(1)} %bitcast.46, ...), custom_call_target="tpu_custom_call" | custom-call | flops 2818572288 | bytes 12582912 | tf_op jit(solution)/shard_map/gradient_terms/pallas_call | solution.py:264
  175.0 1.7 collective-permute-start.18
  176.8 2.4 %collective-permute-start.19 = (bf16[2,48,1792]{2,1,0:T(8,128)(2,1)}, bf16[2,48,1792]{2,1,0:T(8,128)(2,1)}, u32[]{:S(2)}, u32[]{:S(2)}) collective-permute-start(bf16[2,48,1792]{2,1,0:T(8,128)(2,1)} %get-tuple-element.58), channel_id=1, source_target_pairs={{0,48},{16,32},{32,16},{48,0},{1,49},{17,33},{33,17},{49,1},{2,50}... | collective-permute-start | bytes 1032200 | tf_op jit(solution)/shard_map/ppermute | solution.py:32
  179.5 0.9 collective-permute-done.16
  180.8 0.7 reshape.74
  181.5 2.7 %collective-permute-done.17.refs_1_ = bf16[2,48,1792]{2,1,0:T(8,128)(2,1)} collective-permute-done((bf16[2,48,1792]{2,1,0:T(8,128)(2,1)}, bf16[2,48,1792]{2,1,0:T(8,128)(2,1)}, u32[]{:S(2)}, u32[]{:S(2)}) %collective-permute-start.17) | collective-permute-done | bytes 344096 | tf_op jit(solution)/shard_map/ppermute | solution.py:32
  184.3 3.4 %collective-permute-done.18.refs_2_ = bf16[2,48,1792]{2,1,0:T(8,128)(2,1)} collective-permute-done((bf16[2,48,1792]{2,1,0:T(8,128)(2,1)}, bf16[2,48,1792]{2,1,0:T(8,128)(2,1)}, u32[]{:S(2)}, u32[]{:S(2)}) %collective-permute-start.18) | collective-permute-done | bytes 344096 | tf_op jit(solution)/shard_map/ppermute | solution.py:32
  187.6 2.7 %collective-permute-done.19.refs_3_ = bf16[2,48,1792]{2,1,0:T(8,128)(2,1)} collective-permute-done((bf16[2,48,1792]{2,1,0:T(8,128)(2,1)}, bf16[2,48,1792]{2,1,0:T(8,128)(2,1)}, u32[]{:S(2)}, u32[]{:S(2)}) %collective-permute-start.19) | collective-permute-done | bytes 344096 | tf_op jit(solution)/shard_map/ppermute | solution.py:32
  190.3 2.2 %rows.1 = bf16[16,8,1792]{2,1,0:T(8,128)(2,1)S(1)} custom-call(s32[6]{0:T(128)S(1)} %copy-done.6, f32[2,48,1792]{2,1,0:T(8,128)S(1)} %get-tuple-element.55.refs_0_, bf16[2,48,1792]{2,1,0:T(8,128)(2,1)} %collective-permute-done.17.refs_1_, bf16[2,48,1792]{2,1,0:T(8,128)(2,1)} %collective-permute-done.18.refs_2_, ...), custom_call_target="tpu_custom_call" | custom-call | tf_op jit(solution)/shard_map/rows/pallas_call | solution.py:299
  192.6 17.6 %all_to_all.17 = bf16[16,8,1792]{2,1,0:T(8,128)(2,1)S(1)} all-to-all(bf16[16,8,1792]{2,1,0:T(8,128)(2,1)S(1)} %rows.1), channel_id=1, replica_groups=mesh['rep'=2,'tok'=2,'y'=4,'z'=8,'core'=2] {'tok','z'}, dimensions={0} | all-to-all | bytes 917504 | tf_op jit(solution)/shard_map/all_to_all | solution.py:394
  210.2 0.6 pad_maximum_fusion.1
  (73 shorter events, 4.5 us)
Async XLA Ops:
  7.2 1.8 copy-start
  7.2 71.3 %all-gather.3.cloned.1.call-start = ((), (), s32[]{:S(2)}) async-start(), calls=%async_computation.3 | async-start | bytes 3096576 | tf_op jit(solution)/shard_map/all_gather | solution.py:348
  9.2 12.3 %collective-permute-start = (bf16[24,896]{1,0:T(8,128)(2,1)S(1)}, bf16[24,896]{1,0:T(8,128)(2,1)S(1)}, u32[]{:S(2)}, u32[]{:S(2)}) collective-permute-start(bf16[24,896]{1,0:T(8,128)(2,1)S(1)} %convolution_convert_fusion.1), channel_id=1, source_target_pairs={{0,64},{64,0},{128,192},{192,128},{1,65},{65,1},{129,193},{193,129... | collective-permute-start | bytes 129032 | tf_op jit(solution)/shard_map/ppermute | solution.py:28
  11.4 10.1 %collective-permute-start.1 = (bf16[24,896]{1,0:T(8,128)(2,1)S(1)}, bf16[24,896]{1,0:T(8,128)(2,1)S(1)}, u32[]{:S(2)}, u32[]{:S(2)}) collective-permute-start(bf16[24,896]{1,0:T(8,128)(2,1)S(1)} %convolution_convert_fusion.1), channel_id=1, source_target_pairs={{0,192},{64,128},{128,64},{192,0},{1,193},{65,129},{129,65},{193,1... | collective-permute-start | bytes 129032 | tf_op jit(solution)/shard_map/ppermute | solution.py:28
  15.1 6.4 %collective-permute-start.2 = (s32[2,192]{1,0:T(2,128)S(1)}, s32[2,192]{1,0:T(2,128)S(1)}, u32[]{:S(2)}, u32[]{:S(2)}) collective-permute-start(s32[2,192]{1,0:T(2,128)S(1)} %reshape.72), channel_id=1, source_target_pairs={{0,64},{64,0},{128,192},{192,128},{1,65},{65,1},{129,193},{193,129... | collective-permute-start | bytes 4616 | tf_op jit(solution)/shard_map/ppermute | solution.py:28
  21.5 7.0 %collective-permute-start.4 = (bf16[1,48,896]{2,1,0:T(8,128)(2,1)S(1)}, bf16[1,48,896]{2,1,0:T(8,128)(2,1)S(1)}, u32[]{:S(2)}, u32[]{:S(2)}) collective-permute-start(bf16[1,48,896]{2,1,0:T(8,128)(2,1)S(1)} %maximum_bitcast_fusion), channel_id=1, source_target_pairs={{0,16},{16,0},{32,48},{48,32},{1,17},{17,1},{33,49},{49,33},{2,18}... | collective-permute-start | bytes 258056 | tf_op jit(solution)/shard_map/ppermute | solution.py:32
  23.1 6.4 %collective-permute-start.5 = (bf16[1,48,896]{2,1,0:T(8,128)(2,1)S(1)}, bf16[1,48,896]{2,1,0:T(8,128)(2,1)S(1)}, u32[]{:S(2)}, u32[]{:S(2)}) collective-permute-start(bf16[1,48,896]{2,1,0:T(8,128)(2,1)S(1)} %maximum_bitcast_fusion), channel_id=1, source_target_pairs={{0,32},{16,48},{32,0},{48,16},{1,33},{17,49},{33,1},{49,17},{2,34}... | collective-permute-start | bytes 258056 | tf_op jit(solution)/shard_map/ppermute | solution.py:32
  26.0 5.7 %collective-permute-start.6 = (bf16[1,48,896]{2,1,0:T(8,128)(2,1)S(1)}, bf16[1,48,896]{2,1,0:T(8,128)(2,1)S(1)}, u32[]{:S(2)}, u32[]{:S(2)}) collective-permute-start(bf16[1,48,896]{2,1,0:T(8,128)(2,1)S(1)} %maximum_bitcast_fusion), channel_id=1, source_target_pairs={{0,48},{16,32},{32,16},{48,0},{1,49},{17,33},{33,17},{49,1},{2,50}... | collective-permute-start | bytes 258056 | tf_op jit(solution)/shard_map/ppermute | solution.py:32
  32.5 34.9 %collective-permute-start.3 = (bf16[1536,512]{1,0:T(8,128)(2,1)}, bf16[1536,512]{1,0:T(8,128)(2,1)}, u32[]{:S(2)}, u32[]{:S(2)}) collective-permute-start(bf16[1536,512]{1,0:T(8,128)(2,1)} %constant_dynamic-slice_fusion.1), channel_id=1, source_target_pairs={{0,192},{64,128},{128,64},{192,0},{1,193},{65,129},{129,65},{193,1... | collective-permute-start | bytes 4718600 | tf_op jit(solution)/shard_map/ppermute | solution.py:28
  33.2 30.3 %collective-permute-start.7 = (bf16[192,3584]{1,0:T(8,128)(2,1)}, bf16[192,3584]{1,0:T(8,128)(2,1)}, u32[]{:S(2)}, u32[]{:S(2)}) collective-permute-start(bf16[192,3584]{1,0:T(8,128)(2,1)} %convolution_convert_fusion.own), channel_id=1, source_target_pairs={{0,128},{64,192},{128,0},{192,64},{1,129},{65,193},{129,1},{193,65... | collective-permute-start | bytes 4128776 | tf_op jit(solution)/shard_map/ppermute | solution.py:28
  47.4 29.4 %copy-start.7 = (f32[1,2,192]{2,0,1:T(1,128)}, f32[1,2,192]{2,0,1:T(1,128)S(1)}, u32[]{:S(2)}) copy-start(f32[1,2,192]{2,0,1:T(1,128)S(1)} %get-tuple-element.65) | copy-start | bytes 4612
  67.7 10.8 %collective-permute-start.8 = (bf16[1792,512]{1,0:T(8,128)(2,1)}, bf16[1792,512]{1,0:T(8,128)(2,1)}, u32[]{:S(2)}, u32[]{:S(2)}) collective-permute-start(bf16[1792,512]{1,0:T(8,128)(2,1)} %constant_dynamic-slice_fusion), channel_id=1, source_target_pairs={{0,1},{1,0},{2,3},{3,2},{4,5},{5,4},{6,7},{7,6},{8,9},{9,8},{10,11... | collective-permute-start | bytes 5505032 | tf_op jit(solution)/shard_map/ppermute | solution.py:32
  67.8 10.7 %collective-permute-start.10 = (bf16[1536,512]{1,0:T(8,128)(2,1)}, bf16[1536,512]{1,0:T(8,128)(2,1)}, u32[]{:S(2)}, u32[]{:S(2)}) collective-permute-start(bf16[1536,512]{1,0:T(8,128)(2,1)} %collective-permute-done.3.refs_3_), channel_id=1, source_target_pairs={{0,1},{1,0},{2,3},{3,2},{4,5},{5,4},{6,7},{7,6},{8,9},{9,8},{10,11... | collective-permute-start | bytes 4718600 | tf_op jit(solution)/shard_map/ppermute | solution.py:32
  68.3 8.5 %collective-permute-start.9 = (bf16[256,512]{1,0:T(8,128)(2,1)}, bf16[256,512]{1,0:T(8,128)(2,1)S(1)}, u32[]{:S(2)}, u32[]{:S(2)}) collective-permute-start(bf16[256,512]{1,0:T(8,128)(2,1)} %constant_dynamic-slice_fusion.2), channel_id=1, source_target_pairs={{0,192},{64,128},{128,64},{192,0},{1,193},{65,129},{129,65},{193,1... | collective-permute-start | bytes 786440 | tf_op jit(solution)/shard_map/ppermute | solution.py:28
  76.8 1.7 collective-permute-start.11
  76.9 48.2 %copy-start.3 = (s32[6]{0:T(128)}, s32[6]{0:T(128)S(1)}, u32[]{:S(2)}) copy-start(s32[6]{0:T(128)S(1)} %stack.51.at) | copy-start | bytes 76
  78.5 1.3 copy-start.2
  94.0 41.7 %collective-permute-start.13 = (bf16[2048,1792]{1,0:T(8,128)(2,1)}, bf16[2048,1792]{1,0:T(8,128)(2,1)}, u32[]{:S(2)}, u32[]{:S(2)}) collective-permute-start(bf16[2048,1792]{1,0:T(8,128)(2,1)} %bitcast.43), channel_id=1, source_target_pairs={{0,1},{1,0},{2,3},{3,2},{4,5},{5,4},{6,7},{7,6},{8,9},{9,8},{10,11... | collective-permute-start | bytes 22020104 | tf_op jit(solution)/shard_map/ppermute | solution.py:32
  131.1 20.7 %collective-permute-start.15 = (bf16[2,192,1024]{2,1,0:T(8,128)(2,1)}, bf16[2,192,1024]{2,1,0:T(8,128)(2,1)S(1)}, u32[]{:S(2)}, u32[]{:S(2)}) collective-permute-start(bf16[2,192,1024]{2,1,0:T(8,128)(2,1)} %get-tuple-element.51), channel_id=1, source_target_pairs={{0,128},{64,192},{128,0},{192,64},{1,129},{65,193},{129,1},{193,65... | collective-permute-start | bytes 2359304 | tf_op jit(solution)/shard_map/ppermute | solution.py:28
  132.5 33.3 %collective-permute-start.12 = (bf16[2,192,1024]{2,1,0:T(8,128)(2,1)}, bf16[2,192,1024]{2,1,0:T(8,128)(2,1)}, u32[]{:S(2)}, u32[]{:S(2)}) collective-permute-start(bf16[2,192,1024]{2,1,0:T(8,128)(2,1)} %get-tuple-element.49.refs_0_), channel_id=1, source_target_pairs={{0,64},{64,0},{128,192},{192,128},{1,65},{65,1},{129,193},{193,129... | collective-permute-start | bytes 2359304 | tf_op jit(solution)/shard_map/ppermute | solution.py:28
  133.0 34.2 %collective-permute-start.14 = (bf16[2,192,1024]{2,1,0:T(8,128)(2,1)}, bf16[2,192,1024]{2,1,0:T(8,128)(2,1)}, u32[]{:S(2)}, u32[]{:S(2)}) collective-permute-start(bf16[2,192,1024]{2,1,0:T(8,128)(2,1)} %get-tuple-element.51), channel_id=1, source_target_pairs={{0,192},{64,128},{128,64},{192,0},{1,193},{65,129},{129,65},{193,1... | collective-permute-start | bytes 2359304 | tf_op jit(solution)/shard_map/ppermute | solution.py:28
  135.8 3.1 %copy-start.1 = (bf16[1792,2048]{0,1:T(8,128)(2,1)S(1)}, bf16[1792,2048]{0,1:T(8,128)(2,1)}, u32[]{:S(2)}) copy-start(bf16[1792,2048]{0,1:T(8,128)(2,1)} %copy.21) | copy-start | bytes 22020100
  138.9 0.6 copy-start.4
  139.5 12.2 %copy-start.5 = (s32[6]{0:T(128)S(1)}, s32[6]{0:T(128)}, u32[]{:S(2)}) copy-start(s32[6]{0:T(128)} %copy-done.3) | copy-start | bytes 76
  155.7 23.4 %copy-start.8 = (f32[1,2,192]{2,0,1:T(1,128)S(1)}, f32[1,2,192]{2,0,1:T(1,128)}, u32[]{:S(2)}) copy-start(f32[1,2,192]{2,0,1:T(1,128)} %copy-done.7) | copy-start | bytes 4612
  155.8 23.4 %copy-start.9 = (f32[1,1,192]{2,0,1:T(1,128)S(1)}, f32[1,1,192]{2,0,1:T(1,128)}, u32[]{:S(2)}) copy-start(f32[1,1,192]{2,0,1:T(1,128)} %slice.47) | copy-start | bytes 2308
  155.8 34.5 %copy-start.6 = (s32[6]{0:T(128)S(1)}, s32[6]{0:T(128)}, u32[]{:S(2)}) copy-start(s32[6]{0:T(128)} %copy-done.3) | copy-start | bytes 76
  174.4 9.8 %collective-permute-start.17 = (bf16[2,48,1792]{2,1,0:T(8,128)(2,1)}, bf16[2,48,1792]{2,1,0:T(8,128)(2,1)}, u32[]{:S(2)}, u32[]{:S(2)}) collective-permute-start(bf16[2,48,1792]{2,1,0:T(8,128)(2,1)} %get-tuple-element.56), channel_id=1, source_target_pairs={{0,16},{16,0},{32,48},{48,32},{1,17},{17,1},{33,49},{49,33},{2,18}... | collective-permute-start | bytes 1032200 | tf_op jit(solution)/shard_map/ppermute | solution.py:32
  175.0 12.6 %collective-permute-start.18 = (bf16[2,48,1792]{2,1,0:T(8,128)(2,1)}, bf16[2,48,1792]{2,1,0:T(8,128)(2,1)}, u32[]{:S(2)}, u32[]{:S(2)}) collective-permute-start(bf16[2,48,1792]{2,1,0:T(8,128)(2,1)} %get-tuple-element.57), channel_id=1, source_target_pairs={{0,32},{16,48},{32,0},{48,16},{1,33},{17,49},{33,1},{49,17},{2,34}... | collective-permute-start | bytes 1032200 | tf_op jit(solution)/shard_map/ppermute | solution.py:32
  176.8 13.5 %collective-permute-start.19 = (bf16[2,48,1792]{2,1,0:T(8,128)(2,1)}, bf16[2,48,1792]{2,1,0:T(8,128)(2,1)}, u32[]{:S(2)}, u32[]{:S(2)}) collective-permute-start(bf16[2,48,1792]{2,1,0:T(8,128)(2,1)} %get-tuple-element.58), channel_id=1, source_target_pairs={{0,48},{16,32},{32,16},{48,0},{1,49},{17,33},{33,17},{49,1},{2,50}... | collective-permute-start | bytes 1032200 | tf_op jit(solution)/shard_map/ppermute | solution.py:32
  179.2 1.2 collective-permute-start.16
Sparse Core Ops, SparseCore 0:
  32.7 42.4 all-gather.2
